TPU v7x, 32 devices: a whole 2x2x4 slice. The times are simulated.
32 devices in a mesh: wave: 4 (over z), row: 8 (over y, x, core).
Axes of the slice: x: 2, y: 2, z: 4, core: 2. Of those that a mesh axis runs over, the one named last changes fastest.
Arguments:
- lyot_field: bfloat16 [4, 4096, 2, 4096], P('wave', 'row'), may hold values from -6 to 6
- wave_scale: float32 [4], P('wave'), may hold values from 0.35 to 0.7
- trace_start: int32 [4, 1024, 1024], P(None, 'row', 'wave'), may hold values from -8 to 4102, as said below
- trace_length: int32 [4, 1024, 1024], P(None, 'row', 'wave'), may hold values from 1 to 8, as said below
- column_slot: int32 [1024, 1024], P('row', 'wave'), may hold values from 0 to 3
Outputs:
- detector: float32 [4096, 4096], P('row', 'wave')
Inputs may be any that keep to these rules, and one draw needn't show every extreme that they name: trace_start[w, v, u] equals 4 v + w plus an offset between -8 and 7; both ends of the offset are reached. `trace_length`: the value 8 is reached.
All inputs are finite; a program needn't handle non-finite values.
Results may differ from a plain program's by a relative error of at most 0.0031.
Values may be sent and summed in bfloat16 or wider, within the bound.
No kernel may reach another device: no remote copies, remote signals or barrier semaphores. Data moves between devices by JAX's collectives and lax.ppermute only.
A program may use at most 128 MiB of HBM per device.

v0:
```python
import math

import jax
import jax.numpy as jnp
from jax import lax
from jax.sharding import PartitionSpec as P

NQ = 1024
OFFSET = 8
LMAX = 8


def shifted(value, axis, steps):
    count = lax.axis_size(axis)
    initial, last = (max(0, -steps), min(count, count - steps))
    return lax.ppermute(value, axis, [(source, source + steps) for source in range(initial, last)])


def mft_table(scale, pupil_size):
    pupil_pos = jnp.arange(pupil_size, dtype=jnp.float32) - (pupil_size - 1) / 2.0
    lens_pos = jnp.arange(NQ, dtype=jnp.float32) - (NQ - 1) / 2.0
    phase = pupil_pos[:, None] * lens_pos[None, :] * (scale * (2.0 * math.pi / pupil_size))
    norm = 1.0 / math.sqrt(pupil_size)
    table_real = (jnp.cos(phase) * norm).astype(jnp.bfloat16)
    table_imag = (-jnp.sin(phase) * norm).astype(jnp.bfloat16)
    upper = jnp.concatenate([table_real, table_imag], axis=1)
    lower = jnp.concatenate([-table_imag, table_real], axis=1)
    return jnp.concatenate([upper, lower], axis=0)


def lenslet_field(columns, weights):
    count = columns.shape[2]
    products = jnp.einsum("pcn,pk->cnk", columns, weights, preferred_element_type=jnp.float32)
    products = products.reshape(2, count, 2, NQ)
    lens_real = products[0, :, 0] - products[1, :, 1]
    lens_imag = products[1, :, 0] + products[0, :, 1]
    return jnp.stack([lens_real, lens_imag], axis=1)


def per_device(lyot_field, wave_scale, trace_start, trace_length, column_slot):
    wl_count, rows_local, _, pupil_size = lyot_field.shape
    row_index = lax.axis_index("row")
    wave_pos = 0
    table = mft_table(wave_scale[wave_pos], pupil_size)
    pupil_rows = lyot_field[wave_pos].reshape(rows_local, 2 * pupil_size)
    partial_field = jnp.dot(pupil_rows, table, preferred_element_type=jnp.float32)
    partial_field = partial_field.astype(jnp.bfloat16).reshape(rows_local, 2, NQ)
    regrouped = lax.all_to_all(partial_field, "row", split_axis=2, concat_axis=0, tiled=True)
    lens_field = lenslet_field(regrouped, table[:pupil_size])
    intensities = [lens_field[:, 0] * lens_field[:, 0] + lens_field[:, 1] * lens_field[:, 1]]
    stacked = jnp.stack(intensities, axis=0)
    tiles = lax.all_to_all(stacked, "wave", split_axis=2, concat_axis=0, tiled=True)
    waves_all, tile_lens_rows, lens_cols = tiles.shape
    tile_rows = 4 * tile_lens_rows
    detector_cols = 4 * lens_cols
    strip_rows = 4 * ((2 * OFFSET + waves_all + LMAX + 2) // 4)
    groups = strip_rows // 4
    heights = jnp.arange(strip_rows, dtype=jnp.int32)[None, :, None]
    lens_base = 4 * (row_index * tile_lens_rows + jnp.arange(tile_lens_rows, dtype=jnp.int32))

    def add_wave(wave_pos, strip):
        start_rows = lax.dynamic_index_in_dim(trace_start, wave_pos, 0, keepdims=False)
        lengths = lax.dynamic_index_in_dim(trace_length, wave_pos, 0, keepdims=False)
        amount = lax.dynamic_index_in_dim(tiles, wave_pos, 0, keepdims=False) / lengths.astype(
            jnp.float32
        )
        first = (start_rows - lens_base[:, None] + OFFSET)[:, None, :]
        inside = (heights >= first) & (heights < first + lengths[:, None, :])
        return strip + jnp.where(inside, amount[:, None, :], 0.0)

    strip = lax.fori_loop(
        0, waves_all, add_wave, jnp.zeros((tile_lens_rows, strip_rows, lens_cols), jnp.float32)
    )
    slot_hot = (column_slot[:, :, None] == jnp.arange(4, dtype=jnp.int32)[None, None, :]).astype(
        jnp.float32
    )
    spread = (strip[:, :, :, None] * slot_hot[:, None, :, :]).reshape(
        tile_lens_rows, groups, 4, detector_cols
    )
    blocks = tile_lens_rows + groups - 1
    image = jnp.zeros((blocks, 4, detector_cols), jnp.float32)
    for group in range(groups):
        image = image + jnp.pad(spread[:, group], ((group, groups - 1 - group), (0, 0), (0, 0)))
    image = image.reshape(4 * blocks, detector_cols)
    below_count = 4 * blocks - OFFSET - tile_rows
    from_above = shifted(image[OFFSET + tile_rows :], "row", 1)
    from_below = shifted(image[:OFFSET], "row", -1)
    interior = image[OFFSET : OFFSET + tile_rows]
    interior = interior + jnp.pad(from_above, ((0, tile_rows - below_count), (0, 0)))
    interior = interior + jnp.pad(from_below, ((tile_rows - OFFSET, 0), (0, 0)))
    return interior


def solution(mesh):
    placed = (
        P("wave", "row", None, None),
        P("wave"),
        P(None, "row", "wave"),
        P(None, "row", "wave"),
        P("row", "wave"),
    )
    return jax.shard_map(
        per_device, mesh=mesh, in_specs=placed, out_specs=P("row", "wave"), check_vma=False
    )
```

profile of v0, /device:TPU:1, one launch (start us, length us, event | category | flops | bytes accessed | tf_op | source)
XLA Modules:
  0.0 335.4 jit_solution(1115578471834597695)
XLA Ops:
  0.7 62.7 %multiply_convert_fusion.1 = (bf16[4096,1024]{0,1:T(8,128)(2,1)}, bf16[4096,1024]{0,1:T(8,128)(2,1)}) fusion(f32[]{:T(128)} %bitcast, f32[1024]{0:T(1024)S(1)} %iota_add_fusion.1, f32[4096]{0:T(1024)S(1)} %iota_add_fusion), kind=kLoop, calls=%fused_computation.22 | loop fusion | flops 29360128 | bytes 16797700 | tf_op jit(solution)/shard_map/convert_element_type | solution.py:24
  63.4 57.4 %fusion.19 = bf16[4096,1024]{0,1:T(8,128)(2,1)} fusion(f32[]{:T(128)} %bitcast, f32[1024]{0:T(1024)S(1)} %iota_add_fusion.1, f32[4096]{0:T(1024)S(1)} %iota_add_fusion), kind=kLoop, calls=%fused_computation.38 | loop fusion | flops 33554432 | bytes 8409092 | tf_op jit(solution)/shard_map/neg | solution.py:27
  120.8 16.2 %copy.29 = bf16[64,8,2,4096]{3,1,2,0:T(8,128)(2,1)} copy(bf16[64,8,2,4096]{3,2,1,0:T(2,128)(2,1)} %bitcast.68) | data formatting | bytes 16777216
  137.0 38.6 %fusion.14 = bf16[2048,512]{1,0:T(8,128)(2,1)S(1)} fusion(bf16[512,8192]{1,0:T(8,128)(2,1)} %bitcast.69, bf16[4096,1024]{0,1:T(8,128)(2,1)} %get-tuple-element.198, bf16[4096,1024]{0,1:T(8,128)(2,1)} %fusion.19, bf16[4096,1024]{0,1:T(8,128)(2,1)} %get-tuple-element.199), kind=kOutput, calls=%fused_computation.26 | convolution fusion | flops 17315135488 | bytes 35651584 | tf_op jit(solution)/shard_map/dot_general | solution.py:46
  175.5 3.5 %copy.19 = bf16[512,2,1024]{0,1,2:T(2,128)(2,1)} copy(bf16[512,2,1024]{0,2,1:T(8,128)(2,1)S(1)} %bitcast.74) | data formatting | bytes 4194304 | tf_op jit(solution)/shard_map/reshape | solution.py:47
  179.0 5.2 %all-to-all-start = ((bf16[512,2,1024]{0,1,2:T(2,128)(2,1)}), bf16[512,2,1024]{0,1,2:T(2,128)(2,1)S(1)}, u32[]{:S(2)}, u32[]{:S(2)}) async-start(bf16[512,2,1024]{0,1,2:T(2,128)(2,1)} %copy.19), calls=%async_computation | async-start | bytes 4194304 | tf_op jit(solution)/shard_map/all_to_all | solution.py:48
  184.2 13.7 %pad_maximum_fusion = bf16[4096,2048]{0,1:T(8,128)(2,1)} fusion(bf16[4096,1024]{0,1:T(8,128)(2,1)} %get-tuple-element.199, bf16[4096,1024]{0,1:T(8,128)(2,1)} %get-tuple-element.198), kind=kLoop, calls=%fused_computation.20 | loop fusion | flops 33554432 | bytes 33554432 | tf_op jit(solution)/shard_map/concatenate | solution.py:26
  197.9 9.5 %all-to-all-done = bf16[512,2,1024]{0,1,2:T(2,128)(2,1)S(1)} async-done(((bf16[512,2,1024]{0,1,2:T(2,128)(2,1)}), bf16[512,2,1024]{0,1,2:T(2,128)(2,1)S(1)}, u32[]{:S(2)}, u32[]{:S(2)}) %all-to-all-start) | async-done | bytes 2097184 | tf_op jit(solution)/shard_map/all_to_all | solution.py:48
  207.4 2.5 copy.31
  209.9 4.2 %reshape.136 = bf16[4096,2,128,1]{0,2,1,3:T(8,128)(2,1)} reshape(bf16[8,512,2,128]{1,0,3,2:T(8,128)(2,1)} %bitcast.71) | data formatting | bytes 4194304 | tf_op jit(solution)/shard_map/all_to_all | solution.py:48
  214.1 8.7 %fusion.17 = f32[2,128,2,1024]{3,1,2,0:T(8,128)S(1)} fusion(bf16[2,1024,4096,1]{2,1,0,3:T(8,128)(2,1)} %bitcast.67, bf16[4096,2,128,1]{0,2,1,3:T(8,128)(2,1)} %reshape.136), kind=kOutput, calls=%fused_computation.34 | convolution fusion | flops 4294967296 | bytes 20971520 | tf_op jit(solution)/shard_map/pcn,pk->cnk/dot_general | solution.py:33
  222.9 0.0 copy-start.2
  222.9 0.0 copy-start.1
  222.9 0.2 fusion.22
  223.1 1.0 copy.21
  224.1 4.8 %all-to-all-start.1 = ((f32[1,128,1024]{1,0,2:T(1,128)}), f32[1,128,1024]{1,0,2:T(1,128)S(1)}, u32[]{:S(2)}, u32[]{:S(2)}) async-start(f32[1,128,1024]{1,0,2:T(1,128)} %copy.21), calls=%async_computation.1 | async-start | bytes 1048576 | tf_op jit(solution)/shard_map/all_to_all | solution.py:52
  228.9 0.0 copy-done.2
  229.0 0.1 copy.24
  229.1 0.1 eq.26
  229.2 0.1 eq.23
  229.3 0.2 compare_convert_fusion
  229.5 10.3 %all-to-all-done.1 = f32[1,128,1024]{1,0,2:T(1,128)S(1)} async-done(((f32[1,128,1024]{1,0,2:T(1,128)}), f32[1,128,1024]{1,0,2:T(1,128)S(1)}, u32[]{:S(2)}, u32[]{:S(2)}) %all-to-all-start.1) | async-done | bytes 524320 | tf_op jit(solution)/shard_map/all_to_all | solution.py:52
  239.8 0.2 copy.22
  240.0 0.0 copy-done.1
  240.0 23.1 %while.15 = (s32[]{:T(128)}, f32[128,28,256]{2,1,0:T(8,128)}, s32[4,128,256]{2,1,0:T(8,128)}, s32[4,128,256]{2,1,0:T(8,128)S(1)}, f32[4,128,256]{2,1,0:T(8,128)S(1)}, /*index=5*/s32[]{:T(128)}, s32[]{:T(128)}, s32[]{:T(128)}) while((s32[]{:T(128)}, f32[128,28,256]{2,1,0:T(8,128)}, s32[4,128,256]{2,1,0:T(8,128)}, ...), condition=%wide.region_1.2_spmd.clone.clone, body=%wide.region_0.1_spmd.clone.clone.sunk | while | flops 5669123 | bytes 8651883 | solution.py:71
  240.0 1.0 bitcast_add_fusion.2
  241.0 3.1 select_add_fusion.2
  244.1 1.0 bitcast_add_fusion.2
  245.2 5.3 %select_add_fusion.2 = f32[128,28,256]{2,1,0:T(8,128)} fusion(f32[128,28,256]{2,1,0:T(8,128)} %get-tuple-element.250, f32[128,256]{1,0:T(8,128)S(1)} %bitcast_divide_fusion.2, s32[128,256]{1,0:T(8,128)S(1)} %get-tuple-element.239, s32[128,256]{1,0:T(8,128)S(1)} %get-tuple-element.240, pred[]{:T(512)S(6)} %compare.12), kind=kLoop, calls=%fused_computation.4.clone.1 | loop fusion | flops 5505024 | bytes 7733249 | tf_op jit(solution)/shard_map/while/body/eval_jaxpr/add | solution.py:69
  250.4 1.0 bitcast_add_fusion.2
  251.5 5.3 %select_add_fusion.2 = f32[128,28,256]{2,1,0:T(8,128)} fusion(f32[128,28,256]{2,1,0:T(8,128)} %get-tuple-element.250, f32[128,256]{1,0:T(8,128)S(1)} %bitcast_divide_fusion.2, s32[128,256]{1,0:T(8,128)S(1)} %get-tuple-element.239, s32[128,256]{1,0:T(8,128)S(1)} %get-tuple-element.240, pred[]{:T(512)S(6)} %compare.12), kind=kLoop, calls=%fused_computation.4.clone.1 | loop fusion | flops 5505024 | bytes 7733249 | tf_op jit(solution)/shard_map/while/body/eval_jaxpr/add | solution.py:69
  256.7 1.0 bitcast_add_fusion.2
  257.8 5.3 %select_add_fusion.2 = f32[128,28,256]{2,1,0:T(8,128)} fusion(f32[128,28,256]{2,1,0:T(8,128)} %get-tuple-element.250, f32[128,256]{1,0:T(8,128)S(1)} %bitcast_divide_fusion.2, s32[128,256]{1,0:T(8,128)S(1)} %get-tuple-element.239, s32[128,256]{1,0:T(8,128)S(1)} %get-tuple-element.240, pred[]{:T(512)S(6)} %compare.12), kind=kLoop, calls=%fused_computation.4.clone.1 | loop fusion | flops 5505024 | bytes 7733249 | tf_op jit(solution)/shard_map/while/body/eval_jaxpr/add | solution.py:69
  263.0 5.1 %copy.23 = f32[128,28,256]{0,2,1:T(8,128)} copy(f32[128,28,256]{2,1,0:T(8,128)} %get-tuple-element.132) | data formatting | bytes 7340032 | tf_op jit(solution)/shard_map/while | solution.py:71
  268.2 8.7 %mul.92 = f32[128,28,256,4]{0,3,2,1:T(4,128)} broadcast(f32[128,28,256]{0,2,1:T(8,128)} %copy.23), dimensions={0,1,2} | broadcast | bytes 18350080 | tf_op jit(solution)/shard_map/mul | solution.py:77
  276.9 11.9 %broadcast_multiply_fusion = f32[128,7,4,1024]{0,3,2,1:T(8,128)} fusion(f32[128,7,4,1024]{0,3,2,1:T(8,128)} %bitcast.66, f32[128,1024]{0,1:T(8,128)S(1)} %compare_convert_fusion), kind=kLoop, calls=%fused_computation.24 | loop fusion | flops 3670016 | bytes 29884416 | tf_op jit(solution)/shard_map/mul | solution.py:77
  288.7 10.0 %slice_bitcast_fusion.6 = (f32[128,4,1024]{0,2,1:T(8,128)S(1)}, f32[128,4,1024]{0,2,1:T(8,128)}, f32[128,4,1024]{0,2,1:T(8,128)}, f32[128,4,1024]{0,2,1:T(8,128)...) fusion(f32[128,7,4,1024]{0,3,2,1:T(8,128)} %broadcast_multiply_fusion), kind=kLoop, calls=%fused_computation.33 | loop fusion | bytes 29360128 | tf_op jit(solution)/shard_map/squeeze | solution.py:83
  298.7 9.4 %pad_add_fusion = f32[134,4,1024]{0,2,1:T(8,128)S(1)} fusion(f32[128,4,1024]{0,2,1:T(8,128)} %get-tuple-element.192, f32[128,4,1024]{0,2,1:T(8,128)} %get-tuple-element.193, f32[128,4,1024]{0,2,1:T(8,128)} %get-tuple-element.194, f32[128,4,1024]{0,2,1:T(8,128)} %get-tuple-element.195, f32[128,4,1024]{0,2,1:T(8,128)} %get-tuple-element.196, ...), kind=kLoop, calls=%fused_computation.25 | loop fusion | flops 3293184 | bytes 16875520 | tf_op jit(solution)/shard_map/add | solution.py:83
  308.2 0.0 copy-start
  308.2 1.9 copy-done
  310.1 1.9 slice.80
  312.0 0.0 slice-start
  312.1 2.4 copy.26
  314.5 9.6 %collective-permute-start = (f32[16,1024]{1,0:T(8,128)S(1)}, f32[16,1024]{1,0:T(8,128)S(1)}, u32[]{:S(2)}, u32[]{:S(2)}) collective-permute-start(f32[16,1024]{1,0:T(8,128)S(1)} %slice.65), channel_id=1, source_target_pairs={{0,1},{1,2},{2,3},{3,4},{4,5},{5,6},{6,7},{8,9},{9,10},{10,11},{11... | collective-permute-start | bytes 196616 | tf_op jit(solution)/shard_map/ppermute | solution.py:16
  324.1 0.0 slice-done
  324.1 0.6 copy.27
  324.8 1.9 collective-permute-start.1
  326.7 2.8 slice.79
  329.5 2.0 copy.25
  331.5 2.0 slice.63
  333.4 0.0 collective-permute-done.1
  333.5 0.0 collective-permute-done
  333.5 1.5 pad_add_fusion.1
  (14 shorter events, 0.2 us)
Async XLA Ops:
  179.0 28.4 %all-to-all-start = ((bf16[512,2,1024]{0,1,2:T(2,128)(2,1)}), bf16[512,2,1024]{0,1,2:T(2,128)(2,1)S(1)}, u32[]{:S(2)}, u32[]{:S(2)}) async-start(bf16[512,2,1024]{0,1,2:T(2,128)(2,1)} %copy.19), calls=%async_computation | async-start | bytes 4194304 | tf_op jit(solution)/shard_map/all_to_all | solution.py:48
  222.9 6.1 %copy-start.2 = (s32[128,256]{1,0:T(8,128)S(1)}, s32[128,256]{1,0:T(8,128)}, u32[]{:S(2)}) copy-start(s32[128,256]{1,0:T(8,128)} %param.11) | copy-start | bytes 393220
  222.9 17.1 %copy-start.1 = (s32[4,128,256]{2,1,0:T(8,128)S(1)}, s32[4,128,256]{2,1,0:T(8,128)}, u32[]{:S(2)}) copy-start(s32[4,128,256]{2,1,0:T(8,128)} %param.10) | copy-start | bytes 1572868
  224.1 15.6 %all-to-all-start.1 = ((f32[1,128,1024]{1,0,2:T(1,128)}), f32[1,128,1024]{1,0,2:T(1,128)S(1)}, u32[]{:S(2)}, u32[]{:S(2)}) async-start(f32[1,128,1024]{1,0,2:T(1,128)} %copy.21), calls=%async_computation.1 | async-start | bytes 1048576 | tf_op jit(solution)/shard_map/all_to_all | solution.py:52
  308.2 1.9 copy-start
  312.0 12.1 %slice-start = ((f32[134,4,1024]{0,2,1:T(8,128)}), f32[2,4,1024]{0,2,1:T(8,128)S(1)}, s32[]{:S(2)}) async-start(f32[134,4,1024]{0,2,1:T(8,128)} %copy-done), calls=%async_computation.2 | async-start | bytes 4194304 | tf_op jit(solution)/shard_map/slice | solution.py:87
  314.5 19.0 %collective-permute-start = (f32[16,1024]{1,0:T(8,128)S(1)}, f32[16,1024]{1,0:T(8,128)S(1)}, u32[]{:S(2)}, u32[]{:S(2)}) collective-permute-start(f32[16,1024]{1,0:T(8,128)S(1)} %slice.65), channel_id=1, source_target_pairs={{0,1},{1,2},{2,3},{3,4},{4,5},{5,6},{6,7},{8,9},{9,10},{10,11},{11... | collective-permute-start | bytes 196616 | tf_op jit(solution)/shard_map/ppermute | solution.py:16
  324.8 8.7 %collective-permute-start.1 = (f32[8,1024]{1,0:T(8,128)S(1)}, f32[8,1024]{1,0:T(8,128)S(1)}, u32[]{:S(2)}, u32[]{:S(2)}) collective-permute-start(f32[8,1024]{1,0:T(8,128)S(1)} %slice.67), channel_id=1, source_target_pairs={{1,0},{2,1},{3,2},{4,3},{5,4},{6,5},{7,6},{9,8},{10,9},{11,10},{12... | collective-permute-start | bytes 98312 | tf_op jit(solution)/shard_map/ppermute | solution.py:16
where the time goes:
time: 342 us; the launch traced here: 335 us
  other arithmetic  180 us (53%)
  local copies, waits for them, and re-layouts  65.4 us (19%)
  matrix products  47.3 us (14%)
  starting transfers between devices  21.6 us (6%)
  waiting for transfers between devices  19.8 us (6%)
    convert_element_type x1, other arithmetic, mft_table(): table_real = (jnp.cos(phase) * norm).astype(jnp.bfloat16)  62.7 us
    neg x1, other arithmetic, mft_table(): lower = jnp.concatenate([-table_imag, table_real], axis=1)  57.4 us
    dot_general x1, matrix products, per_device(): jnp.dot(pupil_rows, table, preferred_element_type=jnp.float32)  38.6 us
    add x4, other arithmetic, add_wave(): return strip + jnp.where(inside, amount[:, None, :], 0.0)  18.8 us
    unnamed x8, local copies, waits for them, and re-layouts  18.3 us
    concatenate x1, other arithmetic, mft_table(): upper = jnp.concatenate([table_real, table_imag], axis=1)  13.7 us
    mul x1, other arithmetic, per_device(): strip[:, :, :, None] * slot_hot[:, None, :, :]  11.9 us
    ppermute x2, starting transfers between devices, shifted(): lax.ppermute(value, axis, [(source, source + steps) for source in range(i...  11.6 us
  transfers between devices with their start and end apart: 4, of which 2 were waited for; matrix products, arithmetic and copies ran while one was open for 6% of the time, Pallas kernels for 0%

commit v1 on v0

v1 whole, which is shorter than its diff:
```python
import functools
import math

import jax
import jax.numpy as jnp
from jax import lax
from jax.experimental import pallas as pl
from jax.experimental.pallas import tpu as pltpu
from jax.sharding import PartitionSpec as P

NQ = 1024
OFFSET = 8
LMAX = 8
LANES = 128
F32 = jnp.float32
BF16 = jnp.bfloat16
VMEM_LIMIT = 48 * 1024 * 1024


def iota(shape, dim):
    return lax.broadcasted_iota(jnp.int32, shape, dim)


def dot_nt(a, b):
    return lax.dot_general(a, b, (((1,), (1,)), ((), ())), preferred_element_type=F32)


def one_hot(mask):
    return jnp.where(mask, 1.0, 0.0).astype(BF16)


def cos_sin_turns(turns):
    angle = (turns - jnp.round(turns)) * math.pi
    square = angle * angle
    sine = jnp.full_like(angle, 1.0 / math.factorial(13))
    for order in (11, 9, 7, 5, 3, 1):
        sine = sine * square + (-1.0) ** ((order - 1) // 2) / math.factorial(order)
    sine = sine * angle
    cosine = jnp.full_like(angle, 1.0 / math.factorial(16))
    for order in (14, 12, 10, 8, 6, 4, 2, 0):
        cosine = cosine * square + (-1.0) ** (order // 2) / math.factorial(order)
    return 1.0 - 2.0 * sine * sine, 2.0 * sine * cosine


def chunk_rows(block, edge):
    if edge == 0 or 2 * edge >= block:
        return [[(0, block)]]
    return [[(0, edge), (block - edge, block)], [(edge, block - edge)]]


def count_of(ranges):
    return sum(stop - start for start, stop in ranges)


def half_kernel(ranges, parts, block, pupil, me_ref, scale_ref, field_ref, *rest):
    outs, table_ref = rest[:parts], rest[parts]
    total, turn, step, halves = rest[parts + 1 :]
    index = pl.program_id(0)
    rows_total = total.shape[0]
    half = rows_total // 2
    rows = count_of(ranges)
    width = table_ref.shape[1]
    samples = field_ref.shape[0]

    @pl.when(index == 0)
    def start():
        scale = scale_ref[0]
        coarse = jnp.floor(scale * 4096.0) * (1.0 / 4096.0)
        fine = scale - coarse
        for group in range(parts // 2):
            at = group * rows
            for low, high in ranges:
                shape = (high - low, LANES)
                lens = (iota(shape, 0) + (group * block + low)).astype(F32) - (NQ - 1) / 2.0
                place = iota(shape, 1).astype(F32) - (pupil - 1) / 2.0
                cosine, sine = cos_sin_turns(lens * place * (scale * (1.0 / pupil)))
                norm = 1.0 / math.sqrt(pupil)
                here = slice(at, at + high - low)
                turn[0, here] = cosine * norm
                turn[1, here] = sine * norm
                whole = lens * coarse * (LANES / pupil)
                whole = whole - jnp.round(whole)
                cosine, sine = cos_sin_turns(whole + lens * fine * (LANES / pupil))
                step[0, here] = cosine
                step[1, here] = sine
                at += high - low

    for piece in range(width // LANES):
        cosine, sine = turn[0], turn[1]
        lanes = slice(piece * LANES, (piece + 1) * LANES)
        table_ref[:half, lanes] = cosine.astype(BF16)
        table_ref[half:, lanes] = sine.astype(BF16)
        turn[0] = cosine * step[0] - sine * step[1]
        turn[1] = sine * step[0] + cosine * step[1]
    field = field_ref[...].reshape(2 * samples, width)
    product = dot_nt(table_ref[...], field)

    @pl.when(index == 0)
    def first():
        total[...] = product

    @pl.when(index > 0)
    def later():
        total[...] += product

    @pl.when(index == pl.num_programs(0) - 1)
    def finish():
        me = me_ref[0]
        source, target = iota((2 * LANES, 2 * LANES), 0), iota((2 * LANES, 2 * LANES), 1)
        apart = one_hot(
            source == jnp.where(target < LANES, 2 * target, 2 * (target - LANES) + 1)
        )
        for piece in range(samples // LANES):
            even_odd = []
            for side in range(2):
                lanes = slice((2 * piece + side) * LANES, (2 * piece + side + 1) * LANES)
                direct, cross = total[:half, lanes], total[half:, lanes]
                real_lane = iota(cross.shape, 1) % 2 == 0
                swapped = jnp.where(
                    real_lane, pltpu.roll(cross, LANES - 1, 1), -pltpu.roll(cross, 1, 1)
                )
                even_odd.append((direct + swapped, direct - swapped))
            lanes = slice(piece * LANES, (piece + 1) * LANES)
            for mirrored in range(2):
                both = jnp.concatenate([pair[mirrored] for pair in even_odd], axis=1)
                both = jnp.dot(both.astype(BF16), apart, preferred_element_type=F32).astype(BF16)
                for group in range(parts // 2):
                    owner = parts - 1 - group if mirrored else group
                    here = slice(group * rows, (group + 1) * rows)
                    halves[owner, 0, :, lanes] = both[here, :LANES]
                    halves[owner, 1, :, lanes] = both[here, LANES:]
        for hop in range(parts):
            outs[hop][...] = halves[me ^ hop]


def half_transform(ranges, parts, block, me, scale, field):
    samples, _, pupil = field.shape
    rows = count_of(ranges)
    height = parts * rows
    width = min(1024, pupil)
    grid_spec = pltpu.PrefetchScalarGridSpec(
        num_scalar_prefetch=2,
        grid=(pupil // width,),
        in_specs=[pl.BlockSpec((samples, 2, width), lambda i, me, scale: (0, 0, i))],
        out_specs=[pl.BlockSpec((2, rows, samples), lambda i, me, scale: (0, 0, 0))] * parts
        + [pl.BlockSpec((height, width), lambda i, me, scale: (0, i))],
        scratch_shapes=[
            pltpu.VMEM((height, 2 * samples), F32),
            pltpu.VMEM((2, height // 2, LANES), F32),
            pltpu.VMEM((2, height // 2, LANES), F32),
            pltpu.VMEM((parts, 2, rows, samples), BF16),
        ],
    )
    results = pl.pallas_call(
        functools.partial(half_kernel, ranges, parts, block, pupil),
        grid_spec=grid_spec,
        out_shape=[jax.ShapeDtypeStruct((2, rows, samples), BF16)] * parts
        + [jax.ShapeDtypeStruct((height, pupil), BF16)],
        compiler_params=pltpu.CompilerParams(vmem_limit_bytes=VMEM_LIMIT),
        cost_estimate=pl.CostEstimate(
            flops=4 * height * samples * pupil,
            bytes_accessed=2 * (2 * samples * pupil + height * pupil),
            transcendentals=0,
        ),
        name="half_transform",
    )(me, scale, field)
    return results[:parts], results[parts]


def lens_kernel(layout, parts, waves, block, me_ref, wave_ref, *rest):
    tables, rest = rest[: len(layout)], rest[len(layout) :]
    pieces, rest = rest[:parts], rest[parts:]
    outs, totals, tiles = rest[:waves], rest[waves : waves + len(layout)], rest[-1]
    index = pl.program_id(0)
    rows = pieces[0].shape[1]
    samples = pieces[0].shape[2]

    for hop in range(parts):

        @pl.when(index == hop)
        def add(hop=hop):
            piece = pieces[hop][...].reshape(2 * rows, samples)
            for table, total in zip(tables, totals):
                product = dot_nt(table[...], piece)
                if hop == 0:
                    total[...] = product
                else:
                    total[...] += product

    @pl.when(index == parts - 1)
    def finish():
        flip = me_ref[0] >= parts // 2
        shape = (rows, 2 * rows)
        wanted = jnp.where(flip, rows - 1 - iota(shape, 0), iota(shape, 0))
        pick = one_hot(iota(shape, 1) == wanted)
        columns = tiles.shape[2]
        per_tile = columns // block
        back = one_hot(
            iota((columns, columns), 0) == columns - 1 - iota((columns, columns), 1)
        )
        across = {}
        for ranges, total in zip(layout, totals):
            half = total.shape[0] // 2
            direct, cross = total[:half], total[half:]
            swapped = pltpu.roll(cross, rows, 1)
            swapped = jnp.where(iota(cross.shape, 1) < rows, swapped, -swapped)
            for mirrored in range(2):
                value = direct - swapped if mirrored else direct + swapped
                value = value * value
                value = value + pltpu.roll(value, rows, 1)
                across[ranges, mirrored] = value.astype(BF16)
        for group in range(waves // 2):
            for mirrored in range(2):
                strips = []
                for part in range(group * per_tile, (group + 1) * per_tile):
                    spans = []
                    for ranges in layout:
                        at = part * count_of(ranges)
                        for low, high in ranges:
                            spans.append((low, ranges, at, at + high - low))
                            at += high - low
                    for _, ranges, start, stop in sorted(spans):
                        strips.append(across[ranges, mirrored][start:stop])
                strip = jnp.concatenate(strips, axis=0)
                turned = dot_nt(pick, strip).astype(BF16)
                if mirrored:
                    turned = jnp.dot(turned, back, preferred_element_type=F32).astype(BF16)
                tiles[waves - 1 - group if mirrored else group] = turned
        for hop in range(waves):
            outs[hop][...] = tiles[wave_ref[0] ^ hop]


def lens_intensity(layout, parts, waves, block, me, wave, tables, pieces):
    _, rows, samples = pieces[0].shape
    columns = NQ // waves
    heights = [table.shape[0] for table in tables]

    def whole(i, me, wave):
        return (0, 0, 0)

    grid_spec = pltpu.PrefetchScalarGridSpec(
        num_scalar_prefetch=2,
        grid=(parts,),
        in_specs=[
            pl.BlockSpec((height, samples), lambda i, me, wave: (0, me[0] ^ i))
            for height in heights
        ]
        + [pl.BlockSpec((2, rows, samples), whole)] * parts,
        out_specs=[pl.BlockSpec((rows, columns), lambda i, me, wave: (0, 0))] * waves,
        scratch_shapes=[pltpu.VMEM((height, 2 * rows), F32) for height in heights]
        + [pltpu.VMEM((waves, rows, columns), BF16)],
    )
    return pl.pallas_call(
        functools.partial(lens_kernel, layout, parts, waves, block),
        grid_spec=grid_spec,
        out_shape=[jax.ShapeDtypeStruct((rows, columns), BF16)] * waves,
        compiler_params=pltpu.CompilerParams(vmem_limit_bytes=VMEM_LIMIT),
        cost_estimate=pl.CostEstimate(
            flops=4 * rows * sum(heights) * samples * parts,
            bytes_accessed=2 * sum(heights) * samples * parts,
            transcendentals=0,
        ),
        name="lens_intensity",
    )(me, wave, *tables, *pieces)


def shifts(waves):
    return -(OFFSET // 4), (waves - 1 + OFFSET - 1 + LMAX - 1) // 4


def block_light(amounts, masks, slots, at, waves, reach):
    light = [[None] * 4 for _ in range(4)]
    near = pl.ds(at, 24)
    slots_near = slots[near]
    values_near = [amounts[wave, near] for wave in range(waves)]
    masks_near = [masks[wave, near] for wave in range(waves)]
    for shift in range(reach[0], reach[1] + 1):
        rows = slice(8 - shift, 16 - shift)
        slot = slots_near[rows]
        value = [held[rows] for held in values_near]
        mask = [held[rows] for held in masks_near]
        picks = [slot == which for which in range(4)]
        for step in range(4):
            height = 4 * shift + step
            strip = None
            for wave in range(waves):
                if not wave - OFFSET <= height <= wave + OFFSET + LMAX - 2:
                    continue
                bit = (mask[wave] & (1 << (height + OFFSET))) != 0
                term = jnp.where(bit, value[wave], 0.0)
                strip = term if strip is None else strip + term
            if strip is None:
                continue
            for which in range(4):
                term = jnp.where(picks[which], strip, 0.0)
                held = light[step][which]
                light[step][which] = term if held is None else held + term
    return light


def stage_tile(amounts, masks, slots, wave, hop, tile, starts, lengths, slot, first, here, rows):
    which = wave ^ hop
    span = (tile.shape[0], tile.shape[1])
    length = lengths[which, rows]
    place = starts[which, rows] - 4 * (first + iota(span, 0))
    amounts[which, here] = tile.astype(F32) / length.astype(F32)
    masks[which, here] = ((1 << length) - 1) << (place + OFFSET)


def put_planes(light, planes, at):
    for step in range(4):
        for which in range(4):
            value = light[step][which]
            for part in range(value.shape[1] // LANES):
                lanes = slice(part * LANES, (part + 1) * LANES)
                planes.at[4 * part + which][pl.Slice(at + step, 8, 4), :] = value[:, lanes]


def spread(planes, out_ref, rows):
    source, target = iota((2 * LANES, 4 * LANES), 0), iota((2 * LANES, 4 * LANES), 1)
    for part in range(planes.shape[0] // 4):
        value = None
        for pair in range(2):
            slot = 2 * pair + source // LANES
            place = one_hot(target == 4 * (source % LANES) + slot)
            at = 4 * part + 2 * pair
            plane = jnp.concatenate([planes[at, rows], planes[at + 1, rows]], axis=1)
            high = plane.astype(BF16)
            low = (plane - high.astype(F32)).astype(BF16)
            term = jnp.dot(high, place, preferred_element_type=F32)
            term = term + jnp.dot(low, place, preferred_element_type=F32)
            value = term if value is None else value + term
        out_ref[rows, part * 4 * LANES : (part + 1) * 4 * LANES] = value


def edge_kernel(ranges, waves, place_ref, *rest):
    tiles, rest = rest[:waves], rest[waves:]
    starts, lengths, slot, up_ref, down_ref, amounts, masks, slots, planes = rest
    block, columns = slot.shape
    lens0 = place_ref[0] * block
    wave = place_ref[1]
    amounts[...] = jnp.zeros_like(amounts)
    masks[...] = jnp.zeros_like(masks)
    slots[...] = jnp.zeros_like(slots)
    rows_in = count_of(ranges)
    for side, out_ref in enumerate((up_ref, down_ref)):
        rows = slice(block - 8, block) if side else slice(0, 8)
        held = slice(rows_in - 8, rows_in) if side else slice(0, 8)
        first = lens0 + rows.start
        here = slice(16, 24)
        for hop in range(waves):
            tile = tiles[hop][...].astype(F32)[held]
            stage_tile(amounts, masks, slots, wave, hop, tile, starts, lengths, slot, first, here, rows)
        slots[here] = slot[rows]
        low, high = shifts(waves)
        at, reach = (16, (1, high)) if side else (0, (low, -1))
        light = block_light(amounts, masks, slots, at, waves, reach)
        put_planes(light, planes, 0)
        spread(planes, out_ref, slice(0, 32))


def edge_light(ranges, waves, place, tiles, starts, lengths, slot):
    block, columns = slot.shape
    return pl.pallas_call(
        functools.partial(edge_kernel, ranges, waves),
        in_specs=[pl.BlockSpec(memory_space=pltpu.SMEM)]
        + [pl.BlockSpec(memory_space=pltpu.VMEM)] * (waves + 3),
        out_specs=[pl.BlockSpec(memory_space=pltpu.VMEM)] * 2,
        out_shape=[jax.ShapeDtypeStruct((32, 4 * columns), F32)] * 2,
        scratch_shapes=[
            pltpu.VMEM((waves, 40, columns), F32),
            pltpu.VMEM((waves, 40, columns), jnp.int32),
            pltpu.VMEM((40, columns), jnp.int32),
            pltpu.VMEM((4 * columns // LANES, 32, LANES), F32),
        ],
        compiler_params=pltpu.CompilerParams(vmem_limit_bytes=VMEM_LIMIT),
        name="edge_light",
    )(place, *tiles, starts, lengths, slot)


def tile_kernel(layout, waves, place_ref, *rest):
    tiles, rest = rest[: waves * len(layout)], rest[waves * len(layout) :]
    starts, lengths, slot, above, below, out_ref, amounts, masks, slots, planes = rest
    block, columns = slot.shape
    lens0 = place_ref[0] * block
    wave = place_ref[1]
    for edge in (slice(0, 8), slice(block + 8, block + 16)):
        amounts[:, edge] = jnp.zeros((waves, 8, columns), F32)
        masks[:, edge] = jnp.zeros((waves, 8, columns), jnp.int32)
        slots[edge] = jnp.zeros((8, columns), jnp.int32)
    slots[8 : block + 8] = slot[...]
    for part, ranges in enumerate(layout):
        for hop in range(waves):
            at = 0
            for low, high in ranges:
                tile = tiles[part * waves + hop][at : at + high - low].astype(F32)
                at += high - low
                stage_tile(
                    amounts, masks, slots, wave, hop, tile, starts, lengths, slot,
                    lens0 + low, slice(low + 8, high + 8), slice(low, high),
                )

    def body(group, _):
        at = pl.multiple_of(group * 8, 8)
        light = block_light(amounts, masks, slots, at, waves, shifts(waves))
        put_planes(light, planes, at * 4)
        return 0

    lax.fori_loop(0, block // 8, body, 0)
    spread(planes, out_ref, slice(0, 4 * block))
    out_ref[:32] += above[...]
    out_ref[4 * block - 32 :] += below[...]


def tile_light(layout, waves, place, tiles, starts, lengths, slot, above, below):
    block, columns = slot.shape
    return pl.pallas_call(
        functools.partial(tile_kernel, layout, waves),
        in_specs=[pl.BlockSpec(memory_space=pltpu.SMEM)]
        + [pl.BlockSpec(memory_space=pltpu.VMEM)] * (len(tiles) + 5),
        out_specs=pl.BlockSpec(memory_space=pltpu.VMEM),
        out_shape=jax.ShapeDtypeStruct((4 * block, 4 * columns), F32),
        scratch_shapes=[
            pltpu.VMEM((waves, block + 16, columns), F32),
            pltpu.VMEM((waves, block + 16, columns), jnp.int32),
            pltpu.VMEM((block + 16, columns), jnp.int32),
            pltpu.VMEM((4 * columns // LANES, 4 * block, LANES), F32),
        ],
        compiler_params=pltpu.CompilerParams(vmem_limit_bytes=VMEM_LIMIT),
        name="tile_light",
    )(place, *tiles, starts, lengths, slot, above, below)


def exchange(pieces, axis):
    count = lax.axis_size(axis)
    return [pieces[0]] + [
        lax.ppermute(pieces[hop], axis, [(source, source ^ hop) for source in range(count)])
        for hop in range(1, count)
    ]


def shifted(value, axis, steps):
    count = lax.axis_size(axis)
    initial, last = (max(0, -steps), min(count, count - steps))
    return lax.ppermute(value, axis, [(source, source + steps) for source in range(initial, last)])


def per_device(lyot_field, wave_scale, trace_start, trace_length, column_slot):
    parts, waves = lax.axis_size("row"), lax.axis_size("wave")
    block = column_slot.shape[0]
    row_index = lax.axis_index("row").astype(jnp.int32)
    wave_index = lax.axis_index("wave").astype(jnp.int32)
    me, wave = row_index.reshape(1), wave_index.reshape(1)
    place = jnp.stack([row_index, wave_index])
    layout = tuple(tuple(ranges) for ranges in chunk_rows(block, EDGE * block // 128))
    sent, tables = [], []
    for ranges in layout:
        pieces, table = half_transform(ranges, parts, block, me, wave_scale, lyot_field[0])
        sent.append(exchange(pieces, "row"))
        tables.append(table)
    tiles = []
    for pieces in sent:
        intensity = lens_intensity(layout, parts, waves, block, me, wave, tables, pieces)
        tiles.append(exchange(intensity, "wave"))
    up, down = edge_light(layout[0], waves, place, tiles[0], trace_start, trace_length, column_slot)
    above = shifted(down, "row", 1)
    below = shifted(up, "row", -1)
    return tile_light(
        layout, waves, place, [tile for part in tiles for tile in part],
        trace_start, trace_length, column_slot, above, below,
    )


EDGE = 32


def solution(mesh):
    placed = (
        P("wave", "row", None, None),
        P("wave"),
        P(None, "row", "wave"),
        P(None, "row", "wave"),
        P("row", "wave"),
    )
    return jax.shard_map(
        per_device, mesh=mesh, in_specs=placed, out_specs=P("row", "wave"), check_vma=False
    )
```

time: 342 us -> 90.9 us (0.27)
  the two profiles are of different devices: /device:TPU:1 before, /device:TPU:0 now
where the time goes in v1:
time: 90.9 us; the launch traced here: 90.6 us
  Pallas kernels  45.1 us (50%)
  starting transfers between devices  28.6 us (31%)
  waiting for transfers between devices  9.82 us (11%)
  local copies, waits for them, and re-layouts  6.16 us (7%)
    ppermute x20, starting transfers between devices, exchange(): lax.ppermute(pieces[hop], axis, [(source, source ^ hop) for source in ran...  23.7 us
    pallas_call x2, Pallas kernels, half_transform(): pl.pallas_call(functools.partial(half_kernel, ranges, parts, block, pupil...  19.2 us
    pallas_call x2, Pallas kernels, lens_intensity(): pl.pallas_call(functools.partial(lens_kernel, layout, parts, waves, block...  15 us
    ppermute x20, waiting for transfers between devices, exchange(): lax.ppermute(pieces[hop], axis, [(source, source ^ hop) for source in ran...  9.81 us
    pallas_call x1, Pallas kernels, tile_light(): pl.pallas_call(functools.partial(tile_kernel, layout, waves), in_specs=[p...  9.29 us
    unnamed x14, local copies, waits for them, and re-layouts  6.16 us
    ppermute x2, starting transfers between devices, shifted(): lax.ppermute(value, axis, [(source, source + steps) for source in range(i...  4.93 us
  transfers between devices with their start and end apart: 22, of which 4 were waited for; matrix products, arithmetic and copies ran while one was open for 0% of the time, Pallas kernels for 29%

profile of v1, /device:TPU:0, one launch (start us, length us, event | category | flops | bytes accessed | tf_op | source)
XLA Modules:
  0.0 90.6 jit_solution(17355456470514698734)
XLA Ops:
  0.7 9.6 %half_transform.2 = (bf16[2,64,512]{2,1,0:T(8,128)(2,1)S(1)}, bf16[2,64,512]{2,1,0:T(8,128)(2,1)S(1)}, bf16[2,64,512]{2,1,0:T(8,128)(2,1)S(1)}, bf16[2,64,512]{2...) custom-call(s32[1]{0:T(128)} %bitcast.me_ref, ...), custom_call_target="tpu_custom_call" | custom-call | flops 4294967296 | bytes 12582912 | tf_op jit(solution)/shard_map/half_transform/pallas_call | solution.py:154
  10.3 0.0 copy-start
  10.3 2.0 %copy-done = bf16[512,4096]{1,0:T(8,128)(2,1)} copy-done((bf16[512,4096]{1,0:T(8,128)(2,1)}, bf16[512,4096]{1,0:T(8,128)(2,1)S(1)}, u32[]{:S(2)}) %copy-start) | copy-done | bytes 4194328
  12.3 0.5 collective-permute-start
  12.7 2.5 %collective-permute-start.1 = (bf16[2,64,512]{2,1,0:T(8,128)(2,1)S(1)}, bf16[2,64,512]{2,1,0:T(8,128)(2,1)S(1)}, u32[]{:S(2)}, u32[]{:S(2)}) collective-permute-start(bf16[2,64,512]{2,1,0:T(8,128)(2,1)S(1)} %get-tuple-element.37), channel_id=1, source_target_pairs={{0,2},{1,3},{2,0},{3,1},{4,6},{5,7},{6,4},{7,5},{8,10},{9,11},{10,... | collective-permute-start | bytes 393224 | tf_op jit(solution)/shard_map/ppermute | solution.py:437
  15.2 0.1 collective-permute-start.2
  15.4 1.7 %collective-permute-start.3 = (bf16[2,64,512]{2,1,0:T(8,128)(2,1)S(1)}, bf16[2,64,512]{2,1,0:T(8,128)(2,1)S(1)}, u32[]{:S(2)}, u32[]{:S(2)}) collective-permute-start(bf16[2,64,512]{2,1,0:T(8,128)(2,1)S(1)} %get-tuple-element.39), channel_id=1, source_target_pairs={{0,4},{1,5},{2,6},{3,7},{4,0},{5,1},{6,2},{7,3},{8,12},{9,13},{10,... | collective-permute-start | bytes 393224 | tf_op jit(solution)/shard_map/ppermute | solution.py:437
  17.1 0.0 collective-permute-start.4
  17.1 0.0 collective-permute-done.rest_3_
  17.1 2.5 %collective-permute-start.5 = (bf16[2,64,512]{2,1,0:T(8,128)(2,1)S(1)}, bf16[2,64,512]{2,1,0:T(8,128)(2,1)S(1)}, u32[]{:S(2)}, u32[]{:S(2)}) collective-permute-start(bf16[2,64,512]{2,1,0:T(8,128)(2,1)S(1)} %get-tuple-element.41), channel_id=1, source_target_pairs={{0,6},{1,7},{2,4},{3,5},{4,2},{5,3},{6,0},{7,1},{8,14},{9,15},{10,... | collective-permute-start | bytes 393224 | tf_op jit(solution)/shard_map/ppermute | solution.py:437
  19.7 0.0 collective-permute-done.1.rest_4_
  19.7 1.7 %collective-permute-start.6 = (bf16[2,64,512]{2,1,0:T(8,128)(2,1)S(1)}, bf16[2,64,512]{2,1,0:T(8,128)(2,1)S(1)}, u32[]{:S(2)}, u32[]{:S(2)}) collective-permute-start(bf16[2,64,512]{2,1,0:T(8,128)(2,1)S(1)} %get-tuple-element.42), channel_id=1, source_target_pairs={{0,7},{1,6},{2,5},{3,4},{4,3},{5,2},{6,1},{7,0},{8,15},{9,14},{10,... | collective-permute-start | bytes 393224 | tf_op jit(solution)/shard_map/ppermute | solution.py:437
  21.4 9.6 %half_transform.3 = (bf16[2,64,512]{2,1,0:T(8,128)(2,1)S(1)}, bf16[2,64,512]{2,1,0:T(8,128)(2,1)S(1)}, bf16[2,64,512]{2,1,0:T(8,128)(2,1)S(1)}, bf16[2,64,512]{2...) custom-call(s32[1]{0:T(128)} %bitcast.me_ref, ...), custom_call_target="tpu_custom_call" | custom-call | flops 4294967296 | bytes 12582912 | tf_op jit(solution)/shard_map/half_transform/pallas_call | solution.py:154
  31.0 0.0 copy-start.3
  31.0 1.9 %copy-done.3 = bf16[512,4096]{1,0:T(8,128)(2,1)} copy-done((bf16[512,4096]{1,0:T(8,128)(2,1)}, bf16[512,4096]{1,0:T(8,128)(2,1)S(1)}, u32[]{:S(2)}) %copy-start.3) | copy-done | bytes 4194328
  33.0 0.0 collective-permute-done.2.rest_5_
  33.0 1.2 %collective-permute-start.10 = (bf16[2,64,512]{2,1,0:T(8,128)(2,1)S(1)}, bf16[2,64,512]{2,1,0:T(8,128)(2,1)S(1)}, u32[]{:S(2)}, u32[]{:S(2)}) collective-permute-start(bf16[2,64,512]{2,1,0:T(8,128)(2,1)S(1)} %get-tuple-element.48), channel_id=1, source_target_pairs={{0,1},{1,0},{2,3},{3,2},{4,5},{5,4},{6,7},{7,6},{8,9},{9,8},{10,11... | collective-permute-start | bytes 393224 | tf_op jit(solution)/shard_map/ppermute | solution.py:437
  34.1 0.0 collective-permute-done.3.rest_6_
  34.1 0.6 collective-permute-start.11
  34.7 0.0 collective-permute-done.4.rest_7_
  34.7 0.0 collective-permute-done.5.rest_8_
  34.7 0.0 collective-permute-done.6.rest_9_
  34.7 0.0 copy-start.1
  34.7 2.2 %copy-done.1 = bf16[512,4096]{1,0:T(8,128)(2,1)S(1)} copy-done((bf16[512,4096]{1,0:T(8,128)(2,1)S(1)}, bf16[512,4096]{1,0:T(8,128)(2,1)}, u32[]{:S(2)}) %copy-start.1) | copy-done | bytes 4194328
  36.9 0.0 copy-start.4
  36.9 0.0 copy-start.5
  36.9 0.0 copy-start.6
  36.9 7.6 %lens_intensity.2 = (bf16[64,256]{1,0:T(8,128)(2,1)S(1)}, bf16[64,256]{1,0:T(8,128)(2,1)S(1)}, bf16[64,256]{1,0:T(8,128)(2,1)S(1)}, bf16[64,256]{1,0:T(8,128)(2,1)S(1)}) custom-call(s32[1]{0:T(128)} %bitcast.me_ref, s32[1]{0:T(128)} %bitcast.1.wave_ref, bf16[512,4096]{1,0:T(8,128)(2,1)S(1)} %copy-done.1, bf16[512,4096]{1,0:T(8,128)(2,1)} %copy-done.3, ...), custom_call_target="tpu_custom_call" | custom-call | flops 1073741824 | bytes 8388608 | tf_op jit(solution)/shard_map/lens_intensity/pallas_call | solution.py:253
  44.6 1.6 %collective-permute-start.7 = (bf16[64,256]{1,0:T(8,128)(2,1)S(1)}, bf16[64,256]{1,0:T(8,128)(2,1)S(1)}, u32[]{:S(2)}, u32[]{:S(2)}) collective-permute-start(bf16[64,256]{1,0:T(8,128)(2,1)S(1)} %get-tuple-element.44), channel_id=1, source_target_pairs={{0,8},{8,0},{16,24},{24,16},{1,9},{9,1},{17,25},{25,17},{2,10},{10... | collective-permute-start | bytes 98312 | tf_op jit(solution)/shard_map/ppermute | solution.py:437
  46.2 2.6 %collective-permute-start.8 = (bf16[64,256]{1,0:T(8,128)(2,1)S(1)}, bf16[64,256]{1,0:T(8,128)(2,1)S(1)}, u32[]{:S(2)}, u32[]{:S(2)}) collective-permute-start(bf16[64,256]{1,0:T(8,128)(2,1)S(1)} %get-tuple-element.45), channel_id=1, source_target_pairs={{0,16},{8,24},{16,0},{24,8},{1,17},{9,25},{17,1},{25,9},{2,18},{10... | collective-permute-start | bytes 98312 | tf_op jit(solution)/shard_map/ppermute | solution.py:437
  48.8 0.2 collective-permute-start.9
  49.0 0.0 collective-permute-done.10.rest_3_
  49.0 0.1 collective-permute-start.12
  49.1 0.0 collective-permute-done.11.rest_4_
  49.1 0.5 collective-permute-start.13
  49.6 0.0 collective-permute-done.7.rest_1_
  49.6 2.3 %collective-permute-start.14 = (bf16[2,64,512]{2,1,0:T(8,128)(2,1)S(1)}, bf16[2,64,512]{2,1,0:T(8,128)(2,1)S(1)}, u32[]{:S(2)}, u32[]{:S(2)}) collective-permute-start(bf16[2,64,512]{2,1,0:T(8,128)(2,1)S(1)} %get-tuple-element.52), channel_id=1, source_target_pairs={{0,5},{1,4},{2,7},{3,6},{4,1},{5,0},{6,3},{7,2},{8,13},{9,12},{10,... | collective-permute-start | bytes 393224 | tf_op jit(solution)/shard_map/ppermute | solution.py:437
  52.0 0.0 collective-permute-done.8.rest_2_
  52.0 1.0 %collective-permute-start.15 = (bf16[2,64,512]{2,1,0:T(8,128)(2,1)S(1)}, bf16[2,64,512]{2,1,0:T(8,128)(2,1)S(1)}, u32[]{:S(2)}, u32[]{:S(2)}) collective-permute-start(bf16[2,64,512]{2,1,0:T(8,128)(2,1)S(1)} %get-tuple-element.53), channel_id=1, source_target_pairs={{0,6},{1,7},{2,4},{3,5},{4,2},{5,3},{6,0},{7,1},{8,14},{9,15},{10,... | collective-permute-start | bytes 393224 | tf_op jit(solution)/shard_map/ppermute | solution.py:437
  53.0 1.5 %collective-permute-done.9.rest_3_ = bf16[64,256]{1,0:T(8,128)(2,1)S(1)} collective-permute-done((bf16[64,256]{1,0:T(8,128)(2,1)S(1)}, bf16[64,256]{1,0:T(8,128)(2,1)S(1)}, u32[]{:S(2)}, u32[]{:S(2)}) %collective-permute-start.9) | collective-permute-done | bytes 32800 | tf_op jit(solution)/shard_map/ppermute | solution.py:437
  54.5 0.0 collective-permute-start.16
  54.5 0.1 pad_add_fusion.place_ref
  54.6 0.0 copy-done.4
  54.6 0.0 copy-done.5
  54.6 0.0 copy-done.6
  54.6 1.6 %edge_light.1 = (f32[32,1024]{1,0:T(8,128)S(1)}, f32[32,1024]{1,0:T(8,128)S(1)}) custom-call(s32[2]{0:T(128)S(1)} %pad_add_fusion.place_ref, bf16[64,256]{1,0:T(8,128)(2,1)S(1)} %get-tuple-element.43.rest_0_, bf16[64,256]{1,0:T(8,128)(2,1)S(1)} %collective-permute-done.7.rest_1_, bf16[64,256]{1,0:T(8,128)(2,1)S(1)} %collective-permute-done.8.rest_2_, ...), custom_call_target="tpu_custom_call" | custom-call | tf_op jit(solution)/shard_map/edge_light/pallas_call | solution.py:364
  56.2 0.0 collective-permute-done.12.rest_5_
  56.2 3.5 %collective-permute-start.20 = (f32[32,1024]{1,0:T(8,128)S(1)}, f32[32,1024]{1,0:T(8,128)S(1)}, u32[]{:S(2)}, u32[]{:S(2)}) collective-permute-start(f32[32,1024]{1,0:T(8,128)S(1)} %get-tuple-element.59), channel_id=1, source_target_pairs={{0,1},{1,2},{2,3},{3,4},{4,5},{5,6},{6,7},{8,9},{9,10},{10,11},{11... | collective-permute-start | bytes 393224 | tf_op jit(solution)/shard_map/ppermute | solution.py:445
  59.6 0.0 collective-permute-done.13.rest_6_
  59.7 1.5 %collective-permute-start.21 = (f32[32,1024]{1,0:T(8,128)S(1)}, f32[32,1024]{1,0:T(8,128)S(1)}, u32[]{:S(2)}, u32[]{:S(2)}) collective-permute-start(f32[32,1024]{1,0:T(8,128)S(1)} %get-tuple-element.60), channel_id=1, source_target_pairs={{1,0},{2,1},{3,2},{4,3},{5,4},{6,5},{7,6},{9,8},{10,9},{11,10},{12... | collective-permute-start | bytes 393224 | tf_op jit(solution)/shard_map/ppermute | solution.py:445
  61.1 2.8 %collective-permute-done.14.rest_7_ = bf16[2,64,512]{2,1,0:T(8,128)(2,1)S(1)} collective-permute-done((bf16[2,64,512]{2,1,0:T(8,128)(2,1)S(1)}, bf16[2,64,512]{2,1,0:T(8,128)(2,1)S(1)}, u32[]{:S(2)}, u32[]{:S(2)}) %collective-permute-start.14) | collective-permute-done | bytes 131104 | tf_op jit(solution)/shard_map/ppermute | solution.py:437
  63.9 0.0 collective-permute-done.15.rest_8_
  64.0 0.0 collective-permute-done.16.rest_9_
  64.0 0.0 copy-done.2
  64.0 7.4 %lens_intensity.3 = (bf16[64,256]{1,0:T(8,128)(2,1)S(1)}, bf16[64,256]{1,0:T(8,128)(2,1)S(1)}, bf16[64,256]{1,0:T(8,128)(2,1)S(1)}, bf16[64,256]{1,0:T(8,128)(2,1)S(1)}) custom-call(s32[1]{0:T(128)} %bitcast.me_ref, s32[1]{0:T(128)} %bitcast.1.wave_ref, bf16[512,4096]{1,0:T(8,128)(2,1)S(1)} %copy-done.2, bf16[512,4096]{1,0:T(8,128)(2,1)} %copy-done.3, ...), custom_call_target="tpu_custom_call" | custom-call | flops 1073741824 | bytes 8388608 | tf_op jit(solution)/shard_map/lens_intensity/pallas_call | solution.py:253
  71.4 0.7 collective-permute-start.17
  72.1 3.5 %collective-permute-start.18 = (bf16[64,256]{1,0:T(8,128)(2,1)S(1)}, bf16[64,256]{1,0:T(8,128)(2,1)S(1)}, u32[]{:S(2)}, u32[]{:S(2)}) collective-permute-start(bf16[64,256]{1,0:T(8,128)(2,1)S(1)} %get-tuple-element.57), channel_id=1, source_target_pairs={{0,16},{8,24},{16,0},{24,8},{1,17},{9,25},{17,1},{25,9},{2,18},{10... | collective-permute-start | bytes 98312 | tf_op jit(solution)/shard_map/ppermute | solution.py:437
  75.6 0.3 collective-permute-start.19
  75.8 0.0 collective-permute-done.17.rest_5_
  75.8 2.3 %collective-permute-done.18.rest_6_ = bf16[64,256]{1,0:T(8,128)(2,1)S(1)} collective-permute-done((bf16[64,256]{1,0:T(8,128)(2,1)S(1)}, bf16[64,256]{1,0:T(8,128)(2,1)S(1)}, u32[]{:S(2)}, u32[]{:S(2)}) %collective-permute-start.18) | collective-permute-done | bytes 32800 | tf_op jit(solution)/shard_map/ppermute | solution.py:437
  78.1 3.2 %collective-permute-done.19.rest_7_ = bf16[64,256]{1,0:T(8,128)(2,1)S(1)} collective-permute-done((bf16[64,256]{1,0:T(8,128)(2,1)S(1)}, bf16[64,256]{1,0:T(8,128)(2,1)S(1)}, u32[]{:S(2)}, u32[]{:S(2)}) %collective-permute-start.19) | collective-permute-done | bytes 32800 | tf_op jit(solution)/shard_map/ppermute | solution.py:437
  81.3 0.0 collective-permute-done.20.rest_11_
  81.3 0.0 collective-permute-done.21.rest_12_
  81.3 9.3 %tile_light.1 = f32[512,1024]{1,0:T(8,128)} custom-call(s32[2]{0:T(128)S(1)} %pad_add_fusion.place_ref, bf16[64,256]{1,0:T(8,128)(2,1)S(1)} %get-tuple-element.43.rest_0_, bf16[64,256]{1,0:T(8,128)(2,1)S(1)} %collective-permute-done.7.rest_1_, bf16[64,256]{1,0:T(8,128)(2,1)S(1)} %collective-permute-done.8.rest_2_, ...), custom_call_target="tpu_custom_call" | custom-call | tf_op jit(solution)/shard_map/tile_light/pallas_call | solution.py:417
  (1 shorter events, 0.0 us)
Async XLA Ops:
  10.3 2.0 %copy-start = (bf16[512,4096]{1,0:T(8,128)(2,1)}, bf16[512,4096]{1,0:T(8,128)(2,1)S(1)}, u32[]{:S(2)}) copy-start(bf16[512,4096]{1,0:T(8,128)(2,1)S(1)} %get-tuple-element.33.rest_0_) | copy-start | bytes 12582916
  12.3 4.8 %collective-permute-start = (bf16[2,64,512]{2,1,0:T(8,128)(2,1)S(1)}, bf16[2,64,512]{2,1,0:T(8,128)(2,1)S(1)}, u32[]{:S(2)}, u32[]{:S(2)}) collective-permute-start(bf16[2,64,512]{2,1,0:T(8,128)(2,1)S(1)} %get-tuple-element.36), channel_id=1, source_target_pairs={{0,1},{1,0},{2,3},{3,2},{4,5},{5,4},{6,7},{7,6},{8,9},{9,8},{10,11... | collective-permute-start | bytes 393224 | tf_op jit(solution)/shard_map/ppermute | solution.py:437
  12.7 6.9 %collective-permute-start.1 = (bf16[2,64,512]{2,1,0:T(8,128)(2,1)S(1)}, bf16[2,64,512]{2,1,0:T(8,128)(2,1)S(1)}, u32[]{:S(2)}, u32[]{:S(2)}) collective-permute-start(bf16[2,64,512]{2,1,0:T(8,128)(2,1)S(1)} %get-tuple-element.37), channel_id=1, source_target_pairs={{0,2},{1,3},{2,0},{3,1},{4,6},{5,7},{6,4},{7,5},{8,10},{9,11},{10,... | collective-permute-start | bytes 393224 | tf_op jit(solution)/shard_map/ppermute | solution.py:437
  15.2 17.7 %collective-permute-start.2 = (bf16[2,64,512]{2,1,0:T(8,128)(2,1)S(1)}, bf16[2,64,512]{2,1,0:T(8,128)(2,1)S(1)}, u32[]{:S(2)}, u32[]{:S(2)}) collective-permute-start(bf16[2,64,512]{2,1,0:T(8,128)(2,1)S(1)} %get-tuple-element.38), channel_id=1, source_target_pairs={{0,3},{1,2},{2,1},{3,0},{4,7},{5,6},{6,5},{7,4},{8,11},{9,10},{10,... | collective-permute-start | bytes 393224 | tf_op jit(solution)/shard_map/ppermute | solution.py:437
  15.4 18.8 %collective-permute-start.3 = (bf16[2,64,512]{2,1,0:T(8,128)(2,1)S(1)}, bf16[2,64,512]{2,1,0:T(8,128)(2,1)S(1)}, u32[]{:S(2)}, u32[]{:S(2)}) collective-permute-start(bf16[2,64,512]{2,1,0:T(8,128)(2,1)S(1)} %get-tuple-element.39), channel_id=1, source_target_pairs={{0,4},{1,5},{2,6},{3,7},{4,0},{5,1},{6,2},{7,3},{8,12},{9,13},{10,... | collective-permute-start | bytes 393224 | tf_op jit(solution)/shard_map/ppermute | solution.py:437
  17.1 17.6 %collective-permute-start.4 = (bf16[2,64,512]{2,1,0:T(8,128)(2,1)S(1)}, bf16[2,64,512]{2,1,0:T(8,128)(2,1)S(1)}, u32[]{:S(2)}, u32[]{:S(2)}) collective-permute-start(bf16[2,64,512]{2,1,0:T(8,128)(2,1)S(1)} %get-tuple-element.40), channel_id=1, source_target_pairs={{0,5},{1,4},{2,7},{3,6},{4,1},{5,0},{6,3},{7,2},{8,13},{9,12},{10,... | collective-permute-start | bytes 393224 | tf_op jit(solution)/shard_map/ppermute | solution.py:437
  17.1 17.6 %collective-permute-start.5 = (bf16[2,64,512]{2,1,0:T(8,128)(2,1)S(1)}, bf16[2,64,512]{2,1,0:T(8,128)(2,1)S(1)}, u32[]{:S(2)}, u32[]{:S(2)}) collective-permute-start(bf16[2,64,512]{2,1,0:T(8,128)(2,1)S(1)} %get-tuple-element.41), channel_id=1, source_target_pairs={{0,6},{1,7},{2,4},{3,5},{4,2},{5,3},{6,0},{7,1},{8,14},{9,15},{10,... | collective-permute-start | bytes 393224 | tf_op jit(solution)/shard_map/ppermute | solution.py:437
  19.7 15.0 %collective-permute-start.6 = (bf16[2,64,512]{2,1,0:T(8,128)(2,1)S(1)}, bf16[2,64,512]{2,1,0:T(8,128)(2,1)S(1)}, u32[]{:S(2)}, u32[]{:S(2)}) collective-permute-start(bf16[2,64,512]{2,1,0:T(8,128)(2,1)S(1)} %get-tuple-element.42), channel_id=1, source_target_pairs={{0,7},{1,6},{2,5},{3,4},{4,3},{5,2},{6,1},{7,0},{8,15},{9,14},{10,... | collective-permute-start | bytes 393224 | tf_op jit(solution)/shard_map/ppermute | solution.py:437
  31.0 2.0 %copy-start.3 = (bf16[512,4096]{1,0:T(8,128)(2,1)}, bf16[512,4096]{1,0:T(8,128)(2,1)S(1)}, u32[]{:S(2)}) copy-start(bf16[512,4096]{1,0:T(8,128)(2,1)S(1)} %get-tuple-element.34.rest_1_) | copy-start | bytes 12582916
  33.0 16.1 %collective-permute-start.10 = (bf16[2,64,512]{2,1,0:T(8,128)(2,1)S(1)}, bf16[2,64,512]{2,1,0:T(8,128)(2,1)S(1)}, u32[]{:S(2)}, u32[]{:S(2)}) collective-permute-start(bf16[2,64,512]{2,1,0:T(8,128)(2,1)S(1)} %get-tuple-element.48), channel_id=1, source_target_pairs={{0,1},{1,0},{2,3},{3,2},{4,5},{5,4},{6,7},{7,6},{8,9},{9,8},{10,11... | collective-permute-start | bytes 393224 | tf_op jit(solution)/shard_map/ppermute | solution.py:437
  34.1 15.0 %collective-permute-start.11 = (bf16[2,64,512]{2,1,0:T(8,128)(2,1)S(1)}, bf16[2,64,512]{2,1,0:T(8,128)(2,1)S(1)}, u32[]{:S(2)}, u32[]{:S(2)}) collective-permute-start(bf16[2,64,512]{2,1,0:T(8,128)(2,1)S(1)} %get-tuple-element.49), channel_id=1, source_target_pairs={{0,2},{1,3},{2,0},{3,1},{4,6},{5,7},{6,4},{7,5},{8,10},{9,11},{10,... | collective-permute-start | bytes 393224 | tf_op jit(solution)/shard_map/ppermute | solution.py:437
  34.7 2.2 %copy-start.1 = (bf16[512,4096]{1,0:T(8,128)(2,1)S(1)}, bf16[512,4096]{1,0:T(8,128)(2,1)}, u32[]{:S(2)}) copy-start(bf16[512,4096]{1,0:T(8,128)(2,1)} %copy-done) | copy-start | bytes 12582916
  36.9 17.7 %copy-start.4 = (s32[4,128,256]{2,1,0:T(8,128)S(1)}, s32[4,128,256]{2,1,0:T(8,128)}, u32[]{:S(2)}) copy-start(s32[4,128,256]{2,1,0:T(8,128)} %rest_8_.1) | copy-start | bytes 1572868
  36.9 17.7 %copy-start.5 = (s32[4,128,256]{2,1,0:T(8,128)S(1)}, s32[4,128,256]{2,1,0:T(8,128)}, u32[]{:S(2)}) copy-start(s32[4,128,256]{2,1,0:T(8,128)} %rest_9_.1) | copy-start | bytes 1572868
  36.9 17.7 %copy-start.6 = (s32[128,256]{1,0:T(8,128)S(1)}, s32[128,256]{1,0:T(8,128)}, u32[]{:S(2)}) copy-start(s32[128,256]{1,0:T(8,128)} %rest_10_.1) | copy-start | bytes 393220
  36.9 27.0 %copy-start.2 = (bf16[512,4096]{1,0:T(8,128)(2,1)S(1)}, bf16[512,4096]{1,0:T(8,128)(2,1)}, u32[]{:S(2)}) copy-start(bf16[512,4096]{1,0:T(8,128)(2,1)} %copy-done) | copy-start | bytes 12582916
  44.6 5.1 %collective-permute-start.7 = (bf16[64,256]{1,0:T(8,128)(2,1)S(1)}, bf16[64,256]{1,0:T(8,128)(2,1)S(1)}, u32[]{:S(2)}, u32[]{:S(2)}) collective-permute-start(bf16[64,256]{1,0:T(8,128)(2,1)S(1)} %get-tuple-element.44), channel_id=1, source_target_pairs={{0,8},{8,0},{16,24},{24,16},{1,9},{9,1},{17,25},{25,17},{2,10},{10... | collective-permute-start | bytes 98312 | tf_op jit(solution)/shard_map/ppermute | solution.py:437
  46.2 5.8 %collective-permute-start.8 = (bf16[64,256]{1,0:T(8,128)(2,1)S(1)}, bf16[64,256]{1,0:T(8,128)(2,1)S(1)}, u32[]{:S(2)}, u32[]{:S(2)}) collective-permute-start(bf16[64,256]{1,0:T(8,128)(2,1)S(1)} %get-tuple-element.45), channel_id=1, source_target_pairs={{0,16},{8,24},{16,0},{24,8},{1,17},{9,25},{17,1},{25,9},{2,18},{10... | collective-permute-start | bytes 98312 | tf_op jit(solution)/shard_map/ppermute | solution.py:437
  48.8 5.7 %collective-permute-start.9 = (bf16[64,256]{1,0:T(8,128)(2,1)S(1)}, bf16[64,256]{1,0:T(8,128)(2,1)S(1)}, u32[]{:S(2)}, u32[]{:S(2)}) collective-permute-start(bf16[64,256]{1,0:T(8,128)(2,1)S(1)} %get-tuple-element.46), channel_id=1, source_target_pairs={{0,24},{8,16},{16,8},{24,0},{1,25},{9,17},{17,9},{25,1},{2,26},{10... | collective-permute-start | bytes 98312 | tf_op jit(solution)/shard_map/ppermute | solution.py:437
  49.0 7.2 %collective-permute-start.12 = (bf16[2,64,512]{2,1,0:T(8,128)(2,1)S(1)}, bf16[2,64,512]{2,1,0:T(8,128)(2,1)S(1)}, u32[]{:S(2)}, u32[]{:S(2)}) collective-permute-start(bf16[2,64,512]{2,1,0:T(8,128)(2,1)S(1)} %get-tuple-element.50), channel_id=1, source_target_pairs={{0,3},{1,2},{2,1},{3,0},{4,7},{5,6},{6,5},{7,4},{8,11},{9,10},{10,... | collective-permute-start | bytes 393224 | tf_op jit(solution)/shard_map/ppermute | solution.py:437
  49.1 10.5 %collective-permute-start.13 = (bf16[2,64,512]{2,1,0:T(8,128)(2,1)S(1)}, bf16[2,64,512]{2,1,0:T(8,128)(2,1)S(1)}, u32[]{:S(2)}, u32[]{:S(2)}) collective-permute-start(bf16[2,64,512]{2,1,0:T(8,128)(2,1)S(1)} %get-tuple-element.51), channel_id=1, source_target_pairs={{0,4},{1,5},{2,6},{3,7},{4,0},{5,1},{6,2},{7,3},{8,12},{9,13},{10,... | collective-permute-start | bytes 393224 | tf_op jit(solution)/shard_map/ppermute | solution.py:437
  49.6 14.3 %collective-permute-start.14 = (bf16[2,64,512]{2,1,0:T(8,128)(2,1)S(1)}, bf16[2,64,512]{2,1,0:T(8,128)(2,1)S(1)}, u32[]{:S(2)}, u32[]{:S(2)}) collective-permute-start(bf16[2,64,512]{2,1,0:T(8,128)(2,1)S(1)} %get-tuple-element.52), channel_id=1, source_target_pairs={{0,5},{1,4},{2,7},{3,6},{4,1},{5,0},{6,3},{7,2},{8,13},{9,12},{10,... | collective-permute-start | bytes 393224 | tf_op jit(solution)/shard_map/ppermute | solution.py:437
  52.0 12.0 %collective-permute-start.15 = (bf16[2,64,512]{2,1,0:T(8,128)(2,1)S(1)}, bf16[2,64,512]{2,1,0:T(8,128)(2,1)S(1)}, u32[]{:S(2)}, u32[]{:S(2)}) collective-permute-start(bf16[2,64,512]{2,1,0:T(8,128)(2,1)S(1)} %get-tuple-element.53), channel_id=1, source_target_pairs={{0,6},{1,7},{2,4},{3,5},{4,2},{5,3},{6,0},{7,1},{8,14},{9,15},{10,... | collective-permute-start | bytes 393224 | tf_op jit(solution)/shard_map/ppermute | solution.py:437
  54.5 9.4 %collective-permute-start.16 = (bf16[2,64,512]{2,1,0:T(8,128)(2,1)S(1)}, bf16[2,64,512]{2,1,0:T(8,128)(2,1)S(1)}, u32[]{:S(2)}, u32[]{:S(2)}) collective-permute-start(bf16[2,64,512]{2,1,0:T(8,128)(2,1)S(1)} %get-tuple-element.54), channel_id=1, source_target_pairs={{0,7},{1,6},{2,5},{3,4},{4,3},{5,2},{6,1},{7,0},{8,15},{9,14},{10,... | collective-permute-start | bytes 393224 | tf_op jit(solution)/shard_map/ppermute | solution.py:437
  56.2 25.1 %collective-permute-start.20 = (f32[32,1024]{1,0:T(8,128)S(1)}, f32[32,1024]{1,0:T(8,128)S(1)}, u32[]{:S(2)}, u32[]{:S(2)}) collective-permute-start(f32[32,1024]{1,0:T(8,128)S(1)} %get-tuple-element.59), channel_id=1, source_target_pairs={{0,1},{1,2},{2,3},{3,4},{4,5},{5,6},{6,7},{8,9},{9,10},{10,11},{11... | collective-permute-start | bytes 393224 | tf_op jit(solution)/shard_map/ppermute | solution.py:445
  59.7 21.6 %collective-permute-start.21 = (f32[32,1024]{1,0:T(8,128)S(1)}, f32[32,1024]{1,0:T(8,128)S(1)}, u32[]{:S(2)}, u32[]{:S(2)}) collective-permute-start(f32[32,1024]{1,0:T(8,128)S(1)} %get-tuple-element.60), channel_id=1, source_target_pairs={{1,0},{2,1},{3,2},{4,3},{5,4},{6,5},{7,6},{9,8},{10,9},{11,10},{12... | collective-permute-start | bytes 393224 | tf_op jit(solution)/shard_map/ppermute | solution.py:445
  71.4 4.5 %collective-permute-start.17 = (bf16[64,256]{1,0:T(8,128)(2,1)S(1)}, bf16[64,256]{1,0:T(8,128)(2,1)S(1)}, u32[]{:S(2)}, u32[]{:S(2)}) collective-permute-start(bf16[64,256]{1,0:T(8,128)(2,1)S(1)} %get-tuple-element.56), channel_id=1, source_target_pairs={{0,8},{8,0},{16,24},{24,16},{1,9},{9,1},{17,25},{25,17},{2,10},{10... | collective-permute-start | bytes 98312 | tf_op jit(solution)/shard_map/ppermute | solution.py:437
  72.1 6.0 %collective-permute-start.18 = (bf16[64,256]{1,0:T(8,128)(2,1)S(1)}, bf16[64,256]{1,0:T(8,128)(2,1)S(1)}, u32[]{:S(2)}, u32[]{:S(2)}) collective-permute-start(bf16[64,256]{1,0:T(8,128)(2,1)S(1)} %get-tuple-element.57), channel_id=1, source_target_pairs={{0,16},{8,24},{16,0},{24,8},{1,17},{9,25},{17,1},{25,9},{2,18},{10... | collective-permute-start | bytes 98312 | tf_op jit(solution)/shard_map/ppermute | solution.py:437
  75.6 5.7 %collective-permute-start.19 = (bf16[64,256]{1,0:T(8,128)(2,1)S(1)}, bf16[64,256]{1,0:T(8,128)(2,1)S(1)}, u32[]{:S(2)}, u32[]{:S(2)}) collective-permute-start(bf16[64,256]{1,0:T(8,128)(2,1)S(1)} %get-tuple-element.58), channel_id=1, source_target_pairs={{0,24},{8,16},{16,8},{24,0},{1,25},{9,17},{17,9},{25,1},{2,26},{10... | collective-permute-start | bytes 98312 | tf_op jit(solution)/shard_map/ppermute | solution.py:437

commit v2 on v0

v2 whole, which is shorter than its diff:
```python
import functools
import math

import jax
import jax.numpy as jnp
from jax import lax
from jax.experimental import pallas as pl
from jax.experimental.pallas import tpu as pltpu
from jax.sharding import PartitionSpec as P

NQ = 1024
OFFSET = 8
LMAX = 8
LANES = 128
F32 = jnp.float32
BF16 = jnp.bfloat16
MIB = 1024 * 1024
VMEM_LIMIT = 20 * MIB


def iota(shape, dim):
    return lax.broadcasted_iota(jnp.int32, shape, dim)


def dot_nt(a, b):
    return lax.dot_general(a, b, (((1,), (1,)), ((), ())), preferred_element_type=F32)


def one_hot(mask):
    return jnp.where(mask, 1.0, 0.0).astype(BF16)


def cos_sin_turns(turns):
    angle = (turns - jnp.round(turns)) * math.pi
    square = angle * angle
    sine = jnp.full_like(angle, 1.0 / math.factorial(13))
    for order in (11, 9, 7, 5, 3, 1):
        sine = sine * square + (-1.0) ** ((order - 1) // 2) / math.factorial(order)
    sine = sine * angle
    cosine = jnp.full_like(angle, 1.0 / math.factorial(16))
    for order in (14, 12, 10, 8, 6, 4, 2, 0):
        cosine = cosine * square + (-1.0) ** (order // 2) / math.factorial(order)
    return 1.0 - 2.0 * sine * sine, 2.0 * sine * cosine


def chunk_rows(block, halo):
    edge = block // 4 - halo
    return (((-halo, edge), (block - edge, block + halo)), ((edge, block - edge),))


def count_of(ranges):
    return sum(stop - start for start, stop in ranges)


def start_turns(first, here, pupil, scale, turn, step):
    coarse = jnp.floor(scale * 4096.0) * (1.0 / 4096.0)
    fine = scale - coarse
    shape = (here.stop - here.start, LANES)
    lens = (iota(shape, 0) + first).astype(F32) - (NQ - 1) / 2.0
    place = iota(shape, 1).astype(F32) - (pupil - 1) / 2.0
    cosine, sine = cos_sin_turns(lens * place * (scale * (1.0 / pupil)))
    norm = 1.0 / math.sqrt(pupil)
    turn[0, here] = cosine * norm
    turn[1, here] = sine * norm
    whole = lens * coarse * (LANES / pupil)
    whole = whole - jnp.round(whole)
    cosine, sine = cos_sin_turns(whole + lens * fine * (LANES / pupil))
    step[0, here] = cosine
    step[1, here] = sine


def turn_table(low, high, turn, step, table):
    half = table.shape[0] // 2

    for start in range(low, high, LANES):
        cosine, sine = turn[0], turn[1]
        table[:half, start : start + LANES] = cosine.astype(BF16)
        table[half:, start : start + LANES] = sine.astype(BF16)
        turn[0] = cosine * step[0] - sine * step[1]
        turn[1] = sine * step[0] + cosine * step[1]


def table_kernel(scale_ref, *rest):
    table, turn, step = rest[-3:]
    half, pupil = table.shape[0] // 2, table.shape[1]
    for low in range(0, half, 64):
        here = slice(low, min(low + 64, half))
        start_turns(low, here, pupil, scale_ref[0], turn, step)
        rotation = step[0, here], step[1, here]
        cosine, sine = turn[0, here], turn[1, here]
        for start in range(0, pupil, LANES):
            table[here, start : start + LANES] = cosine.astype(BF16)
            table[half + low : half + here.stop, start : start + LANES] = sine.astype(BF16)
            cosine, sine = (
                cosine * rotation[0] - sine * rotation[1],
                sine * rotation[0] + cosine * rotation[1],
            )


def lens_table(scale, pupil, later):
    return pl.pallas_call(
        table_kernel,
        in_specs=[pl.BlockSpec(memory_space=pltpu.SMEM)]
        + [pl.BlockSpec(memory_space=pl.ANY)] * len(later),
        out_specs=pl.BlockSpec(memory_space=pltpu.VMEM),
        out_shape=jax.ShapeDtypeStruct((NQ, pupil), BF16),
        scratch_shapes=[pltpu.VMEM((2, NQ // 2, LANES), F32)] * 2,
        compiler_params=pltpu.CompilerParams(vmem_limit_bytes=VMEM_LIMIT),
        cost_estimate=pl.CostEstimate(flops=1, bytes_accessed=1, transcendentals=0),
        name="lens_table",
    )(scale, *later)


def half_kernel(ranges, parts, block, width, size, extra, me_ref, scale_ref, field_hbm, *rest):
    outs = rest[extra : extra + parts]
    field, table, turn, step, halves, arrived = rest[extra + parts :]
    samples, _, pupil = field_hbm.shape
    half = table.shape[0] // 2
    rows = count_of(ranges)
    loads = {}
    for piece in range(samples // size):
        for low in range(0, pupil, width):
            here = (pl.ds(piece * size, size), slice(None), pl.ds(low, width))
            loads[piece, low] = pltpu.make_async_copy(
                field_hbm.at[here], field.at[here], arrived.at[len(loads)]
            )
            loads[piece, low].start()

    at = 0
    for group in range(parts // 2):
        for low, high in ranges:
            here = slice(at, at + high - low)
            start_turns(group * block + low, here, pupil, scale_ref[0], turn, step)
            at += high - low
    source, target = iota((2 * LANES, 2 * LANES), 0), iota((2 * LANES, 2 * LANES), 1)
    apart = one_hot(source == jnp.where(target < LANES, 2 * target, 2 * (target - LANES) + 1))
    for piece in range(samples // size):
        product = None
        for low in range(0, pupil, width):
            lanes = slice(low, low + width)
            if piece == 0:
                turn_table(low, low + width, turn, step, table)
            loads[piece, low].wait()
            here = field[piece * size : (piece + 1) * size, :, lanes].reshape(2 * size, width)
            term = dot_nt(table[:, lanes], here)
            product = term if product is None else product + term
        for inner in range(size // LANES):
            even_odd = []
            for side in range(2):
                lanes = slice((2 * inner + side) * LANES, (2 * inner + side + 1) * LANES)
                direct, cross = product[:half, lanes], product[half:, lanes]
                swapped = jnp.where(
                    iota(cross.shape, 1) % 2 == 0,
                    pltpu.roll(cross, LANES - 1, 1),
                    -pltpu.roll(cross, 1, 1),
                )
                even_odd.append((direct + swapped, direct - swapped))
            first = piece * size + inner * LANES
            lanes = slice(first, first + LANES)
            for mirrored in range(2):
                both = jnp.concatenate([pair[mirrored] for pair in even_odd], axis=1)
                both = jnp.dot(both.astype(BF16), apart, preferred_element_type=F32)
                for group in range(parts // 2):
                    owner = parts - 1 - group if mirrored else group
                    here = slice(group * rows, (group + 1) * rows)
                    halves[owner, :rows, lanes] = both[here, :LANES].astype(BF16)
                    halves[owner, rows:, lanes] = both[here, LANES:].astype(BF16)
    for hop in range(parts):
        outs[hop][...] = halves[me_ref[0] ^ hop]


def half_transform(ranges, parts, block, me, scale, field, later):
    samples, _, pupil = field.shape
    rows = count_of(ranges)
    height = parts * rows
    width, size = min(WIDTH, pupil), min(SIZE, samples)
    return pl.pallas_call(
        functools.partial(half_kernel, ranges, parts, block, width, size, len(later)),
        in_specs=[pl.BlockSpec(memory_space=pltpu.SMEM)] * 2
        + [pl.BlockSpec(memory_space=pl.ANY)] * (1 + len(later)),
        out_specs=[pl.BlockSpec(memory_space=pltpu.VMEM)] * parts,
        scratch_shapes=[
            pltpu.VMEM(field.shape, BF16),
            pltpu.VMEM((height, pupil), BF16),
            pltpu.VMEM((2, height // 2, LANES), F32),
            pltpu.VMEM((2, height // 2, LANES), F32),
            pltpu.VMEM((parts, 2 * rows, samples), BF16),
            pltpu.SemaphoreType.DMA((pupil // width * (samples // size),)),
        ],
        out_shape=[jax.ShapeDtypeStruct((2 * rows, samples), BF16)] * parts,
        compiler_params=pltpu.CompilerParams(vmem_limit_bytes=ROOM * MIB),
        cost_estimate=pl.CostEstimate(flops=1, bytes_accessed=1, transcendentals=0),
        name="half_transform",
    )(me, scale, field, *later)


def lens_kernel(layout, parts, waves, block, me_ref, wave_ref, table, *rest):
    kinds = len(layout)
    pieces, rest = rest[: kinds * parts], rest[kinds * parts :]
    outs, tiles = rest[:waves], rest[waves]
    me, wave = me_ref[0], wave_ref[0]
    half = table.shape[0] // 2
    samples = pieces[0].shape[1]
    total = None
    for hop in range(parts):
        near = [pieces[kind * parts + hop][...] for kind in range(kinds)]
        lanes = pl.ds(pl.multiple_of((me ^ hop) * samples, samples), samples)
        term = dot_nt(jnp.concatenate(near, axis=0), table[:, lanes])
        total = term if hop == 0 else total + term

    strips, spans, at = ([], []), [], 0
    for ranges in layout:
        rows = count_of(ranges)
        real, imag = total[at : at + rows], total[at + rows : at + 2 * rows]
        at += 2 * rows
        for mirrored, sign in enumerate((1.0, -1.0)):
            lens_real = real[:, :half] + sign * imag[:, half:]
            lens_imag = imag[:, :half] - sign * real[:, half:]
            strips[mirrored].append(lens_real * lens_real + lens_imag * lens_imag)
        spans.extend(ranges)
    height, columns = tiles.shape[1:]
    count = sum(count_of(ranges) for ranges in layout)
    held = iota((height, count), 1)
    row, at = jnp.zeros((height, count), jnp.int32), 0
    for low, high in spans:
        row = jnp.where(held >= at, held - at + low, row)
        at += high - low
    row = jnp.where(me >= parts // 2, block - 1 - row, row)
    pick = one_hot(row == iota((height, count), 0) - MARGIN)
    back = one_hot(iota((columns, columns), 0) == columns - 1 - iota((columns, columns), 1))
    for mirrored in range(2):
        strip = jnp.concatenate(strips[mirrored], axis=0).astype(BF16)
        strip = jnp.dot(pick, strip, preferred_element_type=F32).astype(BF16)
        for group in range(waves // 2):
            tile = strip[:, group * columns : (group + 1) * columns]
            if mirrored:
                tile = jnp.dot(tile, back, preferred_element_type=F32).astype(BF16)
            tiles[waves - 1 - group if mirrored else group] = tile
    for hop in range(waves):
        outs[hop][...] = tiles[wave ^ hop]


def lens_intensity(layout, parts, waves, block, me, wave, table, sent):
    shape = (block + 2 * MARGIN, NQ // waves)
    pieces = [piece for part in sent for piece in part]
    return pl.pallas_call(
        functools.partial(lens_kernel, layout, parts, waves, block),
        in_specs=[pl.BlockSpec(memory_space=pltpu.SMEM)] * 2
        + [pl.BlockSpec(memory_space=pltpu.VMEM)] * (1 + len(pieces)),
        out_specs=[pl.BlockSpec(memory_space=pltpu.VMEM)] * waves,
        out_shape=[jax.ShapeDtypeStruct(shape, BF16)] * waves,
        scratch_shapes=[pltpu.VMEM((waves, *shape), BF16)],
        compiler_params=pltpu.CompilerParams(vmem_limit_bytes=VMEM_LIMIT),
        cost_estimate=pl.CostEstimate(flops=1, bytes_accessed=1, transcendentals=0),
        name="lens_intensity",
    )(me, wave, table, *pieces)


def shifts(waves):
    return -(OFFSET // 4), (waves - 1 + OFFSET - 1 + LMAX - 1) // 4


def block_light(amounts, masks, slots, at, waves, reach):
    light = [[None] * 4 for _ in range(4)]
    near = pl.ds(at, 24)
    slots_near = slots[near]
    values_near = [amounts[wave, near] for wave in range(waves)]
    masks_near = [masks[wave, near] for wave in range(waves)]
    for shift in range(reach[0], reach[1] + 1):
        rows = slice(8 - shift, 16 - shift)
        slot = slots_near[rows]
        value = [held[rows] for held in values_near]
        mask = [held[rows] for held in masks_near]
        picks = [slot == which for which in range(4)]
        for step in range(4):
            height = 4 * shift + step
            strip = None
            for wave in range(waves):
                if not wave - OFFSET <= height <= wave + OFFSET + LMAX - 2:
                    continue
                bit = (mask[wave] & (1 << (height + OFFSET))) != 0
                term = jnp.where(bit, value[wave], 0.0)
                strip = term if strip is None else strip + term
            if strip is None:
                continue
            for which in range(4):
                term = jnp.where(picks[which], strip, 0.0)
                held = light[step][which]
                light[step][which] = term if held is None else held + term
    return light


def put_planes(light, planes, at):
    for step in range(4):
        for which in range(4):
            value = light[step][which]
            for part in range(value.shape[1] // LANES):
                lanes = slice(part * LANES, (part + 1) * LANES)
                planes.at[4 * part + which][pl.Slice(at + step, 8, 4), :] = value[:, lanes]


def spread(planes, out_ref, rows):
    source, target = iota((2 * LANES, 4 * LANES), 0), iota((2 * LANES, 4 * LANES), 1)
    first = jnp.where(source < LANES, 4 * source, 4 * (source - LANES) + 1)
    places = [one_hot(target == first + 2 * pair) for pair in range(2)]
    for part in range(planes.shape[0] // 4):
        value = None
        for pair, place in enumerate(places):
            at = 4 * part + 2 * pair
            plane = jnp.concatenate([planes[at, rows], planes[at + 1, rows]], axis=1)
            high = plane.astype(BF16)
            low = (plane - high.astype(F32)).astype(BF16)
            term = jnp.dot(high, place, preferred_element_type=F32)
            term = term + jnp.dot(low, place, preferred_element_type=F32)
            value = term if value is None else value + term
        out_ref[rows, part * 4 * LANES : (part + 1) * 4 * LANES] = value


def edge_kernel(starts, lengths, slot, *rest):
    up, down = rest[-2:]
    waves, block, _ = starts.shape
    for out, rows in ((up, slice(0, MARGIN)), (down, slice(block - MARGIN, block))):
        out[:waves] = starts[:, rows]
        out[waves : 2 * waves] = lengths[:, rows]
        out[2 * waves] = slot[rows]


def edge_traces(starts, lengths, slot, later):
    waves, _, columns = starts.shape
    shape = jax.ShapeDtypeStruct((2 * waves + 1, MARGIN, columns), jnp.int32)
    return pl.pallas_call(
        edge_kernel,
        in_specs=[pl.BlockSpec(memory_space=pltpu.VMEM)] * 3
        + [pl.BlockSpec(memory_space=pl.ANY)] * len(later),
        out_specs=[pl.BlockSpec(memory_space=pltpu.VMEM)] * 2,
        out_shape=[shape] * 2,
        compiler_params=pltpu.CompilerParams(vmem_limit_bytes=VMEM_LIMIT),
        cost_estimate=pl.CostEstimate(flops=1, bytes_accessed=1, transcendentals=0),
        name="edge_traces",
    )(starts, lengths, slot, *later)


def tile_kernel(waves, place_ref, *rest):
    tiles, rest = rest[:waves], rest[waves:]
    starts, lengths, slot, above, below, out_ref, amounts, masks, slots, planes = rest
    block, columns = slot.shape
    lens0 = place_ref[0] * block
    own = slice(MARGIN, block + MARGIN)
    edges = ((slice(0, MARGIN), above), (slice(block + MARGIN, block + 2 * MARGIN), below))
    slots[own] = slot[...]
    for rows, edge in edges:
        slots[rows] = edge[2 * waves]
    for hop in range(waves):
        which = place_ref[1] ^ hop
        tile = tiles[hop][...].astype(F32)
        parts = [(own, starts[which], lengths[which])]
        parts += [(rows, edge[which], edge[waves + which]) for rows, edge in edges]
        for rows, start, length in parts:
            lens = lens0 + rows.start - MARGIN + iota(start.shape, 0)
            amounts[which, rows] = tile[rows] / jnp.maximum(length, 1).astype(F32)
            masks[which, rows] = ((1 << length) - 1) << jnp.maximum(start - 4 * lens + OFFSET, 0)

    def body(group, _):
        at = pl.multiple_of(group * 8, 8)
        light = block_light(amounts, masks, slots, at, waves, shifts(waves))
        put_planes(light, planes, at * 4)
        return 0

    lax.fori_loop(0, block // 8, body, 0)
    spread(planes, out_ref, slice(0, 4 * block))


def tile_light(waves, place, tiles, starts, lengths, slot, above, below):
    block, columns = slot.shape
    high = block + 2 * MARGIN
    return pl.pallas_call(
        functools.partial(tile_kernel, waves),
        in_specs=[pl.BlockSpec(memory_space=pltpu.SMEM)]
        + [pl.BlockSpec(memory_space=pltpu.VMEM)] * (len(tiles) + 5),
        out_specs=pl.BlockSpec(memory_space=pltpu.VMEM),
        out_shape=jax.ShapeDtypeStruct((4 * block, 4 * columns), F32),
        scratch_shapes=[
            pltpu.VMEM((waves, high, columns), F32),
            pltpu.VMEM((waves, high, columns), jnp.int32),
            pltpu.VMEM((high, columns), jnp.int32),
            pltpu.VMEM((4 * columns // LANES, 4 * block, LANES), F32),
        ],
        compiler_params=pltpu.CompilerParams(vmem_limit_bytes=VMEM_LIMIT),
        cost_estimate=pl.CostEstimate(flops=1, bytes_accessed=1, transcendentals=0),
        name="tile_light",
    )(place, *tiles, starts, lengths, slot, above, below)


def exchange(pieces, axis):
    count = lax.axis_size(axis)
    received = list(pieces)
    for hop in sorted(range(1, count), key=lambda hop: ORDER.index(hop) if hop in ORDER else hop):
        pairs = [(source, source ^ hop) for source in range(count)]
        received[hop] = lax.ppermute(pieces[hop], axis, pairs)
    return received


def shifted(value, axis, steps):
    count = lax.axis_size(axis)
    initial, last = (max(0, -steps), min(count, count - steps))
    return lax.ppermute(value, axis, [(source, source + steps) for source in range(initial, last)])


def per_device(lyot_field, wave_scale, trace_start, trace_length, column_slot):
    parts, waves = lax.axis_size("row"), lax.axis_size("wave")
    block = column_slot.shape[0]
    row_index = lax.axis_index("row").astype(jnp.int32)
    wave_index = lax.axis_index("wave").astype(jnp.int32)
    me, wave = row_index.reshape(1), wave_index.reshape(1)
    place = jnp.stack([row_index, wave_index])
    halo = 4 * -(-max(shifts(waves)[1], -shifts(waves)[0]) // 4)
    layout = chunk_rows(block, halo)
    sent = []
    for ranges in layout:
        later = [sent[-1][hop] for hop in FIRST if hop < parts] if sent else []
        pieces = half_transform(ranges, parts, block, me, wave_scale, lyot_field[0], later)
        sent.append(exchange(pieces, "row"))
    later = [sent[NEAR[0]][hop] for hop in NEAR[1] if hop < parts]
    up, down = edge_traces(trace_start, trace_length, column_slot, later)
    above = shifted(down, "row", 1)
    below = shifted(up, "row", -1)
    later = [sent[-1][hop] for hop in AHEAD if hop < parts]
    table = lens_table(wave_scale, lyot_field.shape[3], [*later, above, below])
    intensity = lens_intensity(layout, parts, waves, block, me, wave, table, sent)
    tiles = exchange(intensity, "wave")
    return tile_light(
        waves, place, tiles, trace_start, trace_length, column_slot, above, below
    )


MARGIN = 8
ROOM = 48
AHEAD = (1, 2)
NEAR = (0, (1,))
ORDER = ()
WIDTH = 4096
SIZE = 512
FIRST = (0, 1, 2)


def solution(mesh):
    placed = (
        P("wave", "row", None, None),
        P("wave"),
        P(None, "row", "wave"),
        P(None, "row", "wave"),
        P("row", "wave"),
    )
    return jax.shard_map(
        per_device, mesh=mesh, in_specs=placed, out_specs=P("row", "wave"), check_vma=False
    )
```

time: 342 us -> 78.5 us (0.23)
  the two profiles are of different devices: /device:TPU:1 before, /device:TPU:0 now
where the time goes in v2:
time: 78.5 us; the launch traced here: 78.3 us
  Pallas kernels  34.8 us (44%)
  starting transfers between devices  23.7 us (30%)
  waiting for transfers between devices  18.9 us (24%)
    ppermute x17, starting transfers between devices, exchange(): received[hop] = lax.ppermute(pieces[hop], axis, pairs)  20.6 us
    pallas_call x2, Pallas kernels, half_transform(): pl.pallas_call(functools.partial(half_kernel, ranges, parts, block, width...  19.6 us
    ppermute x17, waiting for transfers between devices, exchange(): received[hop] = lax.ppermute(pieces[hop], axis, pairs)  18.9 us
    pallas_call x1, Pallas kernels, tile_light(): pl.pallas_call(functools.partial(tile_kernel, waves), in_specs=[pl.BlockS...  9.36 us
    ppermute x2, starting transfers between devices, shifted(): lax.ppermute(value, axis, [(source, source + steps) for source in range(i...  3.08 us
    pallas_call x1, Pallas kernels, lens_intensity(): pl.pallas_call(functools.partial(lens_kernel, layout, parts, waves, block...  2.94 us
    pallas_call x1, Pallas kernels, lens_table(): pl.pallas_call(table_kernel, in_specs=[pl.BlockSpec(memory_space=pltpu.SM...  2.88 us
  transfers between devices with their start and end apart: 19, of which 5 were waited for; matrix products, arithmetic and copies ran while one was open for 0% of the time, Pallas kernels for 17%

profile of v2, /device:TPU:0, one launch (start us, length us, event | category | flops | bytes accessed | tf_op | source)
XLA Modules:
  0.0 78.3 jit_solution(3441714135241555560)
XLA Ops:
  0.7 0.0 copy-start
  0.7 0.0 copy-start.1
  0.7 0.0 copy-start.2
  0.7 9.2 %half_transform.2 = (bf16[128,512]{1,0:T(8,128)(2,1)S(1)}, bf16[128,512]{1,0:T(8,128)(2,1)S(1)}, bf16[128,512]{1,0:T(8,128)(2,1)S(1)}, bf16[128,512]{1,0:T(8,128...) custom-call(s32[1]{0:T(128)} %bitcast.me_ref, ...), custom_call_target="tpu_custom_call" | custom-call | flops 1 | bytes 1 | tf_op jit(solution)/shard_map/half_transform/pallas_call | solution.py:177
  9.9 0.5 collective-permute-start
  10.4 2.6 %collective-permute-start.1 = (bf16[128,512]{1,0:T(8,128)(2,1)S(1)}, bf16[128,512]{1,0:T(8,128)(2,1)S(1)}, u32[]{:S(2)}, u32[]{:S(2)}) collective-permute-start(bf16[128,512]{1,0:T(8,128)(2,1)S(1)} %get-tuple-element.29), channel_id=1, source_target_pairs={{0,2},{1,3},{2,0},{3,1},{4,6},{5,7},{6,4},{7,5},{8,10},{9,11},{10,... | collective-permute-start | bytes 393224 | tf_op jit(solution)/shard_map/ppermute | solution.py:399
  12.9 1.3 %collective-permute-start.10 = (bf16[128,512]{1,0:T(8,128)(2,1)S(1)}, bf16[128,512]{1,0:T(8,128)(2,1)S(1)}, u32[]{:S(2)}, u32[]{:S(2)}) collective-permute-start(bf16[128,512]{1,0:T(8,128)(2,1)S(1)} %get-tuple-element.38), channel_id=1, source_target_pairs={{0,7},{1,6},{2,5},{3,4},{4,3},{5,2},{6,1},{7,0},{8,15},{9,14},{10,... | collective-permute-start | bytes 393224 | tf_op jit(solution)/shard_map/ppermute | solution.py:399
  14.2 1.4 %collective-permute-start.6 = (bf16[128,512]{1,0:T(8,128)(2,1)S(1)}, bf16[128,512]{1,0:T(8,128)(2,1)S(1)}, u32[]{:S(2)}, u32[]{:S(2)}) collective-permute-start(bf16[128,512]{1,0:T(8,128)(2,1)S(1)} %get-tuple-element.34), channel_id=1, source_target_pairs={{0,3},{1,2},{2,1},{3,0},{4,7},{5,6},{6,5},{7,4},{8,11},{9,10},{10,... | collective-permute-start | bytes 393224 | tf_op jit(solution)/shard_map/ppermute | solution.py:399
  15.6 0.5 collective-permute-start.7
  16.2 0.0 collective-permute-done.rest_1_.rest_0_
  16.2 1.0 %collective-permute-start.8 = (bf16[128,512]{1,0:T(8,128)(2,1)S(1)}, bf16[128,512]{1,0:T(8,128)(2,1)S(1)}, u32[]{:S(2)}, u32[]{:S(2)}) collective-permute-start(bf16[128,512]{1,0:T(8,128)(2,1)S(1)} %get-tuple-element.36), channel_id=1, source_target_pairs={{0,5},{1,4},{2,7},{3,6},{4,1},{5,0},{6,3},{7,2},{8,13},{9,12},{10,... | collective-permute-start | bytes 393224 | tf_op jit(solution)/shard_map/ppermute | solution.py:399
  17.2 0.0 collective-permute-done.1.rest_2_
  17.2 10.4 %half_transform.3 = (bf16[144,512]{1,0:T(8,128)(2,1)S(1)}, bf16[144,512]{1,0:T(8,128)(2,1)S(1)}, bf16[144,512]{1,0:T(8,128)(2,1)S(1)}, bf16[144,512]{1,0:T(8,128...) custom-call(s32[1]{0:T(128)} %bitcast.me_ref, ...), custom_call_target="tpu_custom_call" | custom-call | flops 1 | bytes 1 | tf_op jit(solution)/shard_map/half_transform/pallas_call | solution.py:177
  27.6 0.7 collective-permute-start.2
  28.3 0.0 collective-permute-done.10.rest_7_
  28.3 1.5 %collective-permute-start.3 = (bf16[144,512]{1,0:T(8,128)(2,1)S(1)}, bf16[144,512]{1,0:T(8,128)(2,1)S(1)}, u32[]{:S(2)}, u32[]{:S(2)}) collective-permute-start(bf16[144,512]{1,0:T(8,128)(2,1)S(1)} %get-tuple-element.31), channel_id=1, source_target_pairs={{0,2},{1,3},{2,0},{3,1},{4,6},{5,7},{6,4},{7,5},{8,10},{9,11},{10,... | collective-permute-start | bytes 442376 | tf_op jit(solution)/shard_map/ppermute | solution.py:399
  29.8 0.0 collective-permute-done.6.rest_3_
  29.8 1.5 %collective-permute-start.9 = (bf16[128,512]{1,0:T(8,128)(2,1)S(1)}, bf16[128,512]{1,0:T(8,128)(2,1)S(1)}, u32[]{:S(2)}, u32[]{:S(2)}) collective-permute-start(bf16[128,512]{1,0:T(8,128)(2,1)S(1)} %get-tuple-element.37), channel_id=1, source_target_pairs={{0,6},{1,7},{2,4},{3,5},{4,2},{5,3},{6,0},{7,1},{8,14},{9,15},{10,... | collective-permute-start | bytes 393224 | tf_op jit(solution)/shard_map/ppermute | solution.py:399
  31.4 0.0 copy-done
  31.4 0.0 copy-done.1
  31.4 0.0 copy-done.2
  31.4 0.0 collective-permute-done.7.rest_4_
  31.4 1.8 %collective-permute-start.4 = (s32[9,8,256]{2,1,0:T(8,128)S(1)}, s32[9,8,256]{2,1,0:T(8,128)S(1)}, u32[]{:S(2)}, u32[]{:S(2)}) collective-permute-start(s32[9,8,256]{2,1,0:T(8,128)S(1)} %get-tuple-element.32), channel_id=1, source_target_pairs={{0,1},{1,2},{2,3},{3,4},{4,5},{5,6},{6,7},{8,9},{9,10},{10,11},{11... | collective-permute-start | bytes 221192 | tf_op jit(solution)/shard_map/ppermute | solution.py:406
  33.2 0.0 collective-permute-done.8.rest_5_
  33.2 1.3 %collective-permute-start.5 = (s32[9,8,256]{2,1,0:T(8,128)S(1)}, s32[9,8,256]{2,1,0:T(8,128)S(1)}, u32[]{:S(2)}, u32[]{:S(2)}) collective-permute-start(s32[9,8,256]{2,1,0:T(8,128)S(1)} %get-tuple-element.33), channel_id=1, source_target_pairs={{1,0},{2,1},{3,2},{4,3},{5,4},{6,5},{7,6},{9,8},{10,9},{11,10},{12... | collective-permute-start | bytes 221192 | tf_op jit(solution)/shard_map/ppermute | solution.py:406
  34.5 3.8 %collective-permute-done.9.rest_6_ = bf16[128,512]{1,0:T(8,128)(2,1)S(1)} collective-permute-done((bf16[128,512]{1,0:T(8,128)(2,1)S(1)}, bf16[128,512]{1,0:T(8,128)(2,1)S(1)}, u32[]{:S(2)}, u32[]{:S(2)}) %collective-permute-start.9) | collective-permute-done | bytes 131104 | tf_op jit(solution)/shard_map/ppermute | solution.py:399
  38.3 0.7 collective-permute-start.11
  39.0 0.0 collective-permute-done.4.rest_2_.rest_7_
  39.1 0.5 collective-permute-start.12
  39.6 0.0 collective-permute-done.5.rest_3_.rest_8_
  39.6 2.2 %collective-permute-start.13 = (bf16[144,512]{1,0:T(8,128)(2,1)}, bf16[144,512]{1,0:T(8,128)(2,1)S(1)}, u32[]{:S(2)}, u32[]{:S(2)}) collective-permute-start(bf16[144,512]{1,0:T(8,128)(2,1)} %get-tuple-element.42), channel_id=1, source_target_pairs={{0,5},{1,4},{2,7},{3,6},{4,1},{5,0},{6,3},{7,2},{8,13},{9,12},{10,... | collective-permute-start | bytes 442376 | tf_op jit(solution)/shard_map/ppermute | solution.py:399
  41.7 0.0 collective-permute-done.2.rest_0_.rest_9_
  41.7 1.2 %collective-permute-start.14 = (bf16[144,512]{1,0:T(8,128)(2,1)}, bf16[144,512]{1,0:T(8,128)(2,1)S(1)}, u32[]{:S(2)}, u32[]{:S(2)}) collective-permute-start(bf16[144,512]{1,0:T(8,128)(2,1)} %get-tuple-element.43), channel_id=1, source_target_pairs={{0,6},{1,7},{2,4},{3,5},{4,2},{5,3},{6,0},{7,1},{8,14},{9,15},{10,... | collective-permute-start | bytes 442376 | tf_op jit(solution)/shard_map/ppermute | solution.py:399
  43.0 0.0 collective-permute-done.3.rest_1_.rest_10_
  43.0 0.5 collective-permute-start.15
  43.5 2.9 %lens_table.1.table = bf16[1024,4096]{1,0:T(8,128)(2,1)S(1)} custom-call(f32[1]{0:T(128)S(6)} %copy.6.scale_ref, bf16[144,512]{1,0:T(8,128)(2,1)S(1)} %collective-permute-done.2.rest_0_.rest_9_, bf16[144,512]{1,0:T(8,128)(2,1)S(1)} %collective-permute-done.3.rest_1_.rest_10_, s32[9,8,256]{2,1,0:T(8,128)S(1)} %collective-permute-done.4.rest_2_.rest_7_, ...), custom_call_target="tpu_custom_call" | custom-call | flops 1 | bytes 1 | tf_op jit(solution)/shard_map/lens_table/pallas_call | solution.py:101
  46.3 0.0 collective-permute-done.11.rest_11_
  46.4 5.7 %collective-permute-done.12.rest_12_ = bf16[144,512]{1,0:T(8,128)(2,1)S(1)} collective-permute-done((bf16[144,512]{1,0:T(8,128)(2,1)}, bf16[144,512]{1,0:T(8,128)(2,1)S(1)}, u32[]{:S(2)}, u32[]{:S(2)}) %collective-permute-start.12) | collective-permute-done | bytes 147488 | tf_op jit(solution)/shard_map/ppermute | solution.py:399
  52.0 3.4 %collective-permute-done.13.rest_13_ = bf16[144,512]{1,0:T(8,128)(2,1)S(1)} collective-permute-done((bf16[144,512]{1,0:T(8,128)(2,1)}, bf16[144,512]{1,0:T(8,128)(2,1)S(1)}, u32[]{:S(2)}, u32[]{:S(2)}) %collective-permute-start.13) | collective-permute-done | bytes 147488 | tf_op jit(solution)/shard_map/ppermute | solution.py:399
  55.5 0.0 collective-permute-done.14.rest_14_
  55.5 0.0 collective-permute-done.15.rest_15_
  55.5 2.9 %lens_intensity.1 = (bf16[144,256]{1,0:T(8,128)(2,1)S(1)}, bf16[144,256]{1,0:T(8,128)(2,1)S(1)}, bf16[144,256]{1,0:T(8,128)(2,1)S(1)}, bf16[144,256]{1,0:T(8,128)(2,1)S(1)}) custom-call(s32[1]{0:T(128)} %bitcast.me_ref, s32[1]{0:T(128)} %bitcast.1.wave_ref, bf16[1024,4096]{1,0:T(8,128)(2,1)S(1)} %lens_table.1.table, ...), custom_call_target="tpu_custom_call" | custom-call | flops 1 | bytes 1 | tf_op jit(solution)/shard_map/lens_intensity/pallas_call | solution.py:246
  58.4 1.6 %collective-permute-start.16 = (bf16[144,256]{1,0:T(8,128)(2,1)S(1)}, bf16[144,256]{1,0:T(8,128)(2,1)S(1)}, u32[]{:S(2)}, u32[]{:S(2)}) collective-permute-start(bf16[144,256]{1,0:T(8,128)(2,1)S(1)} %get-tuple-element.46), channel_id=1, source_target_pairs={{0,8},{8,0},{16,24},{24,16},{1,9},{9,1},{17,25},{25,17},{2,10},{10... | collective-permute-start | bytes 221192 | tf_op jit(solution)/shard_map/ppermute | solution.py:399
  60.1 2.6 %collective-permute-start.17 = (bf16[144,256]{1,0:T(8,128)(2,1)S(1)}, bf16[144,256]{1,0:T(8,128)(2,1)S(1)}, u32[]{:S(2)}, u32[]{:S(2)}) collective-permute-start(bf16[144,256]{1,0:T(8,128)(2,1)S(1)} %get-tuple-element.47), channel_id=1, source_target_pairs={{0,16},{8,24},{16,0},{24,8},{1,17},{9,25},{17,1},{25,9},{2,18},{10... | collective-permute-start | bytes 221192 | tf_op jit(solution)/shard_map/ppermute | solution.py:399
  62.7 0.2 collective-permute-start.18
  62.9 0.1 pad_add_fusion.place_ref
  63.0 0.0 collective-permute-done.16.rest_1_
  63.0 4.9 %collective-permute-done.17.rest_2_ = bf16[144,256]{1,0:T(8,128)(2,1)S(1)} collective-permute-done((bf16[144,256]{1,0:T(8,128)(2,1)S(1)}, bf16[144,256]{1,0:T(8,128)(2,1)S(1)}, u32[]{:S(2)}, u32[]{:S(2)}) %collective-permute-start.17) | collective-permute-done | bytes 73760 | tf_op jit(solution)/shard_map/ppermute | solution.py:399
  67.9 1.0 %collective-permute-done.18.rest_3_ = bf16[144,256]{1,0:T(8,128)(2,1)S(1)} collective-permute-done((bf16[144,256]{1,0:T(8,128)(2,1)S(1)}, bf16[144,256]{1,0:T(8,128)(2,1)S(1)}, u32[]{:S(2)}, u32[]{:S(2)}) %collective-permute-start.18) | collective-permute-done | bytes 73760 | tf_op jit(solution)/shard_map/ppermute | solution.py:399
  68.9 9.4 %tile_light.1 = f32[512,1024]{1,0:T(8,128)} custom-call(s32[2]{0:T(128)S(1)} %pad_add_fusion.place_ref, bf16[144,256]{1,0:T(8,128)(2,1)S(1)} %get-tuple-element.45.rest_0_, bf16[144,256]{1,0:T(8,128)(2,1)S(1)} %collective-permute-done.16.rest_1_, bf16[144,256]{1,0:T(8,128)(2,1)S(1)} %collective-permute-done.17.rest_2_, ...), custom_call_target="tpu_custom_call" | custom-call | flops 1 | bytes 1 | tf_op jit(solution)/shard_map/tile_light/pallas_call | solution.py:376
  (1 shorter events, 0.0 us)
Async XLA Ops:
  0.7 30.7 %copy-start = (s32[4,128,256]{2,1,0:T(8,128)S(1)}, s32[4,128,256]{2,1,0:T(8,128)}, u32[]{:S(2)}) copy-start(s32[4,128,256]{2,1,0:T(8,128)} %rest_4_.1) | copy-start | bytes 1572868
  0.7 30.7 %copy-start.1 = (s32[4,128,256]{2,1,0:T(8,128)S(1)}, s32[4,128,256]{2,1,0:T(8,128)}, u32[]{:S(2)}) copy-start(s32[4,128,256]{2,1,0:T(8,128)} %rest_5_.1) | copy-start | bytes 1572868
  0.7 30.7 %copy-start.2 = (s32[128,256]{1,0:T(8,128)S(1)}, s32[128,256]{1,0:T(8,128)}, u32[]{:S(2)}) copy-start(s32[128,256]{1,0:T(8,128)} %rest_6_.1) | copy-start | bytes 393220
  9.9 6.3 %collective-permute-start = (bf16[128,512]{1,0:T(8,128)(2,1)S(1)}, bf16[128,512]{1,0:T(8,128)(2,1)S(1)}, u32[]{:S(2)}, u32[]{:S(2)}) collective-permute-start(bf16[128,512]{1,0:T(8,128)(2,1)S(1)} %get-tuple-element.28), channel_id=1, source_target_pairs={{0,1},{1,0},{2,3},{3,2},{4,5},{5,4},{6,7},{7,6},{8,9},{9,8},{10,11... | collective-permute-start | bytes 393224 | tf_op jit(solution)/shard_map/ppermute | solution.py:399
  10.4 6.8 %collective-permute-start.1 = (bf16[128,512]{1,0:T(8,128)(2,1)S(1)}, bf16[128,512]{1,0:T(8,128)(2,1)S(1)}, u32[]{:S(2)}, u32[]{:S(2)}) collective-permute-start(bf16[128,512]{1,0:T(8,128)(2,1)S(1)} %get-tuple-element.29), channel_id=1, source_target_pairs={{0,2},{1,3},{2,0},{3,1},{4,6},{5,7},{6,4},{7,5},{8,10},{9,11},{10,... | collective-permute-start | bytes 393224 | tf_op jit(solution)/shard_map/ppermute | solution.py:399
  12.9 15.4 %collective-permute-start.10 = (bf16[128,512]{1,0:T(8,128)(2,1)S(1)}, bf16[128,512]{1,0:T(8,128)(2,1)S(1)}, u32[]{:S(2)}, u32[]{:S(2)}) collective-permute-start(bf16[128,512]{1,0:T(8,128)(2,1)S(1)} %get-tuple-element.38), channel_id=1, source_target_pairs={{0,7},{1,6},{2,5},{3,4},{4,3},{5,2},{6,1},{7,0},{8,15},{9,14},{10,... | collective-permute-start | bytes 393224 | tf_op jit(solution)/shard_map/ppermute | solution.py:399
  14.2 15.6 %collective-permute-start.6 = (bf16[128,512]{1,0:T(8,128)(2,1)S(1)}, bf16[128,512]{1,0:T(8,128)(2,1)S(1)}, u32[]{:S(2)}, u32[]{:S(2)}) collective-permute-start(bf16[128,512]{1,0:T(8,128)(2,1)S(1)} %get-tuple-element.34), channel_id=1, source_target_pairs={{0,3},{1,2},{2,1},{3,0},{4,7},{5,6},{6,5},{7,4},{8,11},{9,10},{10,... | collective-permute-start | bytes 393224 | tf_op jit(solution)/shard_map/ppermute | solution.py:399
  15.6 15.7 %collective-permute-start.7 = (bf16[128,512]{1,0:T(8,128)(2,1)S(1)}, bf16[128,512]{1,0:T(8,128)(2,1)S(1)}, u32[]{:S(2)}, u32[]{:S(2)}) collective-permute-start(bf16[128,512]{1,0:T(8,128)(2,1)S(1)} %get-tuple-element.35), channel_id=1, source_target_pairs={{0,4},{1,5},{2,6},{3,7},{4,0},{5,1},{6,2},{7,3},{8,12},{9,13},{10,... | collective-permute-start | bytes 393224 | tf_op jit(solution)/shard_map/ppermute | solution.py:399
  16.2 17.0 %collective-permute-start.8 = (bf16[128,512]{1,0:T(8,128)(2,1)S(1)}, bf16[128,512]{1,0:T(8,128)(2,1)S(1)}, u32[]{:S(2)}, u32[]{:S(2)}) collective-permute-start(bf16[128,512]{1,0:T(8,128)(2,1)S(1)} %get-tuple-element.36), channel_id=1, source_target_pairs={{0,5},{1,4},{2,7},{3,6},{4,1},{5,0},{6,3},{7,2},{8,13},{9,12},{10,... | collective-permute-start | bytes 393224 | tf_op jit(solution)/shard_map/ppermute | solution.py:399
  27.6 14.1 %collective-permute-start.2 = (bf16[144,512]{1,0:T(8,128)(2,1)S(1)}, bf16[144,512]{1,0:T(8,128)(2,1)S(1)}, u32[]{:S(2)}, u32[]{:S(2)}) collective-permute-start(bf16[144,512]{1,0:T(8,128)(2,1)S(1)} %get-tuple-element.30), channel_id=1, source_target_pairs={{0,1},{1,0},{2,3},{3,2},{4,5},{5,4},{6,7},{7,6},{8,9},{9,8},{10,11... | collective-permute-start | bytes 442376 | tf_op jit(solution)/shard_map/ppermute | solution.py:399
  28.3 14.7 %collective-permute-start.3 = (bf16[144,512]{1,0:T(8,128)(2,1)S(1)}, bf16[144,512]{1,0:T(8,128)(2,1)S(1)}, u32[]{:S(2)}, u32[]{:S(2)}) collective-permute-start(bf16[144,512]{1,0:T(8,128)(2,1)S(1)} %get-tuple-element.31), channel_id=1, source_target_pairs={{0,2},{1,3},{2,0},{3,1},{4,6},{5,7},{6,4},{7,5},{8,10},{9,11},{10,... | collective-permute-start | bytes 442376 | tf_op jit(solution)/shard_map/ppermute | solution.py:399
  29.8 8.5 %collective-permute-start.9 = (bf16[128,512]{1,0:T(8,128)(2,1)S(1)}, bf16[128,512]{1,0:T(8,128)(2,1)S(1)}, u32[]{:S(2)}, u32[]{:S(2)}) collective-permute-start(bf16[128,512]{1,0:T(8,128)(2,1)S(1)} %get-tuple-element.37), channel_id=1, source_target_pairs={{0,6},{1,7},{2,4},{3,5},{4,2},{5,3},{6,0},{7,1},{8,14},{9,15},{10,... | collective-permute-start | bytes 393224 | tf_op jit(solution)/shard_map/ppermute | solution.py:399
  31.4 7.7 %collective-permute-start.4 = (s32[9,8,256]{2,1,0:T(8,128)S(1)}, s32[9,8,256]{2,1,0:T(8,128)S(1)}, u32[]{:S(2)}, u32[]{:S(2)}) collective-permute-start(s32[9,8,256]{2,1,0:T(8,128)S(1)} %get-tuple-element.32), channel_id=1, source_target_pairs={{0,1},{1,2},{2,3},{3,4},{4,5},{5,6},{6,7},{8,9},{9,10},{10,11},{11... | collective-permute-start | bytes 221192 | tf_op jit(solution)/shard_map/ppermute | solution.py:406
  33.2 6.4 %collective-permute-start.5 = (s32[9,8,256]{2,1,0:T(8,128)S(1)}, s32[9,8,256]{2,1,0:T(8,128)S(1)}, u32[]{:S(2)}, u32[]{:S(2)}) collective-permute-start(s32[9,8,256]{2,1,0:T(8,128)S(1)} %get-tuple-element.33), channel_id=1, source_target_pairs={{1,0},{2,1},{3,2},{4,3},{5,4},{6,5},{7,6},{9,8},{10,9},{11,10},{12... | collective-permute-start | bytes 221192 | tf_op jit(solution)/shard_map/ppermute | solution.py:406
  38.3 8.0 %collective-permute-start.11 = (bf16[144,512]{1,0:T(8,128)(2,1)}, bf16[144,512]{1,0:T(8,128)(2,1)S(1)}, u32[]{:S(2)}, u32[]{:S(2)}) collective-permute-start(bf16[144,512]{1,0:T(8,128)(2,1)} %get-tuple-element.40), channel_id=1, source_target_pairs={{0,3},{1,2},{2,1},{3,0},{4,7},{5,6},{6,5},{7,4},{8,11},{9,10},{10,... | collective-permute-start | bytes 442376 | tf_op jit(solution)/shard_map/ppermute | solution.py:399
  39.1 13.0 %collective-permute-start.12 = (bf16[144,512]{1,0:T(8,128)(2,1)}, bf16[144,512]{1,0:T(8,128)(2,1)S(1)}, u32[]{:S(2)}, u32[]{:S(2)}) collective-permute-start(bf16[144,512]{1,0:T(8,128)(2,1)} %get-tuple-element.41), channel_id=1, source_target_pairs={{0,4},{1,5},{2,6},{3,7},{4,0},{5,1},{6,2},{7,3},{8,12},{9,13},{10,... | collective-permute-start | bytes 442376 | tf_op jit(solution)/shard_map/ppermute | solution.py:399
  39.6 15.9 %collective-permute-start.13 = (bf16[144,512]{1,0:T(8,128)(2,1)}, bf16[144,512]{1,0:T(8,128)(2,1)S(1)}, u32[]{:S(2)}, u32[]{:S(2)}) collective-permute-start(bf16[144,512]{1,0:T(8,128)(2,1)} %get-tuple-element.42), channel_id=1, source_target_pairs={{0,5},{1,4},{2,7},{3,6},{4,1},{5,0},{6,3},{7,2},{8,13},{9,12},{10,... | collective-permute-start | bytes 442376 | tf_op jit(solution)/shard_map/ppermute | solution.py:399
  41.7 13.7 %collective-permute-start.14 = (bf16[144,512]{1,0:T(8,128)(2,1)}, bf16[144,512]{1,0:T(8,128)(2,1)S(1)}, u32[]{:S(2)}, u32[]{:S(2)}) collective-permute-start(bf16[144,512]{1,0:T(8,128)(2,1)} %get-tuple-element.43), channel_id=1, source_target_pairs={{0,6},{1,7},{2,4},{3,5},{4,2},{5,3},{6,0},{7,1},{8,14},{9,15},{10,... | collective-permute-start | bytes 442376 | tf_op jit(solution)/shard_map/ppermute | solution.py:399
  43.0 12.5 %collective-permute-start.15 = (bf16[144,512]{1,0:T(8,128)(2,1)}, bf16[144,512]{1,0:T(8,128)(2,1)S(1)}, u32[]{:S(2)}, u32[]{:S(2)}) collective-permute-start(bf16[144,512]{1,0:T(8,128)(2,1)} %get-tuple-element.44), channel_id=1, source_target_pairs={{0,7},{1,6},{2,5},{3,4},{4,3},{5,2},{6,1},{7,0},{8,15},{9,14},{10,... | collective-permute-start | bytes 442376 | tf_op jit(solution)/shard_map/ppermute | solution.py:399
  58.4 4.5 %collective-permute-start.16 = (bf16[144,256]{1,0:T(8,128)(2,1)S(1)}, bf16[144,256]{1,0:T(8,128)(2,1)S(1)}, u32[]{:S(2)}, u32[]{:S(2)}) collective-permute-start(bf16[144,256]{1,0:T(8,128)(2,1)S(1)} %get-tuple-element.46), channel_id=1, source_target_pairs={{0,8},{8,0},{16,24},{24,16},{1,9},{9,1},{17,25},{25,17},{2,10},{10... | collective-permute-start | bytes 221192 | tf_op jit(solution)/shard_map/ppermute | solution.py:399
  60.1 7.8 %collective-permute-start.17 = (bf16[144,256]{1,0:T(8,128)(2,1)S(1)}, bf16[144,256]{1,0:T(8,128)(2,1)S(1)}, u32[]{:S(2)}, u32[]{:S(2)}) collective-permute-start(bf16[144,256]{1,0:T(8,128)(2,1)S(1)} %get-tuple-element.47), channel_id=1, source_target_pairs={{0,16},{8,24},{16,0},{24,8},{1,17},{9,25},{17,1},{25,9},{2,18},{10... | collective-permute-start | bytes 221192 | tf_op jit(solution)/shard_map/ppermute | solution.py:399
  62.7 6.3 %collective-permute-start.18 = (bf16[144,256]{1,0:T(8,128)(2,1)S(1)}, bf16[144,256]{1,0:T(8,128)(2,1)S(1)}, u32[]{:S(2)}, u32[]{:S(2)}) collective-permute-start(bf16[144,256]{1,0:T(8,128)(2,1)S(1)} %get-tuple-element.48), channel_id=1, source_target_pairs={{0,24},{8,16},{16,8},{24,0},{1,25},{9,17},{17,9},{25,1},{2,26},{10... | collective-permute-start | bytes 221192 | tf_op jit(solution)/shard_map/ppermute | solution.py:399

commit v3 on v2

--- a/solution.py
+++ b/solution.py
@@ -194,10 +194,10 @@
     )(me, scale, field, *later)
 
 
-def lens_kernel(layout, parts, waves, block, me_ref, wave_ref, table, *rest):
+def lens_kernel(layout, parts, waves, block, extra, me_ref, wave_ref, table, *rest):
     kinds = len(layout)
     pieces, rest = rest[: kinds * parts], rest[kinds * parts :]
-    outs, tiles = rest[:waves], rest[waves]
+    outs, tiles = rest[extra : extra + waves], rest[extra + waves]
     me, wave = me_ref[0], wave_ref[0]
     half = table.shape[0] // 2
     samples = pieces[0].shape[1]
@@ -240,32 +240,33 @@
         outs[hop][...] = tiles[wave ^ hop]
 
 
-def lens_intensity(layout, parts, waves, block, me, wave, table, sent):
+def lens_intensity(layout, parts, waves, block, me, wave, table, sent, later):
     shape = (block + 2 * MARGIN, NQ // waves)
     pieces = [piece for part in sent for piece in part]
     return pl.pallas_call(
-        functools.partial(lens_kernel, layout, parts, waves, block),
+        functools.partial(lens_kernel, layout, parts, waves, block, len(later)),
         in_specs=[pl.BlockSpec(memory_space=pltpu.SMEM)] * 2
-        + [pl.BlockSpec(memory_space=pltpu.VMEM)] * (1 + len(pieces)),
+        + [pl.BlockSpec(memory_space=pltpu.VMEM)] * (1 + len(pieces))
+        + [pl.BlockSpec(memory_space=pl.ANY)] * len(later),
         out_specs=[pl.BlockSpec(memory_space=pltpu.VMEM)] * waves,
         out_shape=[jax.ShapeDtypeStruct(shape, BF16)] * waves,
         scratch_shapes=[pltpu.VMEM((waves, *shape), BF16)],
         compiler_params=pltpu.CompilerParams(vmem_limit_bytes=VMEM_LIMIT),
         cost_estimate=pl.CostEstimate(flops=1, bytes_accessed=1, transcendentals=0),
         name="lens_intensity",
-    )(me, wave, table, *pieces)
+    )(me, wave, table, *pieces, *later)
 
 
 def shifts(waves):
     return -(OFFSET // 4), (waves - 1 + OFFSET - 1 + LMAX - 1) // 4
 
 
-def block_light(amounts, masks, slots, at, waves, reach):
+def block_light(amounts, masks, slots, at, lanes, waves, reach):
     light = [[None] * 4 for _ in range(4)]
     near = pl.ds(at, 24)
-    slots_near = slots[near]
-    values_near = [amounts[wave, near] for wave in range(waves)]
-    masks_near = [masks[wave, near] for wave in range(waves)]
+    slots_near = slots[near, lanes]
+    values_near = [amounts[wave, near, lanes] for wave in range(waves)]
+    masks_near = [masks[wave, near, lanes] for wave in range(waves)]
     for shift in range(reach[0], reach[1] + 1):
         rows = slice(8 - shift, 16 - shift)
         slot = slots_near[rows]
@@ -290,13 +291,10 @@
     return light
 
 
-def put_planes(light, planes, at):
+def put_planes(light, planes, at, part):
     for step in range(4):
         for which in range(4):
-            value = light[step][which]
-            for part in range(value.shape[1] // LANES):
-                lanes = slice(part * LANES, (part + 1) * LANES)
-                planes.at[4 * part + which][pl.Slice(at + step, 8, 4), :] = value[:, lanes]
+            planes.at[4 * part + which][pl.Slice(at + step, 8, 4), :] = light[step][which]
 
 
 def spread(planes, out_ref, rows):
@@ -362,8 +360,10 @@
 
     def body(group, _):
         at = pl.multiple_of(group * 8, 8)
-        light = block_light(amounts, masks, slots, at, waves, shifts(waves))
-        put_planes(light, planes, at * 4)
+        for part in range(columns // LANES):
+            lanes = slice(part * LANES, (part + 1) * LANES)
+            light = block_light(amounts, masks, slots, at, lanes, waves, shifts(waves))
+            put_planes(light, planes, at * 4, part)
         return 0
 
     lax.fori_loop(0, block // 8, body, 0)
@@ -420,13 +420,13 @@
         later = [sent[-1][hop] for hop in FIRST if hop < parts] if sent else []
         pieces = half_transform(ranges, parts, block, me, wave_scale, lyot_field[0], later)
         sent.append(exchange(pieces, "row"))
-    later = [sent[NEAR[0]][hop] for hop in NEAR[1] if hop < parts]
+    later = [sent[-1][hop] for hop in AHEAD if hop < parts]
     up, down = edge_traces(trace_start, trace_length, column_slot, later)
     above = shifted(down, "row", 1)
     below = shifted(up, "row", -1)
-    later = [sent[-1][hop] for hop in AHEAD if hop < parts]
-    table = lens_table(wave_scale, lyot_field.shape[3], [*later, above, below])
-    intensity = lens_intensity(layout, parts, waves, block, me, wave, table, sent)
+    table = lens_table(wave_scale, lyot_field.shape[3], [*later, up])
+    later = [above, below]
+    intensity = lens_intensity(layout, parts, waves, block, me, wave, table, sent, later)
     tiles = exchange(intensity, "wave")
     return tile_light(
         waves, place, tiles, trace_start, trace_length, column_slot, above, below
@@ -436,7 +436,6 @@
 MARGIN = 8
 ROOM = 48
 AHEAD = (1, 2)
-NEAR = (0, (1,))
 ORDER = ()
 WIDTH = 4096
 SIZE = 512

time: 78.5 us -> 76.8 us (0.978); the launches traced: 78.3 us -> 75.7 us
  waiting for transfers between devices: 18.9 us -> 15.4 us
    ppermute x17, waiting for transfers between devices: 18.9 us -> 15.4 us  [exchange(): received[hop] = lax.ppermute(pieces[hop], axis, pairs)]
  transfers between devices with their start and end apart: 19 -> 19, of which waited for: 5 -> 4; matrix products, arithmetic and copies ran while one was open for 0% -> 0% of each run, Pallas kernels for 17% -> 18%
where the time goes in v3:
time: 76.8 us; the launch traced here: 75.7 us
  Pallas kernels  35.2 us (46%)
  starting transfers between devices  24.2 us (32%)
  waiting for transfers between devices  15.4 us (20%)
  between operations  0.79 us (1%)
    ppermute x17, starting transfers between devices, exchange(): received[hop] = lax.ppermute(pieces[hop], axis, pairs)  21.1 us
    pallas_call x2, Pallas kernels, half_transform(): pl.pallas_call(functools.partial(half_kernel, ranges, parts, block, width...  19.5 us
    ppermute x17, waiting for transfers between devices, exchange(): received[hop] = lax.ppermute(pieces[hop], axis, pairs)  15.4 us
    pallas_call x1, Pallas kernels, tile_light(): pl.pallas_call(functools.partial(tile_kernel, waves), in_specs=[pl.BlockS...  9.11 us
    ppermute x2, starting transfers between devices, shifted(): lax.ppermute(value, axis, [(source, source + steps) for source in range(i...  3.19 us
    pallas_call x1, Pallas kernels, lens_intensity(): pl.pallas_call(functools.partial(lens_kernel, layout, parts, waves, block...  2.96 us
    pallas_call x1, Pallas kernels, lens_table(): pl.pallas_call(table_kernel, in_specs=[pl.BlockSpec(memory_space=pltpu.SM...  2.89 us
  transfers between devices with their start and end apart: 19, of which 4 were waited for; matrix products, arithmetic and copies ran while one was open for 0% of the time, Pallas kernels for 18%

profile of v3, /device:TPU:0, one launch (start us, length us, event | category | flops | bytes accessed | tf_op | source)
XLA Modules:
  0.0 75.7 jit_solution(17862065035497286007)
XLA Ops:
  0.7 0.0 copy-start
  0.7 0.0 copy-start.1
  0.7 0.0 copy-start.2
  0.7 9.2 %half_transform.2 = (bf16[128,512]{1,0:T(8,128)(2,1)S(1)}, bf16[128,512]{1,0:T(8,128)(2,1)S(1)}, bf16[128,512]{1,0:T(8,128)(2,1)S(1)}, bf16[128,512]{1,0:T(8,128...) custom-call(s32[1]{0:T(128)} %bitcast.me_ref, ...), custom_call_target="tpu_custom_call" | custom-call | flops 1 | bytes 1 | tf_op jit(solution)/shard_map/half_transform/pallas_call | solution.py:177
  9.9 0.5 collective-permute-start
  10.4 2.6 %collective-permute-start.1 = (bf16[128,512]{1,0:T(8,128)(2,1)S(1)}, bf16[128,512]{1,0:T(8,128)(2,1)S(1)}, u32[]{:S(2)}, u32[]{:S(2)}) collective-permute-start(bf16[128,512]{1,0:T(8,128)(2,1)S(1)} %get-tuple-element.29), channel_id=1, source_target_pairs={{0,2},{1,3},{2,0},{3,1},{4,6},{5,7},{6,4},{7,5},{8,10},{9,11},{10,... | collective-permute-start | bytes 393224 | tf_op jit(solution)/shard_map/ppermute | solution.py:399
  12.9 0.1 collective-permute-start.4
  13.0 1.8 %collective-permute-start.5 = (bf16[128,512]{1,0:T(8,128)(2,1)S(1)}, bf16[128,512]{1,0:T(8,128)(2,1)S(1)}, u32[]{:S(2)}, u32[]{:S(2)}) collective-permute-start(bf16[128,512]{1,0:T(8,128)(2,1)S(1)} %get-tuple-element.34), channel_id=1, source_target_pairs={{0,4},{1,5},{2,6},{3,7},{4,0},{5,1},{6,2},{7,3},{8,12},{9,13},{10,... | collective-permute-start | bytes 393224 | tf_op jit(solution)/shard_map/ppermute | solution.py:399
  14.8 0.0 collective-permute-start.6
  14.8 0.0 collective-permute-done.rest_1_
  14.8 2.6 %collective-permute-start.7 = (bf16[128,512]{1,0:T(8,128)(2,1)S(1)}, bf16[128,512]{1,0:T(8,128)(2,1)S(1)}, u32[]{:S(2)}, u32[]{:S(2)}) collective-permute-start(bf16[128,512]{1,0:T(8,128)(2,1)S(1)} %get-tuple-element.36), channel_id=1, source_target_pairs={{0,6},{1,7},{2,4},{3,5},{4,2},{5,3},{6,0},{7,1},{8,14},{9,15},{10,... | collective-permute-start | bytes 393224 | tf_op jit(solution)/shard_map/ppermute | solution.py:399
  17.4 0.0 collective-permute-done.1.rest_2_
  17.4 10.3 %half_transform.3 = (bf16[144,512]{1,0:T(8,128)(2,1)S(1)}, bf16[144,512]{1,0:T(8,128)(2,1)S(1)}, bf16[144,512]{1,0:T(8,128)(2,1)S(1)}, bf16[144,512]{1,0:T(8,128...) custom-call(s32[1]{0:T(128)} %bitcast.me_ref, ...), custom_call_target="tpu_custom_call" | custom-call | flops 1 | bytes 1 | tf_op jit(solution)/shard_map/half_transform/pallas_call | solution.py:177
  27.8 0.2 collective-permute-start.2
  28.0 0.0 collective-permute-done.4.rest_3_
  28.0 1.8 %collective-permute-start.3 = (bf16[144,512]{1,0:T(8,128)(2,1)S(1)}, bf16[144,512]{1,0:T(8,128)(2,1)S(1)}, u32[]{:S(2)}, u32[]{:S(2)}) collective-permute-start(bf16[144,512]{1,0:T(8,128)(2,1)S(1)} %get-tuple-element.31), channel_id=1, source_target_pairs={{0,2},{1,3},{2,0},{3,1},{4,6},{5,7},{6,4},{7,5},{8,10},{9,11},{10,... | collective-permute-start | bytes 442376 | tf_op jit(solution)/shard_map/ppermute | solution.py:399
  29.8 0.0 collective-permute-done.5.rest_4_
  29.8 1.3 %collective-permute-start.8 = (bf16[128,512]{1,0:T(8,128)(2,1)S(1)}, bf16[128,512]{1,0:T(8,128)(2,1)S(1)}, u32[]{:S(2)}, u32[]{:S(2)}) collective-permute-start(bf16[128,512]{1,0:T(8,128)(2,1)S(1)} %get-tuple-element.37), channel_id=1, source_target_pairs={{0,7},{1,6},{2,5},{3,4},{4,3},{5,2},{6,1},{7,0},{8,15},{9,14},{10,... | collective-permute-start | bytes 393224 | tf_op jit(solution)/shard_map/ppermute | solution.py:399
  31.0 0.0 collective-permute-done.6.rest_5_
  31.0 0.3 collective-permute-start.10
  31.3 0.0 collective-permute-done.7.rest_6_
  31.4 1.4 %collective-permute-start.11 = (bf16[144,512]{1,0:T(8,128)(2,1)S(1)}, bf16[144,512]{1,0:T(8,128)(2,1)S(1)}, u32[]{:S(2)}, u32[]{:S(2)}) collective-permute-start(bf16[144,512]{1,0:T(8,128)(2,1)S(1)} %get-tuple-element.41), channel_id=1, source_target_pairs={{0,5},{1,4},{2,7},{3,6},{4,1},{5,0},{6,3},{7,2},{8,13},{9,12},{10,... | collective-permute-start | bytes 442376 | tf_op jit(solution)/shard_map/ppermute | solution.py:399
  32.7 5.1 %collective-permute-done.8.rest_7_ = bf16[128,512]{1,0:T(8,128)(2,1)S(1)} collective-permute-done((bf16[128,512]{1,0:T(8,128)(2,1)S(1)}, bf16[128,512]{1,0:T(8,128)(2,1)S(1)}, u32[]{:S(2)}, u32[]{:S(2)}) %collective-permute-start.8) | collective-permute-done | bytes 131104 | tf_op jit(solution)/shard_map/ppermute | solution.py:399
  37.9 1.4 %collective-permute-start.12 = (bf16[144,512]{1,0:T(8,128)(2,1)}, bf16[144,512]{1,0:T(8,128)(2,1)S(1)}, u32[]{:S(2)}, u32[]{:S(2)}) collective-permute-start(bf16[144,512]{1,0:T(8,128)(2,1)} %get-tuple-element.42), channel_id=1, source_target_pairs={{0,6},{1,7},{2,4},{3,5},{4,2},{5,3},{6,0},{7,1},{8,14},{9,15},{10,... | collective-permute-start | bytes 442376 | tf_op jit(solution)/shard_map/ppermute | solution.py:399
  39.3 0.0 collective-permute-done.2.rest_0_.rest_9_
  39.3 1.1 %collective-permute-start.13 = (bf16[144,512]{1,0:T(8,128)(2,1)}, bf16[144,512]{1,0:T(8,128)(2,1)S(1)}, u32[]{:S(2)}, u32[]{:S(2)}) collective-permute-start(bf16[144,512]{1,0:T(8,128)(2,1)} %get-tuple-element.43), channel_id=1, source_target_pairs={{0,7},{1,6},{2,5},{3,4},{4,3},{5,2},{6,1},{7,0},{8,15},{9,14},{10,... | collective-permute-start | bytes 442376 | tf_op jit(solution)/shard_map/ppermute | solution.py:399
  40.4 0.0 collective-permute-done.3.rest_1_.rest_10_
  40.4 1.6 %collective-permute-start.9 = (bf16[144,512]{1,0:T(8,128)(2,1)}, bf16[144,512]{1,0:T(8,128)(2,1)S(1)}, u32[]{:S(2)}, u32[]{:S(2)}) collective-permute-start(bf16[144,512]{1,0:T(8,128)(2,1)} %get-tuple-element.39), channel_id=1, source_target_pairs={{0,3},{1,2},{2,1},{3,0},{4,7},{5,6},{6,5},{7,4},{8,11},{9,10},{10,... | collective-permute-start | bytes 442376 | tf_op jit(solution)/shard_map/ppermute | solution.py:399
  42.0 0.0 copy-done
  42.0 0.0 copy-done.1
  42.0 0.0 copy-done.2
  42.0 0.7 edge_traces.1
  42.7 0.0 collective-permute-done.10.rest_12_
  42.7 1.9 %collective-permute-start.14 = (s32[9,8,256]{2,1,0:T(8,128)}, s32[9,8,256]{2,1,0:T(8,128)S(1)}, u32[]{:S(2)}, u32[]{:S(2)}) collective-permute-start(s32[9,8,256]{2,1,0:T(8,128)} %get-tuple-element.44), channel_id=1, source_target_pairs={{0,1},{1,2},{2,3},{3,4},{4,5},{5,6},{6,7},{8,9},{9,10},{10,11},{11... | collective-permute-start | bytes 221192 | tf_op jit(solution)/shard_map/ppermute | solution.py:406
  44.6 4.3 %collective-permute-done.11.rest_13_ = bf16[144,512]{1,0:T(8,128)(2,1)S(1)} collective-permute-done((bf16[144,512]{1,0:T(8,128)(2,1)S(1)}, bf16[144,512]{1,0:T(8,128)(2,1)S(1)}, u32[]{:S(2)}, u32[]{:S(2)}) %collective-permute-start.11) | collective-permute-done | bytes 147488 | tf_op jit(solution)/shard_map/ppermute | solution.py:399
  48.9 1.3 %collective-permute-start.15 = (s32[9,8,256]{2,1,0:T(8,128)}, s32[9,8,256]{2,1,0:T(8,128)S(1)}, u32[]{:S(2)}, u32[]{:S(2)}) collective-permute-start(s32[9,8,256]{2,1,0:T(8,128)} %get-tuple-element.32.rest_2_), channel_id=1, source_target_pairs={{1,0},{2,1},{3,2},{4,3},{5,4},{6,5},{7,6},{9,8},{10,9},{11,10},{12... | collective-permute-start | bytes 221192 | tf_op jit(solution)/shard_map/ppermute | solution.py:406
  50.2 2.9 %lens_table.1.table = bf16[1024,4096]{1,0:T(8,128)(2,1)S(1)} custom-call(f32[1]{0:T(128)S(6)} %copy.6.scale_ref, bf16[144,512]{1,0:T(8,128)(2,1)S(1)} %collective-permute-done.2.rest_0_.rest_9_, bf16[144,512]{1,0:T(8,128)(2,1)S(1)} %collective-permute-done.3.rest_1_.rest_10_, s32[9,8,256]{2,1,0:T(8,128)} %get-tuple-element.32.rest_2_), custom_call_target="tpu_custom_call" | custom-call | flops 1 | bytes 1 | tf_op jit(solution)/shard_map/lens_table/pallas_call | solution.py:101
  53.0 0.0 collective-permute-done.12.rest_14_
  53.1 0.0 collective-permute-done.13.rest_15_
  53.1 0.0 collective-permute-done.9.rest_11_
  53.1 0.0 collective-permute-done.14.rest_16_.rest_7_
  53.1 0.0 collective-permute-done.15.rest_17_.rest_8_
  53.1 3.0 %lens_intensity.1 = (bf16[144,256]{1,0:T(8,128)(2,1)S(1)}, bf16[144,256]{1,0:T(8,128)(2,1)S(1)}, bf16[144,256]{1,0:T(8,128)(2,1)S(1)}, bf16[144,256]{1,0:T(8,128)(2,1)S(1)}) custom-call(s32[1]{0:T(128)} %bitcast.me_ref, s32[1]{0:T(128)} %bitcast.1.wave_ref, bf16[1024,4096]{1,0:T(8,128)(2,1)S(1)} %lens_table.1.table, ...), custom_call_target="tpu_custom_call" | custom-call | flops 1 | bytes 1 | tf_op jit(solution)/shard_map/lens_intensity/pallas_call | solution.py:246
  56.1 1.6 %collective-permute-start.16 = (bf16[144,256]{1,0:T(8,128)(2,1)S(1)}, bf16[144,256]{1,0:T(8,128)(2,1)S(1)}, u32[]{:S(2)}, u32[]{:S(2)}) collective-permute-start(bf16[144,256]{1,0:T(8,128)(2,1)S(1)} %get-tuple-element.46), channel_id=1, source_target_pairs={{0,8},{8,0},{16,24},{24,16},{1,9},{9,1},{17,25},{25,17},{2,10},{10... | collective-permute-start | bytes 221192 | tf_op jit(solution)/shard_map/ppermute | solution.py:399
  57.7 2.6 %collective-permute-start.17 = (bf16[144,256]{1,0:T(8,128)(2,1)S(1)}, bf16[144,256]{1,0:T(8,128)(2,1)S(1)}, u32[]{:S(2)}, u32[]{:S(2)}) collective-permute-start(bf16[144,256]{1,0:T(8,128)(2,1)S(1)} %get-tuple-element.47), channel_id=1, source_target_pairs={{0,16},{8,24},{16,0},{24,8},{1,17},{9,25},{17,1},{25,9},{2,18},{10... | collective-permute-start | bytes 221192 | tf_op jit(solution)/shard_map/ppermute | solution.py:399
  60.3 0.2 collective-permute-start.18
  60.5 0.1 pad_add_fusion.place_ref
  60.6 0.0 collective-permute-done.16.rest_1_
  60.6 3.5 %collective-permute-done.17.rest_2_ = bf16[144,256]{1,0:T(8,128)(2,1)S(1)} collective-permute-done((bf16[144,256]{1,0:T(8,128)(2,1)S(1)}, bf16[144,256]{1,0:T(8,128)(2,1)S(1)}, u32[]{:S(2)}, u32[]{:S(2)}) %collective-permute-start.17) | collective-permute-done | bytes 73760 | tf_op jit(solution)/shard_map/ppermute | solution.py:399
  64.1 2.5 %collective-permute-done.18.rest_3_ = bf16[144,256]{1,0:T(8,128)(2,1)S(1)} collective-permute-done((bf16[144,256]{1,0:T(8,128)(2,1)S(1)}, bf16[144,256]{1,0:T(8,128)(2,1)S(1)}, u32[]{:S(2)}, u32[]{:S(2)}) %collective-permute-start.18) | collective-permute-done | bytes 73760 | tf_op jit(solution)/shard_map/ppermute | solution.py:399
  66.6 9.1 %tile_light.1 = f32[512,1024]{1,0:T(8,128)} custom-call(s32[2]{0:T(128)S(1)} %pad_add_fusion.place_ref, bf16[144,256]{1,0:T(8,128)(2,1)S(1)} %get-tuple-element.45.rest_0_, bf16[144,256]{1,0:T(8,128)(2,1)S(1)} %collective-permute-done.16.rest_1_, bf16[144,256]{1,0:T(8,128)(2,1)S(1)} %collective-permute-done.17.rest_2_, ...), custom_call_target="tpu_custom_call" | custom-call | flops 1 | bytes 1 | tf_op jit(solution)/shard_map/tile_light/pallas_call | solution.py:376
Async XLA Ops:
  0.7 41.3 %copy-start = (s32[4,128,256]{2,1,0:T(8,128)S(1)}, s32[4,128,256]{2,1,0:T(8,128)}, u32[]{:S(2)}) copy-start(s32[4,128,256]{2,1,0:T(8,128)} %rest_4_.1) | copy-start | bytes 1572868
  0.7 41.3 %copy-start.1 = (s32[4,128,256]{2,1,0:T(8,128)S(1)}, s32[4,128,256]{2,1,0:T(8,128)}, u32[]{:S(2)}) copy-start(s32[4,128,256]{2,1,0:T(8,128)} %rest_5_.1) | copy-start | bytes 1572868
  0.7 41.3 %copy-start.2 = (s32[128,256]{1,0:T(8,128)S(1)}, s32[128,256]{1,0:T(8,128)}, u32[]{:S(2)}) copy-start(s32[128,256]{1,0:T(8,128)} %rest_6_.1) | copy-start | bytes 393220
  9.9 4.9 %collective-permute-start = (bf16[128,512]{1,0:T(8,128)(2,1)S(1)}, bf16[128,512]{1,0:T(8,128)(2,1)S(1)}, u32[]{:S(2)}, u32[]{:S(2)}) collective-permute-start(bf16[128,512]{1,0:T(8,128)(2,1)S(1)} %get-tuple-element.28), channel_id=1, source_target_pairs={{0,1},{1,0},{2,3},{3,2},{4,5},{5,4},{6,7},{7,6},{8,9},{9,8},{10,11... | collective-permute-start | bytes 393224 | tf_op jit(solution)/shard_map/ppermute | solution.py:399
  10.4 7.0 %collective-permute-start.1 = (bf16[128,512]{1,0:T(8,128)(2,1)S(1)}, bf16[128,512]{1,0:T(8,128)(2,1)S(1)}, u32[]{:S(2)}, u32[]{:S(2)}) collective-permute-start(bf16[128,512]{1,0:T(8,128)(2,1)S(1)} %get-tuple-element.29), channel_id=1, source_target_pairs={{0,2},{1,3},{2,0},{3,1},{4,6},{5,7},{6,4},{7,5},{8,10},{9,11},{10,... | collective-permute-start | bytes 393224 | tf_op jit(solution)/shard_map/ppermute | solution.py:399
  12.9 15.0 %collective-permute-start.4 = (bf16[128,512]{1,0:T(8,128)(2,1)S(1)}, bf16[128,512]{1,0:T(8,128)(2,1)S(1)}, u32[]{:S(2)}, u32[]{:S(2)}) collective-permute-start(bf16[128,512]{1,0:T(8,128)(2,1)S(1)} %get-tuple-element.33), channel_id=1, source_target_pairs={{0,3},{1,2},{2,1},{3,0},{4,7},{5,6},{6,5},{7,4},{8,11},{9,10},{10,... | collective-permute-start | bytes 393224 | tf_op jit(solution)/shard_map/ppermute | solution.py:399
  13.0 16.7 %collective-permute-start.5 = (bf16[128,512]{1,0:T(8,128)(2,1)S(1)}, bf16[128,512]{1,0:T(8,128)(2,1)S(1)}, u32[]{:S(2)}, u32[]{:S(2)}) collective-permute-start(bf16[128,512]{1,0:T(8,128)(2,1)S(1)} %get-tuple-element.34), channel_id=1, source_target_pairs={{0,4},{1,5},{2,6},{3,7},{4,0},{5,1},{6,2},{7,3},{8,12},{9,13},{10,... | collective-permute-start | bytes 393224 | tf_op jit(solution)/shard_map/ppermute | solution.py:399
  14.8 16.2 %collective-permute-start.6 = (bf16[128,512]{1,0:T(8,128)(2,1)S(1)}, bf16[128,512]{1,0:T(8,128)(2,1)S(1)}, u32[]{:S(2)}, u32[]{:S(2)}) collective-permute-start(bf16[128,512]{1,0:T(8,128)(2,1)S(1)} %get-tuple-element.35), channel_id=1, source_target_pairs={{0,5},{1,4},{2,7},{3,6},{4,1},{5,0},{6,3},{7,2},{8,13},{9,12},{10,... | collective-permute-start | bytes 393224 | tf_op jit(solution)/shard_map/ppermute | solution.py:399
  14.8 16.5 %collective-permute-start.7 = (bf16[128,512]{1,0:T(8,128)(2,1)S(1)}, bf16[128,512]{1,0:T(8,128)(2,1)S(1)}, u32[]{:S(2)}, u32[]{:S(2)}) collective-permute-start(bf16[128,512]{1,0:T(8,128)(2,1)S(1)} %get-tuple-element.36), channel_id=1, source_target_pairs={{0,6},{1,7},{2,4},{3,5},{4,2},{5,3},{6,0},{7,1},{8,14},{9,15},{10,... | collective-permute-start | bytes 393224 | tf_op jit(solution)/shard_map/ppermute | solution.py:399
  27.8 11.5 %collective-permute-start.2 = (bf16[144,512]{1,0:T(8,128)(2,1)S(1)}, bf16[144,512]{1,0:T(8,128)(2,1)S(1)}, u32[]{:S(2)}, u32[]{:S(2)}) collective-permute-start(bf16[144,512]{1,0:T(8,128)(2,1)S(1)} %get-tuple-element.30), channel_id=1, source_target_pairs={{0,1},{1,0},{2,3},{3,2},{4,5},{5,4},{6,7},{7,6},{8,9},{9,8},{10,11... | collective-permute-start | bytes 442376 | tf_op jit(solution)/shard_map/ppermute | solution.py:399
  28.0 12.4 %collective-permute-start.3 = (bf16[144,512]{1,0:T(8,128)(2,1)S(1)}, bf16[144,512]{1,0:T(8,128)(2,1)S(1)}, u32[]{:S(2)}, u32[]{:S(2)}) collective-permute-start(bf16[144,512]{1,0:T(8,128)(2,1)S(1)} %get-tuple-element.31), channel_id=1, source_target_pairs={{0,2},{1,3},{2,0},{3,1},{4,6},{5,7},{6,4},{7,5},{8,10},{9,11},{10,... | collective-permute-start | bytes 442376 | tf_op jit(solution)/shard_map/ppermute | solution.py:399
  29.8 8.1 %collective-permute-start.8 = (bf16[128,512]{1,0:T(8,128)(2,1)S(1)}, bf16[128,512]{1,0:T(8,128)(2,1)S(1)}, u32[]{:S(2)}, u32[]{:S(2)}) collective-permute-start(bf16[128,512]{1,0:T(8,128)(2,1)S(1)} %get-tuple-element.37), channel_id=1, source_target_pairs={{0,7},{1,6},{2,5},{3,4},{4,3},{5,2},{6,1},{7,0},{8,15},{9,14},{10,... | collective-permute-start | bytes 393224 | tf_op jit(solution)/shard_map/ppermute | solution.py:399
  31.0 11.6 %collective-permute-start.10 = (bf16[144,512]{1,0:T(8,128)(2,1)S(1)}, bf16[144,512]{1,0:T(8,128)(2,1)S(1)}, u32[]{:S(2)}, u32[]{:S(2)}) collective-permute-start(bf16[144,512]{1,0:T(8,128)(2,1)S(1)} %get-tuple-element.40), channel_id=1, source_target_pairs={{0,4},{1,5},{2,6},{3,7},{4,0},{5,1},{6,2},{7,3},{8,12},{9,13},{10,... | collective-permute-start | bytes 442376 | tf_op jit(solution)/shard_map/ppermute | solution.py:399
  31.4 17.5 %collective-permute-start.11 = (bf16[144,512]{1,0:T(8,128)(2,1)S(1)}, bf16[144,512]{1,0:T(8,128)(2,1)S(1)}, u32[]{:S(2)}, u32[]{:S(2)}) collective-permute-start(bf16[144,512]{1,0:T(8,128)(2,1)S(1)} %get-tuple-element.41), channel_id=1, source_target_pairs={{0,5},{1,4},{2,7},{3,6},{4,1},{5,0},{6,3},{7,2},{8,13},{9,12},{10,... | collective-permute-start | bytes 442376 | tf_op jit(solution)/shard_map/ppermute | solution.py:399
  37.9 15.2 %collective-permute-start.12 = (bf16[144,512]{1,0:T(8,128)(2,1)}, bf16[144,512]{1,0:T(8,128)(2,1)S(1)}, u32[]{:S(2)}, u32[]{:S(2)}) collective-permute-start(bf16[144,512]{1,0:T(8,128)(2,1)} %get-tuple-element.42), channel_id=1, source_target_pairs={{0,6},{1,7},{2,4},{3,5},{4,2},{5,3},{6,0},{7,1},{8,14},{9,15},{10,... | collective-permute-start | bytes 442376 | tf_op jit(solution)/shard_map/ppermute | solution.py:399
  39.3 13.8 %collective-permute-start.13 = (bf16[144,512]{1,0:T(8,128)(2,1)}, bf16[144,512]{1,0:T(8,128)(2,1)S(1)}, u32[]{:S(2)}, u32[]{:S(2)}) collective-permute-start(bf16[144,512]{1,0:T(8,128)(2,1)} %get-tuple-element.43), channel_id=1, source_target_pairs={{0,7},{1,6},{2,5},{3,4},{4,3},{5,2},{6,1},{7,0},{8,15},{9,14},{10,... | collective-permute-start | bytes 442376 | tf_op jit(solution)/shard_map/ppermute | solution.py:399
  40.4 12.6 %collective-permute-start.9 = (bf16[144,512]{1,0:T(8,128)(2,1)}, bf16[144,512]{1,0:T(8,128)(2,1)S(1)}, u32[]{:S(2)}, u32[]{:S(2)}) collective-permute-start(bf16[144,512]{1,0:T(8,128)(2,1)} %get-tuple-element.39), channel_id=1, source_target_pairs={{0,3},{1,2},{2,1},{3,0},{4,7},{5,6},{6,5},{7,4},{8,11},{9,10},{10,... | collective-permute-start | bytes 442376 | tf_op jit(solution)/shard_map/ppermute | solution.py:399
  42.7 10.4 %collective-permute-start.14 = (s32[9,8,256]{2,1,0:T(8,128)}, s32[9,8,256]{2,1,0:T(8,128)S(1)}, u32[]{:S(2)}, u32[]{:S(2)}) collective-permute-start(s32[9,8,256]{2,1,0:T(8,128)} %get-tuple-element.44), channel_id=1, source_target_pairs={{0,1},{1,2},{2,3},{3,4},{4,5},{5,6},{6,7},{8,9},{9,10},{10,11},{11... | collective-permute-start | bytes 221192 | tf_op jit(solution)/shard_map/ppermute | solution.py:406
  48.9 4.2 %collective-permute-start.15 = (s32[9,8,256]{2,1,0:T(8,128)}, s32[9,8,256]{2,1,0:T(8,128)S(1)}, u32[]{:S(2)}, u32[]{:S(2)}) collective-permute-start(s32[9,8,256]{2,1,0:T(8,128)} %get-tuple-element.32.rest_2_), channel_id=1, source_target_pairs={{1,0},{2,1},{3,2},{4,3},{5,4},{6,5},{7,6},{9,8},{10,9},{11,10},{12... | collective-permute-start | bytes 221192 | tf_op jit(solution)/shard_map/ppermute | solution.py:406
  56.1 4.5 %collective-permute-start.16 = (bf16[144,256]{1,0:T(8,128)(2,1)S(1)}, bf16[144,256]{1,0:T(8,128)(2,1)S(1)}, u32[]{:S(2)}, u32[]{:S(2)}) collective-permute-start(bf16[144,256]{1,0:T(8,128)(2,1)S(1)} %get-tuple-element.46), channel_id=1, source_target_pairs={{0,8},{8,0},{16,24},{24,16},{1,9},{9,1},{17,25},{25,17},{2,10},{10... | collective-permute-start | bytes 221192 | tf_op jit(solution)/shard_map/ppermute | solution.py:399
  57.7 6.4 %collective-permute-start.17 = (bf16[144,256]{1,0:T(8,128)(2,1)S(1)}, bf16[144,256]{1,0:T(8,128)(2,1)S(1)}, u32[]{:S(2)}, u32[]{:S(2)}) collective-permute-start(bf16[144,256]{1,0:T(8,128)(2,1)S(1)} %get-tuple-element.47), channel_id=1, source_target_pairs={{0,16},{8,24},{16,0},{24,8},{1,17},{9,25},{17,1},{25,9},{2,18},{10... | collective-permute-start | bytes 221192 | tf_op jit(solution)/shard_map/ppermute | solution.py:399
  60.3 6.3 %collective-permute-start.18 = (bf16[144,256]{1,0:T(8,128)(2,1)S(1)}, bf16[144,256]{1,0:T(8,128)(2,1)S(1)}, u32[]{:S(2)}, u32[]{:S(2)}) collective-permute-start(bf16[144,256]{1,0:T(8,128)(2,1)S(1)} %get-tuple-element.48), channel_id=1, source_target_pairs={{0,24},{8,16},{16,8},{24,0},{1,25},{9,17},{17,9},{25,1},{2,26},{10... | collective-permute-start | bytes 221192 | tf_op jit(solution)/shard_map/ppermute | solution.py:399

commit v4 on v3

--- a/solution.py
+++ b/solution.py
@@ -41,11 +41,6 @@
     for order in (14, 12, 10, 8, 6, 4, 2, 0):
         cosine = cosine * square + (-1.0) ** (order // 2) / math.factorial(order)
     return 1.0 - 2.0 * sine * sine, 2.0 * sine * cosine
-
-
-def chunk_rows(block, halo):
-    edge = block // 4 - halo
-    return (((-halo, edge), (block - edge, block + halo)), ((edge, block - edge),))
 
 
 def count_of(ranges):
@@ -414,7 +409,7 @@
     me, wave = row_index.reshape(1), wave_index.reshape(1)
     place = jnp.stack([row_index, wave_index])
     halo = 4 * -(-max(shifts(waves)[1], -shifts(waves)[0]) // 4)
-    layout = chunk_rows(block, halo)
+    layout = (((-halo, block + halo),),)
     sent = []
     for ranges in layout:
         later = [sent[-1][hop] for hop in FIRST if hop < parts] if sent else []

time: 76.8 us -> 68.7 us (0.89); the launches traced: 75.7 us -> 68.5 us
  starting transfers between devices: 24.2 us -> 18 us
  Pallas kernels: 35.2 us -> 31.5 us
  waiting for transfers between devices: 15.4 us -> 18.1 us
    ppermute x17 -> x10, starting transfers between devices: 21.1 us -> 13.5 us  [exchange(): received[hop] = lax.ppermute(pieces[hop], axis, pairs)]
    pallas_call x2 -> x1, Pallas kernels: 19.5 us -> 15.9 us  [half_transform(): pl.pallas_call(functools.partial(half_kernel, ranges, parts, block, width...]
    ppermute x17 -> x10, waiting for transfers between devices: 15.4 us -> 18.1 us  [exchange(): received[hop] = lax.ppermute(pieces[hop], axis, pairs)]
    ppermute x2, starting transfers between devices: 3.19 us -> 4.45 us  [shifted(): lax.ppermute(value, axis, [(source, source + steps) for source in range(i...]
  transfers between devices with their start and end apart: 19 -> 12, of which waited for: 4 -> 6; matrix products, arithmetic and copies ran while one was open for 0% -> 0% of each run, Pallas kernels for 18% -> 5%
where the time goes in v4:
time: 68.7 us; the launch traced here: 68.5 us
  Pallas kernels  31.5 us (46%)
  waiting for transfers between devices  18.1 us (26%)
  starting transfers between devices  18 us (26%)
  between operations  0.83 us (1%)
    ppermute x10, waiting for transfers between devices, exchange(): received[hop] = lax.ppermute(pieces[hop], axis, pairs)  18.1 us
    pallas_call x1, Pallas kernels, half_transform(): pl.pallas_call(functools.partial(half_kernel, ranges, parts, block, width...  15.9 us
    ppermute x10, starting transfers between devices, exchange(): received[hop] = lax.ppermute(pieces[hop], axis, pairs)  13.5 us
    pallas_call x1, Pallas kernels, tile_light(): pl.pallas_call(functools.partial(tile_kernel, waves), in_specs=[pl.BlockS...  9.11 us
    ppermute x2, starting transfers between devices, shifted(): lax.ppermute(value, axis, [(source, source + steps) for source in range(i...  4.45 us
    pallas_call x1, Pallas kernels, lens_intensity(): pl.pallas_call(functools.partial(lens_kernel, layout, parts, waves, block...  2.96 us
    pallas_call x1, Pallas kernels, lens_table(): pl.pallas_call(table_kernel, in_specs=[pl.BlockSpec(memory_space=pltpu.SM...  2.89 us
  transfers between devices with their start and end apart: 12, of which 6 were waited for; matrix products, arithmetic and copies ran while one was open for 0% of the time, Pallas kernels for 5%

profile of v4, /device:TPU:0, one launch (start us, length us, event | category | flops | bytes accessed | tf_op | source)
XLA Modules:
  0.0 68.5 jit_solution(2810302509595672033)
XLA Ops:
  0.0 0.0 copy-start
  0.0 0.0 copy-start.1
  0.0 0.0 copy-start.2
  0.8 15.9 %half_transform.1 = (bf16[272,512]{1,0:T(8,128)(2,1)S(1)}, bf16[272,512]{1,0:T(8,128)(2,1)S(1)}, bf16[272,512]{1,0:T(8,128)(2,1)S(1)}, bf16[272,512]{1,0:T(8,128...) custom-call(s32[1]{0:T(128)} %bitcast.me_ref, ...), custom_call_target="tpu_custom_call" | custom-call | flops 1 | bytes 1 | tf_op jit(solution)/shard_map/half_transform/pallas_call | solution.py:172
  16.6 0.5 collective-permute-start
  17.2 2.6 %collective-permute-start.1 = (bf16[272,512]{1,0:T(8,128)(2,1)S(1)}, bf16[272,512]{1,0:T(8,128)(2,1)S(1)}, u32[]{:S(2)}, u32[]{:S(2)}) collective-permute-start(bf16[272,512]{1,0:T(8,128)(2,1)S(1)} %get-tuple-element.20), channel_id=1, source_target_pairs={{0,2},{1,3},{2,0},{3,1},{4,6},{5,7},{6,4},{7,5},{8,10},{9,11},{10,... | collective-permute-start | bytes 835592 | tf_op jit(solution)/shard_map/ppermute | solution.py:394
  19.7 0.1 collective-permute-start.2
  19.8 1.8 %collective-permute-start.3 = (bf16[272,512]{1,0:T(8,128)(2,1)S(1)}, bf16[272,512]{1,0:T(8,128)(2,1)S(1)}, u32[]{:S(2)}, u32[]{:S(2)}) collective-permute-start(bf16[272,512]{1,0:T(8,128)(2,1)S(1)} %get-tuple-element.24), channel_id=1, source_target_pairs={{0,4},{1,5},{2,6},{3,7},{4,0},{5,1},{6,2},{7,3},{8,12},{9,13},{10,... | collective-permute-start | bytes 835592 | tf_op jit(solution)/shard_map/ppermute | solution.py:394
  21.6 0.0 collective-permute-start.4
  21.6 0.0 collective-permute-done.rest_0_.rest_1_
  21.6 2.6 %collective-permute-start.5 = (bf16[272,512]{1,0:T(8,128)(2,1)}, bf16[272,512]{1,0:T(8,128)(2,1)S(1)}, u32[]{:S(2)}, u32[]{:S(2)}) collective-permute-start(bf16[272,512]{1,0:T(8,128)(2,1)} %get-tuple-element.26), channel_id=1, source_target_pairs={{0,6},{1,7},{2,4},{3,5},{4,2},{5,3},{6,0},{7,1},{8,14},{9,15},{10,... | collective-permute-start | bytes 835592 | tf_op jit(solution)/shard_map/ppermute | solution.py:394
  24.2 3.0 %collective-permute-done.1.rest_1_.rest_2_ = bf16[272,512]{1,0:T(8,128)(2,1)S(1)} collective-permute-done((bf16[272,512]{1,0:T(8,128)(2,1)S(1)}, bf16[272,512]{1,0:T(8,128)(2,1)S(1)}, u32[]{:S(2)}, u32[]{:S(2)}) %collective-permute-start.1) | collective-permute-done | bytes 278560 | tf_op jit(solution)/shard_map/ppermute | solution.py:394
  27.2 1.7 %collective-permute-start.6 = (bf16[272,512]{1,0:T(8,128)(2,1)}, bf16[272,512]{1,0:T(8,128)(2,1)S(1)}, u32[]{:S(2)}, u32[]{:S(2)}) collective-permute-start(bf16[272,512]{1,0:T(8,128)(2,1)} %get-tuple-element.27), channel_id=1, source_target_pairs={{0,7},{1,6},{2,5},{3,4},{4,3},{5,2},{6,1},{7,0},{8,15},{9,14},{10,... | collective-permute-start | bytes 835592 | tf_op jit(solution)/shard_map/ppermute | solution.py:394
  29.0 0.0 copy-done
  29.0 0.0 copy-done.1
  29.0 0.0 copy-done.2
  29.0 0.7 edge_traces.1
  29.6 3.0 %collective-permute-done.2.rest_3_ = bf16[272,512]{1,0:T(8,128)(2,1)S(1)} collective-permute-done((bf16[272,512]{1,0:T(8,128)(2,1)S(1)}, bf16[272,512]{1,0:T(8,128)(2,1)S(1)}, u32[]{:S(2)}, u32[]{:S(2)}) %collective-permute-start.2) | collective-permute-done | bytes 278560 | tf_op jit(solution)/shard_map/ppermute | solution.py:394
  32.7 1.3 %collective-permute-start.8 = (s32[9,8,256]{2,1,0:T(8,128)}, s32[9,8,256]{2,1,0:T(8,128)S(1)}, u32[]{:S(2)}, u32[]{:S(2)}) collective-permute-start(s32[9,8,256]{2,1,0:T(8,128)} %get-tuple-element.21.rest_2_), channel_id=1, source_target_pairs={{1,0},{2,1},{3,2},{4,3},{5,4},{6,5},{7,6},{9,8},{10,9},{11,10},{12... | collective-permute-start | bytes 221192 | tf_op jit(solution)/shard_map/ppermute | solution.py:401
  34.0 0.0 collective-permute-done.3.rest_4_
  34.0 3.2 %collective-permute-start.7 = (s32[9,8,256]{2,1,0:T(8,128)}, s32[9,8,256]{2,1,0:T(8,128)S(1)}, u32[]{:S(2)}, u32[]{:S(2)}) collective-permute-start(s32[9,8,256]{2,1,0:T(8,128)} %get-tuple-element.28), channel_id=1, source_target_pairs={{0,1},{1,2},{2,3},{3,4},{4,5},{5,6},{6,7},{8,9},{9,10},{10,11},{11... | collective-permute-start | bytes 221192 | tf_op jit(solution)/shard_map/ppermute | solution.py:401
  37.2 2.9 %lens_table.1.table = bf16[1024,4096]{1,0:T(8,128)(2,1)S(1)} custom-call(f32[1]{0:T(128)S(6)} %copy.6.scale_ref, bf16[272,512]{1,0:T(8,128)(2,1)S(1)} %collective-permute-done.rest_0_.rest_1_, bf16[272,512]{1,0:T(8,128)(2,1)S(1)} %collective-permute-done.1.rest_1_.rest_2_, s32[9,8,256]{2,1,0:T(8,128)} %get-tuple-element.21.rest_2_), custom_call_target="tpu_custom_call" | custom-call | flops 1 | bytes 1 | tf_op jit(solution)/shard_map/lens_table/pallas_call | solution.py:96
  40.1 6.7 %collective-permute-done.4.rest_5_ = bf16[272,512]{1,0:T(8,128)(2,1)S(1)} collective-permute-done((bf16[272,512]{1,0:T(8,128)(2,1)}, bf16[272,512]{1,0:T(8,128)(2,1)S(1)}, u32[]{:S(2)}, u32[]{:S(2)}) %collective-permute-start.4) | collective-permute-done | bytes 278560 | tf_op jit(solution)/shard_map/ppermute | solution.py:394
  46.8 0.0 collective-permute-done.5.rest_6_
  46.8 0.0 collective-permute-done.6.rest_7_
  46.8 0.0 collective-permute-done.8.rest_9_.rest_8_
  46.8 0.0 collective-permute-done.7.rest_8_.rest_7_
  46.8 3.0 %lens_intensity.1 = (bf16[144,256]{1,0:T(8,128)(2,1)S(1)}, bf16[144,256]{1,0:T(8,128)(2,1)S(1)}, bf16[144,256]{1,0:T(8,128)(2,1)S(1)}, bf16[144,256]{1,0:T(8,128)(2,1)S(1)}) custom-call(s32[1]{0:T(128)} %bitcast.me_ref, s32[1]{0:T(128)} %bitcast.1.wave_ref, bf16[1024,4096]{1,0:T(8,128)(2,1)S(1)} %lens_table.1.table, ...), custom_call_target="tpu_custom_call" | custom-call | flops 1 | bytes 1 | tf_op jit(solution)/shard_map/lens_intensity/pallas_call | solution.py:241
  49.8 2.7 %collective-permute-start.10 = (bf16[144,256]{1,0:T(8,128)(2,1)S(1)}, bf16[144,256]{1,0:T(8,128)(2,1)S(1)}, u32[]{:S(2)}, u32[]{:S(2)}) collective-permute-start(bf16[144,256]{1,0:T(8,128)(2,1)S(1)} %get-tuple-element.31), channel_id=1, source_target_pairs={{0,16},{8,24},{16,0},{24,8},{1,17},{9,25},{17,1},{25,9},{2,18},{10... | collective-permute-start | bytes 221192 | tf_op jit(solution)/shard_map/ppermute | solution.py:394
  52.4 1.3 %collective-permute-start.11 = (bf16[144,256]{1,0:T(8,128)(2,1)S(1)}, bf16[144,256]{1,0:T(8,128)(2,1)S(1)}, u32[]{:S(2)}, u32[]{:S(2)}) collective-permute-start(bf16[144,256]{1,0:T(8,128)(2,1)S(1)} %get-tuple-element.32), channel_id=1, source_target_pairs={{0,24},{8,16},{16,8},{24,0},{1,25},{9,17},{17,9},{25,1},{2,26},{10... | collective-permute-start | bytes 221192 | tf_op jit(solution)/shard_map/ppermute | solution.py:394
  53.8 0.2 collective-permute-start.9
  54.0 0.1 pad_add_fusion.place_ref
  54.1 3.9 %collective-permute-done.10.rest_2_ = bf16[144,256]{1,0:T(8,128)(2,1)S(1)} collective-permute-done((bf16[144,256]{1,0:T(8,128)(2,1)S(1)}, bf16[144,256]{1,0:T(8,128)(2,1)S(1)}, u32[]{:S(2)}, u32[]{:S(2)}) %collective-permute-start.10) | collective-permute-done | bytes 73760 | tf_op jit(solution)/shard_map/ppermute | solution.py:394
  57.9 1.0 %collective-permute-done.11.rest_3_ = bf16[144,256]{1,0:T(8,128)(2,1)S(1)} collective-permute-done((bf16[144,256]{1,0:T(8,128)(2,1)S(1)}, bf16[144,256]{1,0:T(8,128)(2,1)S(1)}, u32[]{:S(2)}, u32[]{:S(2)}) %collective-permute-start.11) | collective-permute-done | bytes 73760 | tf_op jit(solution)/shard_map/ppermute | solution.py:394
  59.0 0.4 collective-permute-done.9.rest_1_
  59.4 9.1 %tile_light.1 = f32[512,1024]{1,0:T(8,128)} custom-call(s32[2]{0:T(128)S(1)} %pad_add_fusion.place_ref, bf16[144,256]{1,0:T(8,128)(2,1)S(1)} %get-tuple-element.29.rest_0_, bf16[144,256]{1,0:T(8,128)(2,1)S(1)} %collective-permute-done.9.rest_1_, bf16[144,256]{1,0:T(8,128)(2,1)S(1)} %collective-permute-done.10.rest_2_, ...), custom_call_target="tpu_custom_call" | custom-call | flops 1 | bytes 1 | tf_op jit(solution)/shard_map/tile_light/pallas_call | solution.py:371
Async XLA Ops:
  0.0 29.0 %copy-start = (s32[4,128,256]{2,1,0:T(8,128)S(1)}, s32[4,128,256]{2,1,0:T(8,128)}, u32[]{:S(2)}) copy-start(s32[4,128,256]{2,1,0:T(8,128)} %rest_4_.1) | copy-start | bytes 1572868
  0.0 29.0 %copy-start.1 = (s32[4,128,256]{2,1,0:T(8,128)S(1)}, s32[4,128,256]{2,1,0:T(8,128)}, u32[]{:S(2)}) copy-start(s32[4,128,256]{2,1,0:T(8,128)} %rest_5_.1) | copy-start | bytes 1572868
  0.0 29.0 %copy-start.2 = (s32[128,256]{1,0:T(8,128)S(1)}, s32[128,256]{1,0:T(8,128)}, u32[]{:S(2)}) copy-start(s32[128,256]{1,0:T(8,128)} %rest_6_.1) | copy-start | bytes 393220
  16.6 4.9 %collective-permute-start = (bf16[272,512]{1,0:T(8,128)(2,1)S(1)}, bf16[272,512]{1,0:T(8,128)(2,1)S(1)}, u32[]{:S(2)}, u32[]{:S(2)}) collective-permute-start(bf16[272,512]{1,0:T(8,128)(2,1)S(1)} %get-tuple-element.19), channel_id=1, source_target_pairs={{0,1},{1,0},{2,3},{3,2},{4,5},{5,4},{6,7},{7,6},{8,9},{9,8},{10,11... | collective-permute-start | bytes 835592 | tf_op jit(solution)/shard_map/ppermute | solution.py:394
  17.2 10.1 %collective-permute-start.1 = (bf16[272,512]{1,0:T(8,128)(2,1)S(1)}, bf16[272,512]{1,0:T(8,128)(2,1)S(1)}, u32[]{:S(2)}, u32[]{:S(2)}) collective-permute-start(bf16[272,512]{1,0:T(8,128)(2,1)S(1)} %get-tuple-element.20), channel_id=1, source_target_pairs={{0,2},{1,3},{2,0},{3,1},{4,6},{5,7},{6,4},{7,5},{8,10},{9,11},{10,... | collective-permute-start | bytes 835592 | tf_op jit(solution)/shard_map/ppermute | solution.py:394
  19.7 13.0 %collective-permute-start.2 = (bf16[272,512]{1,0:T(8,128)(2,1)S(1)}, bf16[272,512]{1,0:T(8,128)(2,1)S(1)}, u32[]{:S(2)}, u32[]{:S(2)}) collective-permute-start(bf16[272,512]{1,0:T(8,128)(2,1)S(1)} %get-tuple-element.23), channel_id=1, source_target_pairs={{0,3},{1,2},{2,1},{3,0},{4,7},{5,6},{6,5},{7,4},{8,11},{9,10},{10,... | collective-permute-start | bytes 835592 | tf_op jit(solution)/shard_map/ppermute | solution.py:394
  19.8 14.2 %collective-permute-start.3 = (bf16[272,512]{1,0:T(8,128)(2,1)S(1)}, bf16[272,512]{1,0:T(8,128)(2,1)S(1)}, u32[]{:S(2)}, u32[]{:S(2)}) collective-permute-start(bf16[272,512]{1,0:T(8,128)(2,1)S(1)} %get-tuple-element.24), channel_id=1, source_target_pairs={{0,4},{1,5},{2,6},{3,7},{4,0},{5,1},{6,2},{7,3},{8,12},{9,13},{10,... | collective-permute-start | bytes 835592 | tf_op jit(solution)/shard_map/ppermute | solution.py:394
  21.6 25.2 %collective-permute-start.4 = (bf16[272,512]{1,0:T(8,128)(2,1)}, bf16[272,512]{1,0:T(8,128)(2,1)S(1)}, u32[]{:S(2)}, u32[]{:S(2)}) collective-permute-start(bf16[272,512]{1,0:T(8,128)(2,1)} %get-tuple-element.25), channel_id=1, source_target_pairs={{0,5},{1,4},{2,7},{3,6},{4,1},{5,0},{6,3},{7,2},{8,13},{9,12},{10,... | collective-permute-start | bytes 835592 | tf_op jit(solution)/shard_map/ppermute | solution.py:394
  21.6 25.2 %collective-permute-start.5 = (bf16[272,512]{1,0:T(8,128)(2,1)}, bf16[272,512]{1,0:T(8,128)(2,1)S(1)}, u32[]{:S(2)}, u32[]{:S(2)}) collective-permute-start(bf16[272,512]{1,0:T(8,128)(2,1)} %get-tuple-element.26), channel_id=1, source_target_pairs={{0,6},{1,7},{2,4},{3,5},{4,2},{5,3},{6,0},{7,1},{8,14},{9,15},{10,... | collective-permute-start | bytes 835592 | tf_op jit(solution)/shard_map/ppermute | solution.py:394
  27.2 19.6 %collective-permute-start.6 = (bf16[272,512]{1,0:T(8,128)(2,1)}, bf16[272,512]{1,0:T(8,128)(2,1)S(1)}, u32[]{:S(2)}, u32[]{:S(2)}) collective-permute-start(bf16[272,512]{1,0:T(8,128)(2,1)} %get-tuple-element.27), channel_id=1, source_target_pairs={{0,7},{1,6},{2,5},{3,4},{4,3},{5,2},{6,1},{7,0},{8,15},{9,14},{10,... | collective-permute-start | bytes 835592 | tf_op jit(solution)/shard_map/ppermute | solution.py:394
  32.7 14.1 %collective-permute-start.8 = (s32[9,8,256]{2,1,0:T(8,128)}, s32[9,8,256]{2,1,0:T(8,128)S(1)}, u32[]{:S(2)}, u32[]{:S(2)}) collective-permute-start(s32[9,8,256]{2,1,0:T(8,128)} %get-tuple-element.21.rest_2_), channel_id=1, source_target_pairs={{1,0},{2,1},{3,2},{4,3},{5,4},{6,5},{7,6},{9,8},{10,9},{11,10},{12... | collective-permute-start | bytes 221192 | tf_op jit(solution)/shard_map/ppermute | solution.py:401
  34.0 12.8 %collective-permute-start.7 = (s32[9,8,256]{2,1,0:T(8,128)}, s32[9,8,256]{2,1,0:T(8,128)S(1)}, u32[]{:S(2)}, u32[]{:S(2)}) collective-permute-start(s32[9,8,256]{2,1,0:T(8,128)} %get-tuple-element.28), channel_id=1, source_target_pairs={{0,1},{1,2},{2,3},{3,4},{4,5},{5,6},{6,7},{8,9},{9,10},{10,11},{11... | collective-permute-start | bytes 221192 | tf_op jit(solution)/shard_map/ppermute | solution.py:401
  49.8 8.2 %collective-permute-start.10 = (bf16[144,256]{1,0:T(8,128)(2,1)S(1)}, bf16[144,256]{1,0:T(8,128)(2,1)S(1)}, u32[]{:S(2)}, u32[]{:S(2)}) collective-permute-start(bf16[144,256]{1,0:T(8,128)(2,1)S(1)} %get-tuple-element.31), channel_id=1, source_target_pairs={{0,16},{8,24},{16,0},{24,8},{1,17},{9,25},{17,1},{25,9},{2,18},{10... | collective-permute-start | bytes 221192 | tf_op jit(solution)/shard_map/ppermute | solution.py:394
  52.4 6.5 %collective-permute-start.11 = (bf16[144,256]{1,0:T(8,128)(2,1)S(1)}, bf16[144,256]{1,0:T(8,128)(2,1)S(1)}, u32[]{:S(2)}, u32[]{:S(2)}) collective-permute-start(bf16[144,256]{1,0:T(8,128)(2,1)S(1)} %get-tuple-element.32), channel_id=1, source_target_pairs={{0,24},{8,16},{16,8},{24,0},{1,25},{9,17},{17,9},{25,1},{2,26},{10... | collective-permute-start | bytes 221192 | tf_op jit(solution)/shard_map/ppermute | solution.py:394
  53.8 5.6 %collective-permute-start.9 = (bf16[144,256]{1,0:T(8,128)(2,1)S(1)}, bf16[144,256]{1,0:T(8,128)(2,1)S(1)}, u32[]{:S(2)}, u32[]{:S(2)}) collective-permute-start(bf16[144,256]{1,0:T(8,128)(2,1)S(1)} %get-tuple-element.30), channel_id=1, source_target_pairs={{0,8},{8,0},{16,24},{24,16},{1,9},{9,1},{17,25},{25,17},{2,10},{10... | collective-permute-start | bytes 221192 | tf_op jit(solution)/shard_map/ppermute | solution.py:394

commit v5 on v4

--- a/solution.py
+++ b/solution.py
@@ -256,17 +256,13 @@
     return -(OFFSET // 4), (waves - 1 + OFFSET - 1 + LMAX - 1) // 4
 
 
-def block_light(amounts, masks, slots, at, lanes, waves, reach):
+def block_light(amounts, masks, slots, at, part, waves, reach):
     light = [[None] * 4 for _ in range(4)]
-    near = pl.ds(at, 24)
-    slots_near = slots[near, lanes]
-    values_near = [amounts[wave, near, lanes] for wave in range(waves)]
-    masks_near = [masks[wave, near, lanes] for wave in range(waves)]
     for shift in range(reach[0], reach[1] + 1):
-        rows = slice(8 - shift, 16 - shift)
-        slot = slots_near[rows]
-        value = [held[rows] for held in values_near]
-        mask = [held[rows] for held in masks_near]
+        rows = pl.Slice(2 * (at + MARGIN - shift), 8, 2)
+        slot = slots.at[part][rows, :]
+        value = [amounts.at[wave, part][rows, :] for wave in range(waves)]
+        mask = [masks.at[wave, part][rows, :] for wave in range(waves)]
         picks = [slot == which for which in range(4)]
         for step in range(4):
             height = 4 * shift + step
@@ -340,9 +336,16 @@
     lens0 = place_ref[0] * block
     own = slice(MARGIN, block + MARGIN)
     edges = ((slice(0, MARGIN), above), (slice(block + MARGIN, block + 2 * MARGIN), below))
-    slots[own] = slot[...]
+    every = range(columns // LANES)
+
+    def keep(ref, rows, value):
+        for part in every:
+            here = pl.Slice(2 * rows.start, rows.stop - rows.start, 2)
+            ref.at[part][here, :] = value[:, part * LANES : (part + 1) * LANES]
+
+    keep(slots, own, slot[...])
     for rows, edge in edges:
-        slots[rows] = edge[2 * waves]
+        keep(slots, rows, edge[2 * waves])
     for hop in range(waves):
         which = place_ref[1] ^ hop
         tile = tiles[hop][...].astype(F32)
@@ -350,14 +353,15 @@
         parts += [(rows, edge[which], edge[waves + which]) for rows, edge in edges]
         for rows, start, length in parts:
             lens = lens0 + rows.start - MARGIN + iota(start.shape, 0)
-            amounts[which, rows] = tile[rows] / jnp.maximum(length, 1).astype(F32)
-            masks[which, rows] = ((1 << length) - 1) << jnp.maximum(start - 4 * lens + OFFSET, 0)
+            amount = tile[rows] / jnp.maximum(length, 1).astype(F32)
+            keep(amounts.at[which], rows, amount)
+            mask = ((1 << length) - 1) << jnp.maximum(start - 4 * lens + OFFSET, 0)
+            keep(masks.at[which], rows, mask)
 
     def body(group, _):
         at = pl.multiple_of(group * 8, 8)
         for part in range(columns // LANES):
-            lanes = slice(part * LANES, (part + 1) * LANES)
-            light = block_light(amounts, masks, slots, at, lanes, waves, shifts(waves))
+            light = block_light(amounts, masks, slots, at, part, waves, shifts(waves))
             put_planes(light, planes, at * 4, part)
         return 0
 
@@ -375,9 +379,9 @@
         out_specs=pl.BlockSpec(memory_space=pltpu.VMEM),
         out_shape=jax.ShapeDtypeStruct((4 * block, 4 * columns), F32),
         scratch_shapes=[
-            pltpu.VMEM((waves, high, columns), F32),
-            pltpu.VMEM((waves, high, columns), jnp.int32),
-            pltpu.VMEM((high, columns), jnp.int32),
+            pltpu.VMEM((waves, columns // LANES, 2 * high, LANES), F32),
+            pltpu.VMEM((waves, columns // LANES, 2 * high, LANES), jnp.int32),
+            pltpu.VMEM((columns // LANES, 2 * high, LANES), jnp.int32),
             pltpu.VMEM((4 * columns // LANES, 4 * block, LANES), F32),
         ],
         compiler_params=pltpu.CompilerParams(vmem_limit_bytes=VMEM_LIMIT),

time: 68.7 us -> 66 us (0.961)
  Pallas kernels: 31.5 us -> 28.8 us
    pallas_call x1, Pallas kernels: 9.11 us -> 6.43 us  [tile_light(): pl.pallas_call(functools.partial(tile_kernel, waves), in_specs=[pl.BlockS...]
where the time goes in v5:
time: 66 us; the launch traced here: 65.8 us
  Pallas kernels  28.8 us (44%)
  waiting for transfers between devices  18.1 us (27%)
  starting transfers between devices  18 us (27%)
  between operations  0.83 us (1%)
    ppermute x10, waiting for transfers between devices, exchange(): received[hop] = lax.ppermute(pieces[hop], axis, pairs)  18.1 us
    pallas_call x1, Pallas kernels, half_transform(): pl.pallas_call(functools.partial(half_kernel, ranges, parts, block, width...  15.9 us
    ppermute x10, starting transfers between devices, exchange(): received[hop] = lax.ppermute(pieces[hop], axis, pairs)  13.5 us
    pallas_call x1, Pallas kernels, tile_light(): pl.pallas_call(functools.partial(tile_kernel, waves), in_specs=[pl.BlockS...  6.43 us
    ppermute x2, starting transfers between devices, shifted(): lax.ppermute(value, axis, [(source, source + steps) for source in range(i...  4.45 us
    pallas_call x1, Pallas kernels, lens_intensity(): pl.pallas_call(functools.partial(lens_kernel, layout, parts, waves, block...  2.96 us
    pallas_call x1, Pallas kernels, lens_table(): pl.pallas_call(table_kernel, in_specs=[pl.BlockSpec(memory_space=pltpu.SM...  2.89 us
  transfers between devices with their start and end apart: 12, of which 6 were waited for; matrix products, arithmetic and copies ran while one was open for 0% of the time, Pallas kernels for 5%

profile of v5, /device:TPU:0, one launch (start us, length us, event | category | flops | bytes accessed | tf_op | source)
XLA Modules:
  0.0 65.8 jit_solution(384946475841680537)
XLA Ops:
  0.0 0.0 copy-start
  0.0 0.0 copy-start.1
  0.0 0.0 copy-start.2
  0.8 15.9 %half_transform.1 = (bf16[272,512]{1,0:T(8,128)(2,1)S(1)}, bf16[272,512]{1,0:T(8,128)(2,1)S(1)}, bf16[272,512]{1,0:T(8,128)(2,1)S(1)}, bf16[272,512]{1,0:T(8,128...) custom-call(s32[1]{0:T(128)} %bitcast.me_ref, ...), custom_call_target="tpu_custom_call" | custom-call | flops 1 | bytes 1 | tf_op jit(solution)/shard_map/half_transform/pallas_call | solution.py:172
  16.6 0.5 collective-permute-start
  17.2 2.6 %collective-permute-start.1 = (bf16[272,512]{1,0:T(8,128)(2,1)S(1)}, bf16[272,512]{1,0:T(8,128)(2,1)S(1)}, u32[]{:S(2)}, u32[]{:S(2)}) collective-permute-start(bf16[272,512]{1,0:T(8,128)(2,1)S(1)} %get-tuple-element.20), channel_id=1, source_target_pairs={{0,2},{1,3},{2,0},{3,1},{4,6},{5,7},{6,4},{7,5},{8,10},{9,11},{10,... | collective-permute-start | bytes 835592 | tf_op jit(solution)/shard_map/ppermute | solution.py:398
  19.7 0.1 collective-permute-start.2
  19.8 1.8 %collective-permute-start.3 = (bf16[272,512]{1,0:T(8,128)(2,1)S(1)}, bf16[272,512]{1,0:T(8,128)(2,1)S(1)}, u32[]{:S(2)}, u32[]{:S(2)}) collective-permute-start(bf16[272,512]{1,0:T(8,128)(2,1)S(1)} %get-tuple-element.24), channel_id=1, source_target_pairs={{0,4},{1,5},{2,6},{3,7},{4,0},{5,1},{6,2},{7,3},{8,12},{9,13},{10,... | collective-permute-start | bytes 835592 | tf_op jit(solution)/shard_map/ppermute | solution.py:398
  21.6 0.0 collective-permute-start.4
  21.6 0.0 collective-permute-done.rest_0_.rest_1_
  21.6 2.6 %collective-permute-start.5 = (bf16[272,512]{1,0:T(8,128)(2,1)}, bf16[272,512]{1,0:T(8,128)(2,1)S(1)}, u32[]{:S(2)}, u32[]{:S(2)}) collective-permute-start(bf16[272,512]{1,0:T(8,128)(2,1)} %get-tuple-element.26), channel_id=1, source_target_pairs={{0,6},{1,7},{2,4},{3,5},{4,2},{5,3},{6,0},{7,1},{8,14},{9,15},{10,... | collective-permute-start | bytes 835592 | tf_op jit(solution)/shard_map/ppermute | solution.py:398
  24.2 3.0 %collective-permute-done.1.rest_1_.rest_2_ = bf16[272,512]{1,0:T(8,128)(2,1)S(1)} collective-permute-done((bf16[272,512]{1,0:T(8,128)(2,1)S(1)}, bf16[272,512]{1,0:T(8,128)(2,1)S(1)}, u32[]{:S(2)}, u32[]{:S(2)}) %collective-permute-start.1) | collective-permute-done | bytes 278560 | tf_op jit(solution)/shard_map/ppermute | solution.py:398
  27.2 1.7 %collective-permute-start.6 = (bf16[272,512]{1,0:T(8,128)(2,1)}, bf16[272,512]{1,0:T(8,128)(2,1)S(1)}, u32[]{:S(2)}, u32[]{:S(2)}) collective-permute-start(bf16[272,512]{1,0:T(8,128)(2,1)} %get-tuple-element.27), channel_id=1, source_target_pairs={{0,7},{1,6},{2,5},{3,4},{4,3},{5,2},{6,1},{7,0},{8,15},{9,14},{10,... | collective-permute-start | bytes 835592 | tf_op jit(solution)/shard_map/ppermute | solution.py:398
  29.0 0.0 copy-done
  29.0 0.0 copy-done.1
  29.0 0.0 copy-done.2
  29.0 0.7 %edge_traces.1 = (s32[9,8,256]{2,1,0:T(8,128)}, s32[9,8,256]{2,1,0:T(8,128)}) custom-call(s32[4,128,256]{2,1,0:T(8,128)S(1)} %copy-done, s32[4,128,256]{2,1,0:T(8,128)S(1)} %copy-done.1, s32[128,256]{1,0:T(8,128)S(1)} %copy-done.2, bf16[272,512]{1,0:T(8,128)(2,1)S(1)} %collective-permute-done.rest_0_.rest_1_, ...), custom_call_target="tpu_custom_call" | custom-call | flops 1 | bytes 1 | tf_op jit(solution)/shard_map/edge_traces/pallas_call | solution.py:320
  29.6 3.0 %collective-permute-done.2.rest_3_ = bf16[272,512]{1,0:T(8,128)(2,1)S(1)} collective-permute-done((bf16[272,512]{1,0:T(8,128)(2,1)S(1)}, bf16[272,512]{1,0:T(8,128)(2,1)S(1)}, u32[]{:S(2)}, u32[]{:S(2)}) %collective-permute-start.2) | collective-permute-done | bytes 278560 | tf_op jit(solution)/shard_map/ppermute | solution.py:398
  32.7 1.3 %collective-permute-start.8 = (s32[9,8,256]{2,1,0:T(8,128)}, s32[9,8,256]{2,1,0:T(8,128)S(1)}, u32[]{:S(2)}, u32[]{:S(2)}) collective-permute-start(s32[9,8,256]{2,1,0:T(8,128)} %get-tuple-element.21.rest_2_), channel_id=1, source_target_pairs={{1,0},{2,1},{3,2},{4,3},{5,4},{6,5},{7,6},{9,8},{10,9},{11,10},{12... | collective-permute-start | bytes 221192 | tf_op jit(solution)/shard_map/ppermute | solution.py:405
  34.0 0.0 collective-permute-done.3.rest_4_
  34.0 3.2 %collective-permute-start.7 = (s32[9,8,256]{2,1,0:T(8,128)}, s32[9,8,256]{2,1,0:T(8,128)S(1)}, u32[]{:S(2)}, u32[]{:S(2)}) collective-permute-start(s32[9,8,256]{2,1,0:T(8,128)} %get-tuple-element.28), channel_id=1, source_target_pairs={{0,1},{1,2},{2,3},{3,4},{4,5},{5,6},{6,7},{8,9},{9,10},{10,11},{11... | collective-permute-start | bytes 221192 | tf_op jit(solution)/shard_map/ppermute | solution.py:405
  37.2 2.9 %lens_table.1.table = bf16[1024,4096]{1,0:T(8,128)(2,1)S(1)} custom-call(f32[1]{0:T(128)S(6)} %copy.6.scale_ref, bf16[272,512]{1,0:T(8,128)(2,1)S(1)} %collective-permute-done.rest_0_.rest_1_, bf16[272,512]{1,0:T(8,128)(2,1)S(1)} %collective-permute-done.1.rest_1_.rest_2_, s32[9,8,256]{2,1,0:T(8,128)} %get-tuple-element.21.rest_2_), custom_call_target="tpu_custom_call" | custom-call | flops 1 | bytes 1 | tf_op jit(solution)/shard_map/lens_table/pallas_call | solution.py:96
  40.1 6.7 %collective-permute-done.4.rest_5_ = bf16[272,512]{1,0:T(8,128)(2,1)S(1)} collective-permute-done((bf16[272,512]{1,0:T(8,128)(2,1)}, bf16[272,512]{1,0:T(8,128)(2,1)S(1)}, u32[]{:S(2)}, u32[]{:S(2)}) %collective-permute-start.4) | collective-permute-done | bytes 278560 | tf_op jit(solution)/shard_map/ppermute | solution.py:398
  46.8 0.0 collective-permute-done.5.rest_6_
  46.8 0.0 collective-permute-done.6.rest_7_
  46.8 0.0 collective-permute-done.8.rest_9_.rest_8_
  46.8 0.0 collective-permute-done.7.rest_8_.rest_7_
  46.8 3.0 %lens_intensity.1 = (bf16[144,256]{1,0:T(8,128)(2,1)S(1)}, bf16[144,256]{1,0:T(8,128)(2,1)S(1)}, bf16[144,256]{1,0:T(8,128)(2,1)S(1)}, bf16[144,256]{1,0:T(8,128)(2,1)S(1)}) custom-call(s32[1]{0:T(128)} %bitcast.me_ref, s32[1]{0:T(128)} %bitcast.1.wave_ref, bf16[1024,4096]{1,0:T(8,128)(2,1)S(1)} %lens_table.1.table, ...), custom_call_target="tpu_custom_call" | custom-call | flops 1 | bytes 1 | tf_op jit(solution)/shard_map/lens_intensity/pallas_call | solution.py:241
  49.8 2.7 %collective-permute-start.10 = (bf16[144,256]{1,0:T(8,128)(2,1)S(1)}, bf16[144,256]{1,0:T(8,128)(2,1)S(1)}, u32[]{:S(2)}, u32[]{:S(2)}) collective-permute-start(bf16[144,256]{1,0:T(8,128)(2,1)S(1)} %get-tuple-element.31), channel_id=1, source_target_pairs={{0,16},{8,24},{16,0},{24,8},{1,17},{9,25},{17,1},{25,9},{2,18},{10... | collective-permute-start | bytes 221192 | tf_op jit(solution)/shard_map/ppermute | solution.py:398
  52.4 1.3 %collective-permute-start.11 = (bf16[144,256]{1,0:T(8,128)(2,1)S(1)}, bf16[144,256]{1,0:T(8,128)(2,1)S(1)}, u32[]{:S(2)}, u32[]{:S(2)}) collective-permute-start(bf16[144,256]{1,0:T(8,128)(2,1)S(1)} %get-tuple-element.32), channel_id=1, source_target_pairs={{0,24},{8,16},{16,8},{24,0},{1,25},{9,17},{17,9},{25,1},{2,26},{10... | collective-permute-start | bytes 221192 | tf_op jit(solution)/shard_map/ppermute | solution.py:398
  53.8 0.2 collective-permute-start.9
  54.0 0.1 pad_add_fusion.place_ref
  54.1 3.9 %collective-permute-done.10.rest_2_ = bf16[144,256]{1,0:T(8,128)(2,1)S(1)} collective-permute-done((bf16[144,256]{1,0:T(8,128)(2,1)S(1)}, bf16[144,256]{1,0:T(8,128)(2,1)S(1)}, u32[]{:S(2)}, u32[]{:S(2)}) %collective-permute-start.10) | collective-permute-done | bytes 73760 | tf_op jit(solution)/shard_map/ppermute | solution.py:398
  57.9 1.0 %collective-permute-done.11.rest_3_ = bf16[144,256]{1,0:T(8,128)(2,1)S(1)} collective-permute-done((bf16[144,256]{1,0:T(8,128)(2,1)S(1)}, bf16[144,256]{1,0:T(8,128)(2,1)S(1)}, u32[]{:S(2)}, u32[]{:S(2)}) %collective-permute-start.11) | collective-permute-done | bytes 73760 | tf_op jit(solution)/shard_map/ppermute | solution.py:398
  59.0 0.4 collective-permute-done.9.rest_1_
  59.4 6.4 %tile_light.1 = f32[512,1024]{1,0:T(8,128)} custom-call(s32[2]{0:T(128)S(1)} %pad_add_fusion.place_ref, bf16[144,256]{1,0:T(8,128)(2,1)S(1)} %get-tuple-element.29.rest_0_, bf16[144,256]{1,0:T(8,128)(2,1)S(1)} %collective-permute-done.9.rest_1_, bf16[144,256]{1,0:T(8,128)(2,1)S(1)} %collective-permute-done.10.rest_2_, ...), custom_call_target="tpu_custom_call" | custom-call | flops 1 | bytes 1 | tf_op jit(solution)/shard_map/tile_light/pallas_call | solution.py:375
Async XLA Ops:
  0.0 29.0 %copy-start = (s32[4,128,256]{2,1,0:T(8,128)S(1)}, s32[4,128,256]{2,1,0:T(8,128)}, u32[]{:S(2)}) copy-start(s32[4,128,256]{2,1,0:T(8,128)} %rest_4_.1) | copy-start | bytes 1572868
  0.0 29.0 %copy-start.1 = (s32[4,128,256]{2,1,0:T(8,128)S(1)}, s32[4,128,256]{2,1,0:T(8,128)}, u32[]{:S(2)}) copy-start(s32[4,128,256]{2,1,0:T(8,128)} %rest_5_.1) | copy-start | bytes 1572868
  0.0 29.0 %copy-start.2 = (s32[128,256]{1,0:T(8,128)S(1)}, s32[128,256]{1,0:T(8,128)}, u32[]{:S(2)}) copy-start(s32[128,256]{1,0:T(8,128)} %rest_6_.1) | copy-start | bytes 393220
  16.6 4.9 %collective-permute-start = (bf16[272,512]{1,0:T(8,128)(2,1)S(1)}, bf16[272,512]{1,0:T(8,128)(2,1)S(1)}, u32[]{:S(2)}, u32[]{:S(2)}) collective-permute-start(bf16[272,512]{1,0:T(8,128)(2,1)S(1)} %get-tuple-element.19), channel_id=1, source_target_pairs={{0,1},{1,0},{2,3},{3,2},{4,5},{5,4},{6,7},{7,6},{8,9},{9,8},{10,11... | collective-permute-start | bytes 835592 | tf_op jit(solution)/shard_map/ppermute | solution.py:398
  17.2 10.1 %collective-permute-start.1 = (bf16[272,512]{1,0:T(8,128)(2,1)S(1)}, bf16[272,512]{1,0:T(8,128)(2,1)S(1)}, u32[]{:S(2)}, u32[]{:S(2)}) collective-permute-start(bf16[272,512]{1,0:T(8,128)(2,1)S(1)} %get-tuple-element.20), channel_id=1, source_target_pairs={{0,2},{1,3},{2,0},{3,1},{4,6},{5,7},{6,4},{7,5},{8,10},{9,11},{10,... | collective-permute-start | bytes 835592 | tf_op jit(solution)/shard_map/ppermute | solution.py:398
  19.7 13.0 %collective-permute-start.2 = (bf16[272,512]{1,0:T(8,128)(2,1)S(1)}, bf16[272,512]{1,0:T(8,128)(2,1)S(1)}, u32[]{:S(2)}, u32[]{:S(2)}) collective-permute-start(bf16[272,512]{1,0:T(8,128)(2,1)S(1)} %get-tuple-element.23), channel_id=1, source_target_pairs={{0,3},{1,2},{2,1},{3,0},{4,7},{5,6},{6,5},{7,4},{8,11},{9,10},{10,... | collective-permute-start | bytes 835592 | tf_op jit(solution)/shard_map/ppermute | solution.py:398
  19.8 14.2 %collective-permute-start.3 = (bf16[272,512]{1,0:T(8,128)(2,1)S(1)}, bf16[272,512]{1,0:T(8,128)(2,1)S(1)}, u32[]{:S(2)}, u32[]{:S(2)}) collective-permute-start(bf16[272,512]{1,0:T(8,128)(2,1)S(1)} %get-tuple-element.24), channel_id=1, source_target_pairs={{0,4},{1,5},{2,6},{3,7},{4,0},{5,1},{6,2},{7,3},{8,12},{9,13},{10,... | collective-permute-start | bytes 835592 | tf_op jit(solution)/shard_map/ppermute | solution.py:398
  21.6 25.2 %collective-permute-start.4 = (bf16[272,512]{1,0:T(8,128)(2,1)}, bf16[272,512]{1,0:T(8,128)(2,1)S(1)}, u32[]{:S(2)}, u32[]{:S(2)}) collective-permute-start(bf16[272,512]{1,0:T(8,128)(2,1)} %get-tuple-element.25), channel_id=1, source_target_pairs={{0,5},{1,4},{2,7},{3,6},{4,1},{5,0},{6,3},{7,2},{8,13},{9,12},{10,... | collective-permute-start | bytes 835592 | tf_op jit(solution)/shard_map/ppermute | solution.py:398
  21.6 25.2 %collective-permute-start.5 = (bf16[272,512]{1,0:T(8,128)(2,1)}, bf16[272,512]{1,0:T(8,128)(2,1)S(1)}, u32[]{:S(2)}, u32[]{:S(2)}) collective-permute-start(bf16[272,512]{1,0:T(8,128)(2,1)} %get-tuple-element.26), channel_id=1, source_target_pairs={{0,6},{1,7},{2,4},{3,5},{4,2},{5,3},{6,0},{7,1},{8,14},{9,15},{10,... | collective-permute-start | bytes 835592 | tf_op jit(solution)/shard_map/ppermute | solution.py:398
  27.2 19.6 %collective-permute-start.6 = (bf16[272,512]{1,0:T(8,128)(2,1)}, bf16[272,512]{1,0:T(8,128)(2,1)S(1)}, u32[]{:S(2)}, u32[]{:S(2)}) collective-permute-start(bf16[272,512]{1,0:T(8,128)(2,1)} %get-tuple-element.27), channel_id=1, source_target_pairs={{0,7},{1,6},{2,5},{3,4},{4,3},{5,2},{6,1},{7,0},{8,15},{9,14},{10,... | collective-permute-start | bytes 835592 | tf_op jit(solution)/shard_map/ppermute | solution.py:398
  32.7 14.1 %collective-permute-start.8 = (s32[9,8,256]{2,1,0:T(8,128)}, s32[9,8,256]{2,1,0:T(8,128)S(1)}, u32[]{:S(2)}, u32[]{:S(2)}) collective-permute-start(s32[9,8,256]{2,1,0:T(8,128)} %get-tuple-element.21.rest_2_), channel_id=1, source_target_pairs={{1,0},{2,1},{3,2},{4,3},{5,4},{6,5},{7,6},{9,8},{10,9},{11,10},{12... | collective-permute-start | bytes 221192 | tf_op jit(solution)/shard_map/ppermute | solution.py:405
  34.0 12.8 %collective-permute-start.7 = (s32[9,8,256]{2,1,0:T(8,128)}, s32[9,8,256]{2,1,0:T(8,128)S(1)}, u32[]{:S(2)}, u32[]{:S(2)}) collective-permute-start(s32[9,8,256]{2,1,0:T(8,128)} %get-tuple-element.28), channel_id=1, source_target_pairs={{0,1},{1,2},{2,3},{3,4},{4,5},{5,6},{6,7},{8,9},{9,10},{10,11},{11... | collective-permute-start | bytes 221192 | tf_op jit(solution)/shard_map/ppermute | solution.py:405
  49.8 8.2 %collective-permute-start.10 = (bf16[144,256]{1,0:T(8,128)(2,1)S(1)}, bf16[144,256]{1,0:T(8,128)(2,1)S(1)}, u32[]{:S(2)}, u32[]{:S(2)}) collective-permute-start(bf16[144,256]{1,0:T(8,128)(2,1)S(1)} %get-tuple-element.31), channel_id=1, source_target_pairs={{0,16},{8,24},{16,0},{24,8},{1,17},{9,25},{17,1},{25,9},{2,18},{10... | collective-permute-start | bytes 221192 | tf_op jit(solution)/shard_map/ppermute | solution.py:398
  52.4 6.5 %collective-permute-start.11 = (bf16[144,256]{1,0:T(8,128)(2,1)S(1)}, bf16[144,256]{1,0:T(8,128)(2,1)S(1)}, u32[]{:S(2)}, u32[]{:S(2)}) collective-permute-start(bf16[144,256]{1,0:T(8,128)(2,1)S(1)} %get-tuple-element.32), channel_id=1, source_target_pairs={{0,24},{8,16},{16,8},{24,0},{1,25},{9,17},{17,9},{25,1},{2,26},{10... | collective-permute-start | bytes 221192 | tf_op jit(solution)/shard_map/ppermute | solution.py:398
  53.8 5.6 %collective-permute-start.9 = (bf16[144,256]{1,0:T(8,128)(2,1)S(1)}, bf16[144,256]{1,0:T(8,128)(2,1)S(1)}, u32[]{:S(2)}, u32[]{:S(2)}) collective-permute-start(bf16[144,256]{1,0:T(8,128)(2,1)S(1)} %get-tuple-element.30), channel_id=1, source_target_pairs={{0,8},{8,0},{16,24},{24,16},{1,9},{9,1},{17,25},{25,17},{2,10},{10... | collective-permute-start | bytes 221192 | tf_op jit(solution)/shard_map/ppermute | solution.py:398

commit v6 on v5

--- a/solution.py
+++ b/solution.py
@@ -67,12 +67,19 @@
 def turn_table(low, high, turn, step, table):
     half = table.shape[0] // 2
 
-    for start in range(low, high, LANES):
-        cosine, sine = turn[0], turn[1]
-        table[:half, start : start + LANES] = cosine.astype(BF16)
-        table[half:, start : start + LANES] = sine.astype(BF16)
-        turn[0] = cosine * step[0] - sine * step[1]
-        turn[1] = sine * step[0] + cosine * step[1]
+    for first in range(0, half, 32):
+        here = slice(first, min(first + 32, half))
+        rotation = step[0, here], step[1, here]
+        cosine, sine = turn[0, here], turn[1, here]
+        for start in range(low, high, LANES):
+            table[here, start : start + LANES] = cosine.astype(BF16)
+            table[half + first : half + here.stop, start : start + LANES] = sine.astype(BF16)
+            cosine, sine = (
+                cosine * rotation[0] - sine * rotation[1],
+                sine * rotation[0] + cosine * rotation[1],
+            )
+        turn[0, here] = cosine
+        turn[1, here] = sine
 
 
 def table_kernel(scale_ref, *rest):

time: 66 us -> 64.8 us (0.982)
  Pallas kernels: 28.8 us -> 27.7 us
    pallas_call x1, Pallas kernels: 15.9 us -> 14.7 us  [half_transform(): pl.pallas_call(functools.partial(half_kernel, ranges, parts, block, width...]
where the time goes in v6:
time: 64.8 us; the launch traced here: 64.7 us
  Pallas kernels  27.7 us (43%)
  waiting for transfers between devices  18.1 us (28%)
  starting transfers between devices  17.9 us (28%)
  between operations  0.83 us (1%)
    ppermute x10, waiting for transfers between devices, exchange(): received[hop] = lax.ppermute(pieces[hop], axis, pairs)  18.1 us
    pallas_call x1, Pallas kernels, half_transform(): pl.pallas_call(functools.partial(half_kernel, ranges, parts, block, width...  14.7 us
    ppermute x10, starting transfers between devices, exchange(): received[hop] = lax.ppermute(pieces[hop], axis, pairs)  13.5 us
    pallas_call x1, Pallas kernels, tile_light(): pl.pallas_call(functools.partial(tile_kernel, waves), in_specs=[pl.BlockS...  6.43 us
    ppermute x2, starting transfers between devices, shifted(): lax.ppermute(value, axis, [(source, source + steps) for source in range(i...  4.45 us
    pallas_call x1, Pallas kernels, lens_intensity(): pl.pallas_call(functools.partial(lens_kernel, layout, parts, waves, block...  2.96 us
    pallas_call x1, Pallas kernels, lens_table(): pl.pallas_call(table_kernel, in_specs=[pl.BlockSpec(memory_space=pltpu.SM...  2.89 us
  transfers between devices with their start and end apart: 12, of which 6 were waited for; matrix products, arithmetic and copies ran while one was open for 0% of the time, Pallas kernels for 5%

profile of v6, /device:TPU:0, one launch (start us, length us, event | category | flops | bytes accessed | tf_op | source)
XLA Modules:
  0.0 64.7 jit_solution(8746460621494372200)
XLA Ops:
  0.0 0.0 copy-start
  0.0 0.0 copy-start.1
  0.0 0.0 copy-start.2
  0.8 14.7 %half_transform.1 = (bf16[272,512]{1,0:T(8,128)(2,1)S(1)}, bf16[272,512]{1,0:T(8,128)(2,1)S(1)}, bf16[272,512]{1,0:T(8,128)(2,1)S(1)}, bf16[272,512]{1,0:T(8,128...) custom-call(s32[1]{0:T(128)} %bitcast.me_ref, ...), custom_call_target="tpu_custom_call" | custom-call | flops 1 | bytes 1 | tf_op jit(solution)/shard_map/half_transform/pallas_call | solution.py:179
  15.5 0.5 collective-permute-start
  16.0 2.6 %collective-permute-start.1 = (bf16[272,512]{1,0:T(8,128)(2,1)S(1)}, bf16[272,512]{1,0:T(8,128)(2,1)S(1)}, u32[]{:S(2)}, u32[]{:S(2)}) collective-permute-start(bf16[272,512]{1,0:T(8,128)(2,1)S(1)} %get-tuple-element.20), channel_id=1, source_target_pairs={{0,2},{1,3},{2,0},{3,1},{4,6},{5,7},{6,4},{7,5},{8,10},{9,11},{10,... | collective-permute-start | bytes 835592 | tf_op jit(solution)/shard_map/ppermute | solution.py:405
  18.6 0.1 collective-permute-start.2
  18.7 1.8 %collective-permute-start.3 = (bf16[272,512]{1,0:T(8,128)(2,1)S(1)}, bf16[272,512]{1,0:T(8,128)(2,1)S(1)}, u32[]{:S(2)}, u32[]{:S(2)}) collective-permute-start(bf16[272,512]{1,0:T(8,128)(2,1)S(1)} %get-tuple-element.24), channel_id=1, source_target_pairs={{0,4},{1,5},{2,6},{3,7},{4,0},{5,1},{6,2},{7,3},{8,12},{9,13},{10,... | collective-permute-start | bytes 835592 | tf_op jit(solution)/shard_map/ppermute | solution.py:405
  20.4 0.0 collective-permute-start.4
  20.4 0.0 collective-permute-done.rest_0_.rest_1_
  20.4 2.6 %collective-permute-start.5 = (bf16[272,512]{1,0:T(8,128)(2,1)}, bf16[272,512]{1,0:T(8,128)(2,1)S(1)}, u32[]{:S(2)}, u32[]{:S(2)}) collective-permute-start(bf16[272,512]{1,0:T(8,128)(2,1)} %get-tuple-element.26), channel_id=1, source_target_pairs={{0,6},{1,7},{2,4},{3,5},{4,2},{5,3},{6,0},{7,1},{8,14},{9,15},{10,... | collective-permute-start | bytes 835592 | tf_op jit(solution)/shard_map/ppermute | solution.py:405
  23.0 3.1 %collective-permute-done.1.rest_1_.rest_2_ = bf16[272,512]{1,0:T(8,128)(2,1)S(1)} collective-permute-done((bf16[272,512]{1,0:T(8,128)(2,1)S(1)}, bf16[272,512]{1,0:T(8,128)(2,1)S(1)}, u32[]{:S(2)}, u32[]{:S(2)}) %collective-permute-start.1) | collective-permute-done | bytes 278560 | tf_op jit(solution)/shard_map/ppermute | solution.py:405
  26.1 1.7 %collective-permute-start.6 = (bf16[272,512]{1,0:T(8,128)(2,1)}, bf16[272,512]{1,0:T(8,128)(2,1)S(1)}, u32[]{:S(2)}, u32[]{:S(2)}) collective-permute-start(bf16[272,512]{1,0:T(8,128)(2,1)} %get-tuple-element.27), channel_id=1, source_target_pairs={{0,7},{1,6},{2,5},{3,4},{4,3},{5,2},{6,1},{7,0},{8,15},{9,14},{10,... | collective-permute-start | bytes 835592 | tf_op jit(solution)/shard_map/ppermute | solution.py:405
  27.8 0.0 copy-done
  27.8 0.0 copy-done.1
  27.8 0.0 copy-done.2
  27.8 0.7 %edge_traces.1 = (s32[9,8,256]{2,1,0:T(8,128)}, s32[9,8,256]{2,1,0:T(8,128)}) custom-call(s32[4,128,256]{2,1,0:T(8,128)S(1)} %copy-done, s32[4,128,256]{2,1,0:T(8,128)S(1)} %copy-done.1, s32[128,256]{1,0:T(8,128)S(1)} %copy-done.2, bf16[272,512]{1,0:T(8,128)(2,1)S(1)} %collective-permute-done.rest_0_.rest_1_, ...), custom_call_target="tpu_custom_call" | custom-call | flops 1 | bytes 1 | tf_op jit(solution)/shard_map/edge_traces/pallas_call | solution.py:327
  28.5 3.1 %collective-permute-done.2.rest_3_ = bf16[272,512]{1,0:T(8,128)(2,1)S(1)} collective-permute-done((bf16[272,512]{1,0:T(8,128)(2,1)S(1)}, bf16[272,512]{1,0:T(8,128)(2,1)S(1)}, u32[]{:S(2)}, u32[]{:S(2)}) %collective-permute-start.2) | collective-permute-done | bytes 278560 | tf_op jit(solution)/shard_map/ppermute | solution.py:405
  31.6 1.3 %collective-permute-start.8 = (s32[9,8,256]{2,1,0:T(8,128)}, s32[9,8,256]{2,1,0:T(8,128)S(1)}, u32[]{:S(2)}, u32[]{:S(2)}) collective-permute-start(s32[9,8,256]{2,1,0:T(8,128)} %get-tuple-element.21.rest_2_), channel_id=1, source_target_pairs={{1,0},{2,1},{3,2},{4,3},{5,4},{6,5},{7,6},{9,8},{10,9},{11,10},{12... | collective-permute-start | bytes 221192 | tf_op jit(solution)/shard_map/ppermute | solution.py:412
  32.8 0.0 collective-permute-done.3.rest_4_
  32.8 3.2 %collective-permute-start.7 = (s32[9,8,256]{2,1,0:T(8,128)}, s32[9,8,256]{2,1,0:T(8,128)S(1)}, u32[]{:S(2)}, u32[]{:S(2)}) collective-permute-start(s32[9,8,256]{2,1,0:T(8,128)} %get-tuple-element.28), channel_id=1, source_target_pairs={{0,1},{1,2},{2,3},{3,4},{4,5},{5,6},{6,7},{8,9},{9,10},{10,11},{11... | collective-permute-start | bytes 221192 | tf_op jit(solution)/shard_map/ppermute | solution.py:412
  36.0 2.9 %lens_table.1.table = bf16[1024,4096]{1,0:T(8,128)(2,1)S(1)} custom-call(f32[1]{0:T(128)S(6)} %copy.6.scale_ref, bf16[272,512]{1,0:T(8,128)(2,1)S(1)} %collective-permute-done.rest_0_.rest_1_, bf16[272,512]{1,0:T(8,128)(2,1)S(1)} %collective-permute-done.1.rest_1_.rest_2_, s32[9,8,256]{2,1,0:T(8,128)} %get-tuple-element.21.rest_2_), custom_call_target="tpu_custom_call" | custom-call | flops 1 | bytes 1 | tf_op jit(solution)/shard_map/lens_table/pallas_call | solution.py:103
  38.9 6.7 %collective-permute-done.4.rest_5_ = bf16[272,512]{1,0:T(8,128)(2,1)S(1)} collective-permute-done((bf16[272,512]{1,0:T(8,128)(2,1)}, bf16[272,512]{1,0:T(8,128)(2,1)S(1)}, u32[]{:S(2)}, u32[]{:S(2)}) %collective-permute-start.4) | collective-permute-done | bytes 278560 | tf_op jit(solution)/shard_map/ppermute | solution.py:405
  45.6 0.0 collective-permute-done.5.rest_6_
  45.7 0.0 collective-permute-done.6.rest_7_
  45.7 0.0 collective-permute-done.8.rest_9_.rest_8_
  45.7 0.0 collective-permute-done.7.rest_8_.rest_7_
  45.7 3.0 %lens_intensity.1 = (bf16[144,256]{1,0:T(8,128)(2,1)S(1)}, bf16[144,256]{1,0:T(8,128)(2,1)S(1)}, bf16[144,256]{1,0:T(8,128)(2,1)S(1)}, bf16[144,256]{1,0:T(8,128)(2,1)S(1)}) custom-call(s32[1]{0:T(128)} %bitcast.me_ref, s32[1]{0:T(128)} %bitcast.1.wave_ref, bf16[1024,4096]{1,0:T(8,128)(2,1)S(1)} %lens_table.1.table, ...), custom_call_target="tpu_custom_call" | custom-call | flops 1 | bytes 1 | tf_op jit(solution)/shard_map/lens_intensity/pallas_call | solution.py:248
  48.6 2.7 %collective-permute-start.10 = (bf16[144,256]{1,0:T(8,128)(2,1)S(1)}, bf16[144,256]{1,0:T(8,128)(2,1)S(1)}, u32[]{:S(2)}, u32[]{:S(2)}) collective-permute-start(bf16[144,256]{1,0:T(8,128)(2,1)S(1)} %get-tuple-element.31), channel_id=1, source_target_pairs={{0,16},{8,24},{16,0},{24,8},{1,17},{9,25},{17,1},{25,9},{2,18},{10... | collective-permute-start | bytes 221192 | tf_op jit(solution)/shard_map/ppermute | solution.py:405
  51.3 1.3 %collective-permute-start.11 = (bf16[144,256]{1,0:T(8,128)(2,1)S(1)}, bf16[144,256]{1,0:T(8,128)(2,1)S(1)}, u32[]{:S(2)}, u32[]{:S(2)}) collective-permute-start(bf16[144,256]{1,0:T(8,128)(2,1)S(1)} %get-tuple-element.32), channel_id=1, source_target_pairs={{0,24},{8,16},{16,8},{24,0},{1,25},{9,17},{17,9},{25,1},{2,26},{10... | collective-permute-start | bytes 221192 | tf_op jit(solution)/shard_map/ppermute | solution.py:405
  52.6 0.2 collective-permute-start.9
  52.9 0.1 pad_add_fusion.place_ref
  52.9 3.8 %collective-permute-done.10.rest_2_ = bf16[144,256]{1,0:T(8,128)(2,1)S(1)} collective-permute-done((bf16[144,256]{1,0:T(8,128)(2,1)S(1)}, bf16[144,256]{1,0:T(8,128)(2,1)S(1)}, u32[]{:S(2)}, u32[]{:S(2)}) %collective-permute-start.10) | collective-permute-done | bytes 73760 | tf_op jit(solution)/shard_map/ppermute | solution.py:405
  56.8 1.0 %collective-permute-done.11.rest_3_ = bf16[144,256]{1,0:T(8,128)(2,1)S(1)} collective-permute-done((bf16[144,256]{1,0:T(8,128)(2,1)S(1)}, bf16[144,256]{1,0:T(8,128)(2,1)S(1)}, u32[]{:S(2)}, u32[]{:S(2)}) %collective-permute-start.11) | collective-permute-done | bytes 73760 | tf_op jit(solution)/shard_map/ppermute | solution.py:405
  57.8 0.4 collective-permute-done.9.rest_1_
  58.2 6.4 %tile_light.1 = f32[512,1024]{1,0:T(8,128)} custom-call(s32[2]{0:T(128)S(1)} %pad_add_fusion.place_ref, bf16[144,256]{1,0:T(8,128)(2,1)S(1)} %get-tuple-element.29.rest_0_, bf16[144,256]{1,0:T(8,128)(2,1)S(1)} %collective-permute-done.9.rest_1_, bf16[144,256]{1,0:T(8,128)(2,1)S(1)} %collective-permute-done.10.rest_2_, ...), custom_call_target="tpu_custom_call" | custom-call | flops 1 | bytes 1 | tf_op jit(solution)/shard_map/tile_light/pallas_call | solution.py:382
Async XLA Ops:
  0.0 27.8 %copy-start = (s32[4,128,256]{2,1,0:T(8,128)S(1)}, s32[4,128,256]{2,1,0:T(8,128)}, u32[]{:S(2)}) copy-start(s32[4,128,256]{2,1,0:T(8,128)} %rest_4_.1) | copy-start | bytes 1572868
  0.0 27.8 %copy-start.1 = (s32[4,128,256]{2,1,0:T(8,128)S(1)}, s32[4,128,256]{2,1,0:T(8,128)}, u32[]{:S(2)}) copy-start(s32[4,128,256]{2,1,0:T(8,128)} %rest_5_.1) | copy-start | bytes 1572868
  0.0 27.8 %copy-start.2 = (s32[128,256]{1,0:T(8,128)S(1)}, s32[128,256]{1,0:T(8,128)}, u32[]{:S(2)}) copy-start(s32[128,256]{1,0:T(8,128)} %rest_6_.1) | copy-start | bytes 393220
  15.5 4.9 %collective-permute-start = (bf16[272,512]{1,0:T(8,128)(2,1)S(1)}, bf16[272,512]{1,0:T(8,128)(2,1)S(1)}, u32[]{:S(2)}, u32[]{:S(2)}) collective-permute-start(bf16[272,512]{1,0:T(8,128)(2,1)S(1)} %get-tuple-element.19), channel_id=1, source_target_pairs={{0,1},{1,0},{2,3},{3,2},{4,5},{5,4},{6,7},{7,6},{8,9},{9,8},{10,11... | collective-permute-start | bytes 835592 | tf_op jit(solution)/shard_map/ppermute | solution.py:405
  16.0 10.1 %collective-permute-start.1 = (bf16[272,512]{1,0:T(8,128)(2,1)S(1)}, bf16[272,512]{1,0:T(8,128)(2,1)S(1)}, u32[]{:S(2)}, u32[]{:S(2)}) collective-permute-start(bf16[272,512]{1,0:T(8,128)(2,1)S(1)} %get-tuple-element.20), channel_id=1, source_target_pairs={{0,2},{1,3},{2,0},{3,1},{4,6},{5,7},{6,4},{7,5},{8,10},{9,11},{10,... | collective-permute-start | bytes 835592 | tf_op jit(solution)/shard_map/ppermute | solution.py:405
  18.6 13.0 %collective-permute-start.2 = (bf16[272,512]{1,0:T(8,128)(2,1)S(1)}, bf16[272,512]{1,0:T(8,128)(2,1)S(1)}, u32[]{:S(2)}, u32[]{:S(2)}) collective-permute-start(bf16[272,512]{1,0:T(8,128)(2,1)S(1)} %get-tuple-element.23), channel_id=1, source_target_pairs={{0,3},{1,2},{2,1},{3,0},{4,7},{5,6},{6,5},{7,4},{8,11},{9,10},{10,... | collective-permute-start | bytes 835592 | tf_op jit(solution)/shard_map/ppermute | solution.py:405
  18.7 14.2 %collective-permute-start.3 = (bf16[272,512]{1,0:T(8,128)(2,1)S(1)}, bf16[272,512]{1,0:T(8,128)(2,1)S(1)}, u32[]{:S(2)}, u32[]{:S(2)}) collective-permute-start(bf16[272,512]{1,0:T(8,128)(2,1)S(1)} %get-tuple-element.24), channel_id=1, source_target_pairs={{0,4},{1,5},{2,6},{3,7},{4,0},{5,1},{6,2},{7,3},{8,12},{9,13},{10,... | collective-permute-start | bytes 835592 | tf_op jit(solution)/shard_map/ppermute | solution.py:405
  20.4 25.2 %collective-permute-start.4 = (bf16[272,512]{1,0:T(8,128)(2,1)}, bf16[272,512]{1,0:T(8,128)(2,1)S(1)}, u32[]{:S(2)}, u32[]{:S(2)}) collective-permute-start(bf16[272,512]{1,0:T(8,128)(2,1)} %get-tuple-element.25), channel_id=1, source_target_pairs={{0,5},{1,4},{2,7},{3,6},{4,1},{5,0},{6,3},{7,2},{8,13},{9,12},{10,... | collective-permute-start | bytes 835592 | tf_op jit(solution)/shard_map/ppermute | solution.py:405
  20.4 25.2 %collective-permute-start.5 = (bf16[272,512]{1,0:T(8,128)(2,1)}, bf16[272,512]{1,0:T(8,128)(2,1)S(1)}, u32[]{:S(2)}, u32[]{:S(2)}) collective-permute-start(bf16[272,512]{1,0:T(8,128)(2,1)} %get-tuple-element.26), channel_id=1, source_target_pairs={{0,6},{1,7},{2,4},{3,5},{4,2},{5,3},{6,0},{7,1},{8,14},{9,15},{10,... | collective-permute-start | bytes 835592 | tf_op jit(solution)/shard_map/ppermute | solution.py:405
  26.1 19.6 %collective-permute-start.6 = (bf16[272,512]{1,0:T(8,128)(2,1)}, bf16[272,512]{1,0:T(8,128)(2,1)S(1)}, u32[]{:S(2)}, u32[]{:S(2)}) collective-permute-start(bf16[272,512]{1,0:T(8,128)(2,1)} %get-tuple-element.27), channel_id=1, source_target_pairs={{0,7},{1,6},{2,5},{3,4},{4,3},{5,2},{6,1},{7,0},{8,15},{9,14},{10,... | collective-permute-start | bytes 835592 | tf_op jit(solution)/shard_map/ppermute | solution.py:405
  31.6 14.1 %collective-permute-start.8 = (s32[9,8,256]{2,1,0:T(8,128)}, s32[9,8,256]{2,1,0:T(8,128)S(1)}, u32[]{:S(2)}, u32[]{:S(2)}) collective-permute-start(s32[9,8,256]{2,1,0:T(8,128)} %get-tuple-element.21.rest_2_), channel_id=1, source_target_pairs={{1,0},{2,1},{3,2},{4,3},{5,4},{6,5},{7,6},{9,8},{10,9},{11,10},{12... | collective-permute-start | bytes 221192 | tf_op jit(solution)/shard_map/ppermute | solution.py:412
  32.8 12.8 %collective-permute-start.7 = (s32[9,8,256]{2,1,0:T(8,128)}, s32[9,8,256]{2,1,0:T(8,128)S(1)}, u32[]{:S(2)}, u32[]{:S(2)}) collective-permute-start(s32[9,8,256]{2,1,0:T(8,128)} %get-tuple-element.28), channel_id=1, source_target_pairs={{0,1},{1,2},{2,3},{3,4},{4,5},{5,6},{6,7},{8,9},{9,10},{10,11},{11... | collective-permute-start | bytes 221192 | tf_op jit(solution)/shard_map/ppermute | solution.py:412
  48.6 8.1 %collective-permute-start.10 = (bf16[144,256]{1,0:T(8,128)(2,1)S(1)}, bf16[144,256]{1,0:T(8,128)(2,1)S(1)}, u32[]{:S(2)}, u32[]{:S(2)}) collective-permute-start(bf16[144,256]{1,0:T(8,128)(2,1)S(1)} %get-tuple-element.31), channel_id=1, source_target_pairs={{0,16},{8,24},{16,0},{24,8},{1,17},{9,25},{17,1},{25,9},{2,18},{10... | collective-permute-start | bytes 221192 | tf_op jit(solution)/shard_map/ppermute | solution.py:405
  51.3 6.5 %collective-permute-start.11 = (bf16[144,256]{1,0:T(8,128)(2,1)S(1)}, bf16[144,256]{1,0:T(8,128)(2,1)S(1)}, u32[]{:S(2)}, u32[]{:S(2)}) collective-permute-start(bf16[144,256]{1,0:T(8,128)(2,1)S(1)} %get-tuple-element.32), channel_id=1, source_target_pairs={{0,24},{8,16},{16,8},{24,0},{1,25},{9,17},{17,9},{25,1},{2,26},{10... | collective-permute-start | bytes 221192 | tf_op jit(solution)/shard_map/ppermute | solution.py:405
  52.6 5.6 %collective-permute-start.9 = (bf16[144,256]{1,0:T(8,128)(2,1)S(1)}, bf16[144,256]{1,0:T(8,128)(2,1)S(1)}, u32[]{:S(2)}, u32[]{:S(2)}) collective-permute-start(bf16[144,256]{1,0:T(8,128)(2,1)S(1)} %get-tuple-element.30), channel_id=1, source_target_pairs={{0,8},{8,0},{16,24},{24,16},{1,9},{9,1},{17,25},{25,17},{2,10},{10... | collective-permute-start | bytes 221192 | tf_op jit(solution)/shard_map/ppermute | solution.py:405
